TPU v7x, 32 devices: a whole 2x2x4 slice. The times are simulated.
32 devices in a mesh: grp: 2 (over y), frame: 4 (over x, core), band: 4 (over z).
Axes of the slice: x: 2, y: 2, z: 4, core: 2. Of those that a mesh axis runs over, the one named last changes fastest.
Arguments:
- features: bfloat16 [16, 64, 128, 256], P(('grp', 'frame'), 'band'), parts along dimension 0, may hold values from -6 to 6
- space_kernel: bfloat16 [3, 3, 256, 256], replicated, may hold values from -0.125 to 0.125
- space_gain: float32 [256], replicated, may hold values from 0.5 to 2
- space_bias: float32 [256], replicated, may hold values from -3 to 3
- time_kernel: bfloat16 [3, 256, 256], replicated, may hold values from -0.21875 to 0.21875
- time_gain: float32 [256], replicated, may hold values from 0.5 to 2
- time_bias: float32 [256], replicated, may hold values from -3 to 3
Outputs:
- decoded: bfloat16 [16, 64, 128, 256], P(('grp', 'frame'), 'band'), parts along dimension 0
There are 2 independent parts, one for each index of `grp`. A program takes and returns all parts, laid end to end along the dimension named above; an argument that names none is the same for every part. Nothing has to cross between parts.
All inputs are finite; a program needn't handle non-finite values.
Results may differ from a plain program's by a relative error of at most 0.0056.
Values may be sent and summed in bfloat16 or wider, within the bound.
No kernel may reach another device: no remote copies, remote signals or barrier semaphores. Data moves between devices by JAX's collectives and lax.ppermute only.
A program may use at most 64 MiB of HBM per device.

v0:
```python
import jax
import jax.numpy as jnp
from jax import lax
from jax.sharding import PartitionSpec as P


def with_halo(array, sides, width):
    for axis, dim in sides:
        count, length = (lax.axis_size(axis), array.shape[dim])
        up = [(i, (i + 1) % count) for i in range(count - 1)]
        down = [(j, i) for i, j in up]
        last = lax.slice_in_dim(array, length - width, length, axis=dim)
        first = lax.slice_in_dim(array, 0, width, axis=dim)
        before = lax.ppermute(last, axis, up)
        after = lax.ppermute(first, axis, down)
        array = jnp.concatenate([before, array, after], axis=dim)
    return array


def passed_along(array, axis, by):
    count = lax.axis_size(axis)
    pairs = [(i, i + by) for i in range(count) if 0 <= i + by < count]
    return lax.ppermute(array, axis, pairs)


def rms_silu(values, gain_vector):
    widened = values.astype(jnp.float32)
    scaled = (
        widened
        * lax.rsqrt(jnp.mean(widened * widened, axis=-1, keepdims=True) + 1e-06)
        * gain_vector
    )
    return jax.nn.silu(scaled).astype(jnp.bfloat16)


def lag_product(frames_in, kernel_slice):
    channels = frames_in.shape[-1]
    product = jnp.dot(
        frames_in.reshape(-1, channels), kernel_slice, preferred_element_type=jnp.float32
    )
    return product.reshape(frames_in.shape[:-1] + (kernel_slice.shape[1],))


def body(features, space_kernel, space_gain, space_bias, time_kernel, time_gain, time_bias):
    frame_count, rows_count, cols_count, channels = features.shape
    normed = rms_silu(features, space_gain)
    padded = with_halo(normed, (("band", 1),), 1)
    padded = jnp.pad(padded, ((0, 0), (0, 0), (1, 1), (0, 0)))
    summed = None
    for tap_row in range(3):
        for tap_col in range(3):
            window = padded[
                :, tap_row : tap_row + rows_count, tap_col : tap_col + cols_count
            ].reshape(-1, channels)
            product = jnp.dot(
                window, space_kernel[tap_row, tap_col], preferred_element_type=jnp.float32
            )
            summed = product if summed is None else summed + product
    spatial = summed.reshape(features.shape)
    hidden = (features.astype(jnp.float32) + spatial + space_bias).astype(jnp.bfloat16)
    hidden = lax.optimization_barrier(hidden)
    normed_time = rms_silu(hidden, time_gain)
    local_sum = lag_product(normed_time, time_kernel[0])
    for time_lag in range(1, 3):
        shifted = lag_product(normed_time[: frame_count - time_lag], time_kernel[time_lag])
        local_sum = local_sum + jnp.pad(shifted, ((time_lag, 0), (0, 0), (0, 0), (0, 0)))
    earlier = passed_along(normed_time, "frame", 1)
    for time_lag in range(1, 3):
        remote = lag_product(earlier[2 - time_lag :], time_kernel[time_lag])
        local_sum = local_sum + jnp.pad(
            remote, ((0, frame_count - time_lag), (0, 0), (0, 0), (0, 0))
        )
    temporal = local_sum.astype(jnp.bfloat16)
    temporal = lax.optimization_barrier(temporal)
    decoded = hidden.astype(jnp.float32) + temporal.astype(jnp.float32) + time_bias
    return decoded.astype(jnp.bfloat16)


def solution(mesh):
    return jax.shard_map(
        body,
        mesh=mesh,
        in_specs=(P(("grp", "frame"), "band", None, None), P(), P(), P(), P(), P(), P()),
        out_specs=P(("grp", "frame"), "band", None, None),
        check_vma=False,
    )
```

profile of v0, /device:TPU:18, one launch (start us, length us, event | category | flops | bytes accessed | tf_op | source)
XLA Modules:
  0.0 61.6 jit_solution(18141599922598498462)
XLA Ops:
  0.0 2.4 %fusion.2 = f32[2,16,128]{2,1,0:T(8,128)S(1)} fusion(bf16[2,16,128,256]{3,2,1,0:T(8,128)(2,1)} %param.7), kind=kLoop, calls=%fused_computation.17 | loop fusion | flops 3141632 | bytes 2113536 | tf_op jit(solution)/shard_map/reduce_sum | solution.py:30
  2.4 1.4 %fusion.9 = bf16[2,16,128,256]{3,2,1,0:T(8,128)(2,1)S(1)} fusion(bf16[2,16,128,256]{3,2,1,0:T(8,128)(2,1)S(1)} %copy-done, f32[256]{0:T(256)S(1)} %copy-done.3, f32[2,16,128]{2,1,0:T(8,128)S(1)} %add_rsqrt_fusion.1), kind=kLoop, calls=%fused_computation.24 | loop fusion | flops 8388608 | bytes 4211712 | tf_op jit(solution)/shard_map/convert_element_type | solution.py:33
  3.8 3.5 %collective-permute-start = (bf16[2,1,128,256]{3,2,1,0:T(8,128)(2,1)S(1)}, bf16[2,1,128,256]{3,2,1,0:T(8,128)(2,1)S(1)}, u32[]{:S(2)}, u32[]{:S(2)}) collective-permute-start(bf16[2,1,128,256]{3,2,1,0:T(8,128)(2,1)S(1)} %get-tuple-element.13), channel_id=1, source_target_pairs={{0,1},{1,2},{2,3},{4,5},{5,6},{6,7},{8,9},{9,10},{10,11},{12,13},{... | collective-permute-start | bytes 393224 | tf_op jit(solution)/shard_map/ppermute | solution.py:14
  7.3 2.4 %collective-permute-start.1 = (bf16[2,1,128,256]{3,2,1,0:T(8,128)(2,1)S(1)}, bf16[2,1,128,256]{3,2,1,0:T(8,128)(2,1)S(1)}, u32[]{:S(2)}, u32[]{:S(2)}) collective-permute-start(bf16[2,1,128,256]{3,2,1,0:T(8,128)(2,1)S(1)} %get-tuple-element.14), channel_id=1, source_target_pairs={{1,0},{2,1},{3,2},{5,4},{6,5},{7,6},{9,8},{10,9},{11,10},{13,12},{... | collective-permute-start | bytes 393224 | tf_op jit(solution)/shard_map/ppermute | solution.py:15
  9.7 1.3 %collective-permute-done = bf16[2,1,128,256]{3,2,1,0:T(8,128)(2,1)S(1)} collective-permute-done((bf16[2,1,128,256]{3,2,1,0:T(8,128)(2,1)S(1)}, bf16[2,1,128,256]{3,2,1,0:T(8,128)(2,1)S(1)}, u32[]{:S(2)}, u32[]{:S(2)}) %collective-permute-start) | collective-permute-done | bytes 131104 | tf_op jit(solution)/shard_map/ppermute | solution.py:14
  11.0 3.2 %collective-permute-done.1 = bf16[2,1,128,256]{3,2,1,0:T(8,128)(2,1)S(1)} collective-permute-done((bf16[2,1,128,256]{3,2,1,0:T(8,128)(2,1)S(1)}, bf16[2,1,128,256]{3,2,1,0:T(8,128)(2,1)S(1)}, u32[]{:S(2)}, u32[]{:S(2)}) %collective-permute-start.1) | collective-permute-done | bytes 131104 | tf_op jit(solution)/shard_map/ppermute | solution.py:15
  14.2 1.1 %fusion.26 = bf16[2,18,130,256]{3,2,1,0:T(8,128)(2,1)S(1)} fusion(bf16[2,1,128,256]{3,2,1,0:T(8,128)(2,1)S(1)} %collective-permute-done.1, bf16[2,16,128,256]{3,2,1,0:T(8,128)(2,1)S(1)} %fusion.9, bf16[2,1,128,256]{3,2,1,0:T(8,128)(2,1)S(1)} %collective-permute-done), kind=kLoop, calls=%fused_computation.42 | loop fusion | flops 14376960 | bytes 4755456 | tf_op jit(solution)/shard_map/concatenate | solution.py:16
  15.3 0.0 copy-start.1
  15.3 5.2 %fusion.56 = (bf16[2,16,128,256]{3,2,1,0:T(8,128)(2,1)S(1)}, bf16[2,16,128,256]{3,2,1,0:T(8,128)(2,1)S(1)}, bf16[2,16,128,256]{3,2,1,0:T(8,128)(2,1)S(1)}, bf16[...) fusion(bf16[2,18,130,256]{3,2,1,0:T(8,128)(2,1)S(1)} %fusion.26), kind=kLoop, calls=%fused_computation.80 | loop fusion | bytes 25165824 | tf_op jit(solution)/shard_map/slice | solution.py:52
  20.5 0.7 %fusion.41 = f32[4096,256]{1,0:T(8,128)S(1)} fusion(bf16[4096,256]{1,0:T(8,128)(2,1)S(1)} %bitcast.81, bf16[3,3,256,256]{3,2,1,0:T(8,128)(2,1)S(1)} %copy-done.1), kind=kOutput, calls=%fused_computation.63 | convolution fusion | flops 536870912 | bytes 6422528 | tf_op jit(solution)/shard_map/dot_general | solution.py:55
  21.2 0.7 %fusion.32 = f32[4096,256]{1,0:T(8,128)S(1)} fusion(bf16[4096,256]{1,0:T(8,128)(2,1)S(1)} %bitcast.80, bf16[3,3,256,256]{3,2,1,0:T(8,128)(2,1)S(1)} %copy-done.1), kind=kOutput, calls=%fused_computation.54 | convolution fusion | flops 536870912 | bytes 6422528 | tf_op jit(solution)/shard_map/dot_general | solution.py:55
  21.9 0.3 pad_maximum_fusion
  22.2 0.8 %convolution_add_fusion.6 = f32[4096,256]{1,0:T(8,128)S(1)} fusion(f32[4096,256]{1,0:T(8,128)S(1)} %fusion.41, bf16[4096,256]{1,0:T(8,128)(2,1)S(1)} %bitcast.87, bf16[3,3,256,256]{3,2,1,0:T(8,128)(2,1)S(1)} %copy-done.1), kind=kOutput, calls=%fused_computation.15 | convolution fusion | flops 537919488 | bytes 10616832 | tf_op jit(solution)/shard_map/dot_general | solution.py:55
  23.0 0.8 %convolution_add_fusion.5 = f32[4096,256]{1,0:T(8,128)S(1)} fusion(f32[4096,256]{1,0:T(8,128)S(1)} %convolution_add_fusion.6, bf16[4096,256]{1,0:T(8,128)(2,1)S(1)} %bitcast.86, bf16[3,3,256,256]{3,2,1,0:T(8,128)(2,1)S(1)} %copy-done.1), kind=kOutput, calls=%fused_computation.14 | convolution fusion | flops 537919488 | bytes 10616832 | tf_op jit(solution)/shard_map/dot_general | solution.py:55
  23.7 0.8 %convolution_add_fusion.4 = f32[4096,256]{1,0:T(8,128)S(1)} fusion(f32[4096,256]{1,0:T(8,128)S(1)} %convolution_add_fusion.5, bf16[4096,256]{1,0:T(8,128)(2,1)S(1)} %bitcast.85, bf16[3,3,256,256]{3,2,1,0:T(8,128)(2,1)S(1)} %copy-done.1), kind=kOutput, calls=%fused_computation.13 | convolution fusion | flops 537919488 | bytes 10616832 | tf_op jit(solution)/shard_map/dot_general | solution.py:55
  24.5 0.8 %convolution_add_fusion.3 = f32[4096,256]{1,0:T(8,128)S(1)} fusion(f32[4096,256]{1,0:T(8,128)S(1)} %convolution_add_fusion.4, bf16[4096,256]{1,0:T(8,128)(2,1)S(1)} %bitcast.78, bf16[3,3,256,256]{3,2,1,0:T(8,128)(2,1)S(1)} %copy-done.1), kind=kOutput, calls=%fused_computation.12 | convolution fusion | flops 537919488 | bytes 10616832 | tf_op jit(solution)/shard_map/dot_general | solution.py:55
  25.3 0.8 %convolution_add_fusion.2 = f32[4096,256]{1,0:T(8,128)S(1)} fusion(f32[4096,256]{1,0:T(8,128)S(1)} %convolution_add_fusion.3, bf16[4096,256]{1,0:T(8,128)(2,1)S(1)} %bitcast.84, bf16[3,3,256,256]{3,2,1,0:T(8,128)(2,1)S(1)} %copy-done.1), kind=kOutput, calls=%fused_computation.11 | convolution fusion | flops 537919488 | bytes 10616832 | tf_op jit(solution)/shard_map/dot_general | solution.py:55
  26.1 0.8 %convolution_add_fusion.1 = f32[4096,256]{1,0:T(8,128)S(1)} fusion(f32[4096,256]{1,0:T(8,128)S(1)} %convolution_add_fusion.2, bf16[4096,256]{1,0:T(8,128)(2,1)S(1)} %bitcast.83, bf16[3,3,256,256]{3,2,1,0:T(8,128)(2,1)S(1)} %copy-done.1), kind=kOutput, calls=%fused_computation.10 | convolution fusion | flops 537919488 | bytes 10616832 | tf_op jit(solution)/shard_map/dot_general | solution.py:55
  26.9 0.0 copy-start.4
  26.9 0.9 %fusion = f32[4096,256]{1,0:T(8,128)S(1)} fusion(f32[4096,256]{1,0:T(8,128)S(1)} %fusion.32, f32[4096,256]{1,0:T(8,128)S(1)} %convolution_add_fusion.1, bf16[4096,256]{1,0:T(8,128)(2,1)S(1)} %bitcast.82, bf16[3,3,256,256]{3,2,1,0:T(8,128)(2,1)S(1)} %copy-done.1), kind=kOutput, calls=%fused_computation.9 | convolution fusion | flops 538968064 | bytes 14811136 | tf_op jit(solution)/shard_map/dot_general | solution.py:55
  27.8 0.8 %fusion.11 = bf16[2,16,128,256]{3,2,1,0:T(8,128)(2,1)S(1)} fusion(f32[2,16,128,256]{3,2,1,0:T(8,128)S(1)} %bitcast.79, bf16[2,16,128,256]{3,2,1,0:T(8,128)(2,1)S(1)} %copy-done, f32[256]{0:T(256)S(1)} %copy-done.4), kind=kLoop, calls=%fused_computation.26 | loop fusion | flops 4194304 | bytes 8389632 | tf_op jit(solution)/shard_map/convert_element_type | solution.py:60
  28.7 0.0 copy-start.5
  28.7 0.6 fusion.12
  29.3 0.0 copy-done.5
  29.4 1.4 %fusion.19 = bf16[2,16,128,256]{3,2,1,0:T(8,128)(2,1)S(1)} fusion(bf16[2,16,128,256]{3,2,1,0:T(8,128)(2,1)S(1)} %fusion.11, f32[256]{0:T(256)S(1)} %copy-done.5, f32[2,16,128]{2,1,0:T(8,128)S(1)} %add_rsqrt_fusion), kind=kLoop, calls=%fused_computation.34 | loop fusion | flops 8388608 | bytes 4211712 | tf_op jit(solution)/shard_map/convert_element_type | solution.py:33
  30.7 2.1 %collective-permute-start.2 = (bf16[2,16,128,256]{3,2,1,0:T(8,128)(2,1)S(1)}, bf16[2,16,128,256]{3,2,1,0:T(8,128)(2,1)S(1)}, u32[]{:S(2)}, u32[]{:S(2)}) collective-permute-start(bf16[2,16,128,256]{3,2,1,0:T(8,128)(2,1)S(1)} %fusion.19), channel_id=1, source_target_pairs={{0,4},{4,8},{8,12},{1,5},{5,9},{9,13},{2,6},{6,10},{10,14},{3,7},{... | collective-permute-start | bytes 6291464 | tf_op jit(solution)/shard_map/ppermute | solution.py:23
  32.9 0.4 convolution_bitcast_fusion.1
  33.3 0.7 %fusion.28 = f32[2,16,128,256]{3,2,1,0:T(8,128)S(1)} fusion(bf16[2,16,128,256]{3,2,1,0:T(8,128)(2,1)S(1)} %fusion.19, bf16[3,256,256]{2,1,0:T(8,128)(2,1)S(1)} %copy-done.2), kind=kOutput, calls=%fused_computation.50 | convolution fusion | flops 536870912 | bytes 6422528 | tf_op jit(solution)/shard_map/dot_general | solution.py:38
  34.0 24.1 %collective-permute-done.2 = bf16[2,16,128,256]{3,2,1,0:T(8,128)(2,1)S(1)} collective-permute-done((bf16[2,16,128,256]{3,2,1,0:T(8,128)(2,1)S(1)}, bf16[2,16,128,256]{3,2,1,0:T(8,128)(2,1)S(1)}, u32[]{:S(2)}, u32[]{:S(2)}) %collective-permute-start.2) | collective-permute-done | bytes 2097184 | tf_op jit(solution)/shard_map/ppermute | solution.py:23
  58.1 0.4 convolution_bitcast_fusion
  58.5 0.9 %add_convert_fusion = bf16[2,16,128,256]{3,2,1,0:T(8,128)(2,1)S(1)} fusion(f32[1,16,128,256]{3,2,1,0:T(8,128)S(1)} %convolution_bitcast_fusion, f32[2,16,128,256]{3,2,1,0:T(8,128)S(1)} %fusion.28, f32[1,16,128,256]{3,2,1,0:T(8,128)S(1)} %convolution_bitcast_fusion.1, bf16[2,16,128,256]{3,2,1,0:T(8,128)(2,1)S(1)} %collective-permute-done.2, ...), kind=kOutput, calls=%fused_computation.37 | convolution fusion | flops 541065216 | bytes 12713984 | tf_op jit(solution)/shard_map/dot_general | solution.py:38
  59.4 2.2 %fusion.21 = bf16[2,16,128,256]{3,2,1,0:T(8,128)(2,1)} fusion(bf16[2,16,128,256]{3,2,1,0:T(8,128)(2,1)S(1)} %fusion.11, bf16[2,16,128,256]{3,2,1,0:T(8,128)(2,1)S(1)} %add_convert_fusion, f32[256]{0:T(256)S(1)} %copy-done.6), kind=kLoop, calls=%fused_computation.36 | loop fusion | flops 5242880 | bytes 6292480 | tf_op jit(solution)/shard_map/convert_element_type | solution.py:76
  (13 shorter events, 0.1 us)
Async XLA Ops:
  0.0 2.4 %copy-start = (bf16[2,16,128,256]{3,2,1,0:T(8,128)(2,1)S(1)}, bf16[2,16,128,256]{3,2,1,0:T(8,128)(2,1)}, u32[]{:S(2)}) copy-start(bf16[2,16,128,256]{3,2,1,0:T(8,128)(2,1)} %param.7) | copy-start | bytes 6291460
  0.0 2.4 %copy-start.3 = (f32[256]{0:T(256)S(1)}, f32[256]{0:T(256)}, u32[]{:S(2)}) copy-start(f32[256]{0:T(256)} %param.9) | copy-start | bytes 3076
  3.8 7.1 %collective-permute-start = (bf16[2,1,128,256]{3,2,1,0:T(8,128)(2,1)S(1)}, bf16[2,1,128,256]{3,2,1,0:T(8,128)(2,1)S(1)}, u32[]{:S(2)}, u32[]{:S(2)}) collective-permute-start(bf16[2,1,128,256]{3,2,1,0:T(8,128)(2,1)S(1)} %get-tuple-element.13), channel_id=1, source_target_pairs={{0,1},{1,2},{2,3},{4,5},{5,6},{6,7},{8,9},{9,10},{10,11},{12,13},{... | collective-permute-start | bytes 393224 | tf_op jit(solution)/shard_map/ppermute | solution.py:14
  7.3 6.9 %collective-permute-start.1 = (bf16[2,1,128,256]{3,2,1,0:T(8,128)(2,1)S(1)}, bf16[2,1,128,256]{3,2,1,0:T(8,128)(2,1)S(1)}, u32[]{:S(2)}, u32[]{:S(2)}) collective-permute-start(bf16[2,1,128,256]{3,2,1,0:T(8,128)(2,1)S(1)} %get-tuple-element.14), channel_id=1, source_target_pairs={{1,0},{2,1},{3,2},{5,4},{6,5},{7,6},{9,8},{10,9},{11,10},{13,12},{... | collective-permute-start | bytes 393224 | tf_op jit(solution)/shard_map/ppermute | solution.py:15
  15.3 5.2 %copy-start.1 = (bf16[3,3,256,256]{3,2,1,0:T(8,128)(2,1)S(1)}, bf16[3,3,256,256]{3,2,1,0:T(8,128)(2,1)}, u32[]{:S(2)}) copy-start(bf16[3,3,256,256]{3,2,1,0:T(8,128)(2,1)} %param.8) | copy-start | bytes 3538948
  26.9 1.0 %copy-start.4 = (f32[256]{0:T(256)S(1)}, f32[256]{0:T(256)}, u32[]{:S(2)}) copy-start(f32[256]{0:T(256)} %param.10) | copy-start | bytes 3076
  28.7 0.7 %copy-start.5 = (f32[256]{0:T(256)S(1)}, f32[256]{0:T(256)}, u32[]{:S(2)}) copy-start(f32[256]{0:T(256)} %param.12) | copy-start | bytes 3076
  29.4 3.5 %copy-start.2 = (bf16[3,256,256]{2,1,0:T(8,128)(2,1)S(1)}, bf16[3,256,256]{2,1,0:T(8,128)(2,1)}, u32[]{:S(2)}) copy-start(bf16[3,256,256]{2,1,0:T(8,128)(2,1)} %param.11) | copy-start | bytes 1179652
  30.7 27.4 %collective-permute-start.2 = (bf16[2,16,128,256]{3,2,1,0:T(8,128)(2,1)S(1)}, bf16[2,16,128,256]{3,2,1,0:T(8,128)(2,1)S(1)}, u32[]{:S(2)}, u32[]{:S(2)}) collective-permute-start(bf16[2,16,128,256]{3,2,1,0:T(8,128)(2,1)S(1)} %fusion.19), channel_id=1, source_target_pairs={{0,4},{4,8},{8,12},{1,5},{5,9},{9,13},{2,6},{6,10},{10,14},{3,7},{... | collective-permute-start | bytes 6291464 | tf_op jit(solution)/shard_map/ppermute | solution.py:23
  58.5 0.9 %copy-start.6 = (f32[256]{0:T(256)S(1)}, f32[256]{0:T(256)}, u32[]{:S(2)}) copy-start(f32[256]{0:T(256)} %param.13) | copy-start | bytes 3076
where the time goes:
time: 62 us; the launch traced here: 61.6 us
  waiting for transfers between devices  28.6 us (46%)
  other arithmetic  10.1 us (16%)
  matrix products  9.43 us (15%)
  starting transfers between devices  7.94 us (13%)
  local copies, waits for them, and re-layouts  5.29 us (9%)
    ppermute x1, waiting for transfers between devices, passed_along(): return lax.ppermute(array, axis, pairs)  24.1 us
    dot_general x9, matrix products, body(): jnp.dot(window, space_kernel[tap_row, tap_col], preferred_element_type=jn...  6.97 us
    slice x1, local copies, waits for them, and re-layouts, body(): padded[:, tap_row:tap_row + rows_count, tap_col:tap_col + cols_count]  5.21 us
    ppermute x1, starting transfers between devices, with_halo(): before = lax.ppermute(last, axis, up)  3.48 us
    ppermute x1, waiting for transfers between devices, with_halo(): after = lax.ppermute(first, axis, down)  3.22 us
    reduce_sum x2, other arithmetic, rms_silu(): jnp.mean(widened * widened, axis=-1, keepdims=True) + 1e-06  2.97 us
    convert_element_type x2, other arithmetic, rms_silu(): return jax.nn.silu(scaled).astype(jnp.bfloat16)  2.78 us
    dot_general x4, matrix products, lag_product(): jnp.dot(frames_in.reshape(-1, channels), kernel_slice, preferred_element_...  2.45 us
  transfers between devices with their start and end apart: 3, of which 3 were waited for; matrix products, arithmetic and copies ran while one was open for 2% of the time, Pallas kernels for 0%

commit v1 on v0

v1 whole, which is shorter than its diff:
```python
import functools

import jax
import jax.numpy as jnp
from jax import lax
from jax.experimental import pallas as pl
from jax.experimental.pallas import tpu as pltpu
from jax.sharding import PartitionSpec as P

F32 = jnp.float32
BF16 = jnp.bfloat16


def half_silu(values, half_gain):
    mean_square = jnp.mean(values * values, axis=-1, keepdims=True)
    u = values * lax.rsqrt(mean_square + 1e-06) * half_gain
    return u + u * jnp.tanh(u)


def norm_into(shifted, place, row, half_gain):
    normed = half_silu(row.astype(F32), half_gain)
    cols = normed.shape[0]
    column = lax.broadcasted_iota(jnp.int32, normed.shape, 0)
    before = jnp.where(column == 0, 0.0, pltpu.roll(normed, 1, 0))
    after = jnp.where(column == cols - 1, 0.0, pltpu.roll(normed, cols - 1, 0))
    shifted[0, place] = before.astype(BF16)
    shifted[1, place] = normed.astype(BF16)
    shifted[2, place] = after.astype(BF16)


def conv_rows(shifted, kernel, first, count):
    _, _, cols, channels = shifted.shape
    total = None
    for i in range(3):
        for j in range(3):
            window = shifted[j, first + i : first + i + count].reshape(count * cols, channels)
            product = jnp.dot(window, kernel[i, j], preferred_element_type=F32)
            total = product if total is None else total + product
    return total


def spatial_rows(get_row, rows, step, shifted, kernel, space_half, space_bias, time_half, emit):
    channels = shifted.shape[-1]
    ready = 0
    for first in range(0, rows, step):
        while ready < first + step + 2:
            norm_into(shifted, ready, get_row(ready - 1), space_half)
            ready += 1
        total = conv_rows(shifted, kernel, first, step)
        own = jnp.concatenate([get_row(r) for r in range(first, first + step)], axis=0)
        hidden = (own.astype(F32) + total + space_bias).astype(BF16)
        emit(first, hidden, half_silu(hidden.astype(F32), time_half))


def own_kernel(frame, step, feats, above, below, kernel, space_half, space_bias, time_half,
               hidden_ref, *rest):
    *normed_refs, shifted = rest
    rows = feats.shape[1]

    def get_row(r):
        if r < 0:
            return above[frame]
        if r >= rows:
            return below[frame]
        return feats[0, r]

    starts = []
    for ref in normed_refs:
        starts.append(sum(other.shape[0] for other in normed_refs[: len(starts)]))

    def emit(first, hidden, normed):
        cols, channels = feats.shape[2:]
        hidden_ref[first : first + step] = hidden.reshape(step, cols, channels)
        which = max(n for n, s in enumerate(starts) if s <= first)
        at = first - starts[which]
        normed_refs[which][at : at + step] = normed.astype(BF16).reshape(step, cols, channels)

    spatial_rows(get_row, rows, step, shifted, kernel[...], space_half[...], space_bias[...],
                 time_half[...], emit)


def joint_kernel(step, valid, edge, inner, above, below, kernel, space_half, space_bias, time_half,
                 time_kernel, time_bias, hidden_b, normed_b, *rest):
    *normed_a, out_ref, partial, shifted = rest
    rows, cols, channels = hidden_b.shape
    starts = []
    for ref in normed_a:
        starts.append(sum(other.shape[0] for other in normed_a[: len(starts)]))
    keep = valid[0]

    def get_row(r):
        if r < 0:
            return above[2]
        if r >= rows:
            return below[2]
        if r == 0:
            return edge[0]
        if r == rows - 1:
            return edge[1]
        return inner[r - 1]

    def flat(ref, first):
        return ref[first : first + step].reshape(step * cols, channels)

    def emit(first, hidden, normed):
        prior = jnp.where(keep > 0, normed, 0.0).astype(BF16)
        which = max(n for n, s in enumerate(starts) if s <= first)
        before = flat(normed_a[which], first - starts[which])
        total = jnp.dot(flat(normed_b, first), time_kernel[0], preferred_element_type=F32)
        total += jnp.dot(before, time_kernel[1], preferred_element_type=F32)
        total += jnp.dot(prior, time_kernel[2], preferred_element_type=F32)
        temporal = total.astype(BF16).astype(F32)
        decoded = flat(hidden_b, first).astype(F32) + temporal + time_bias[...]
        out_ref[0, first : first + step] = decoded.astype(BF16).reshape(step, cols, channels)
        other = jnp.dot(before, time_kernel[0], preferred_element_type=F32)
        other += jnp.dot(prior, time_kernel[1], preferred_element_type=F32)
        partial[first : first + step] = other.reshape(step, cols, channels)

    spatial_rows(get_row, rows, step, shifted, kernel[...], space_half[...], space_bias[...],
                 time_half[...], emit)


def last_kernel(arrived, partial, hidden, time_kernel, time_bias, _, out_ref):
    count, cols, channels = arrived.shape
    total = partial[...].reshape(count * cols, channels)
    total += jnp.dot(arrived[...].reshape(count * cols, channels), time_kernel[0],
                     preferred_element_type=F32)
    temporal = total.astype(BF16).astype(F32)
    decoded = hidden[...].reshape(count * cols, channels).astype(F32) + temporal + time_bias[...]
    out_ref[0] = decoded.astype(BF16).reshape(count, cols, channels)


def whole(shape):
    return pl.BlockSpec(shape, lambda *_: (0,) * len(shape))


def chunks_of(rows):
    head = rows - rows // 4
    return (head, rows - head)


def body(features, space_kernel, space_gain, space_bias, time_kernel, time_gain, time_bias):
    frames, rows, cols, channels = features.shape
    row_shape = (cols, channels)
    step = 2
    sizes = chunks_of(rows)
    pixels = rows * cols
    count_f, count_b = lax.axis_size("frame"), lax.axis_size("band")
    onward = [(i, i + 1) for i in range(count_f - 1)]
    up = [(i, i + 1) for i in range(count_b - 1)]
    down = [(j, i) for i, j in up]
    params = pltpu.CompilerParams(vmem_limit_bytes=32 * 1024 * 1024)
    flops_conv = 2 * 9 * pixels * channels * channels

    space_half = (0.5 * space_gain).reshape(1, channels)
    time_half = (0.5 * time_gain).reshape(1, channels)
    space_bias = space_bias.reshape(1, channels)
    time_bias = time_bias.reshape(1, channels)
    valid = (lax.axis_index("frame") > 0).astype(jnp.int32).reshape(1)

    last = features[1]
    edge = lax.ppermute(jnp.stack([last[0], last[rows - 1]]), "frame", onward)
    inner = lax.ppermute(last[1 : rows - 1], "frame", onward)
    above = lax.ppermute(
        jnp.concatenate([features[:, rows - 1], edge[1:]], axis=0), "band", up
    )
    below = lax.ppermute(jnp.concatenate([features[:, 0], edge[:1]], axis=0), "band", down)

    def own(frame, parts):
        return pl.pallas_call(
            functools.partial(own_kernel, frame, step),
            grid=(1,),
            in_specs=[
                pl.BlockSpec((1, rows) + row_shape, lambda *_: (frame, 0, 0, 0)),
                whole(above.shape), whole(below.shape), whole(space_kernel.shape),
                whole(space_half.shape), whole(space_bias.shape), whole(time_half.shape),
            ],
            out_specs=[whole((rows,) + row_shape)] + [whole((n,) + row_shape) for n in parts],
            out_shape=[jax.ShapeDtypeStruct((n,) + row_shape, BF16) for n in (rows,) + parts],
            scratch_shapes=[pltpu.VMEM((3, rows + 2) + row_shape, BF16)],
            compiler_params=params,
            cost_estimate=pl.CostEstimate(
                flops=flops_conv, bytes_accessed=5 * pixels * channels * 2, transcendentals=2 * pixels * channels
            ),
            name=f"own_frame_{frame}",
        )(features, above, below, space_kernel, space_half, space_bias, time_half)

    hidden_a, *normed_a = own(0, sizes)
    arrived = [lax.ppermute(part, "frame", onward) for part in normed_a]
    hidden_b, normed_b = own(1, (rows,))

    inputs = [valid, edge, inner, above, below, space_kernel, space_half, space_bias, time_half,
              time_kernel, time_bias, hidden_b, normed_b, *normed_a]
    decoded, partial = pl.pallas_call(
        functools.partial(joint_kernel, step),
        grid=(1,),
        in_specs=[pl.BlockSpec(memory_space=pltpu.SMEM)] + [whole(x.shape) for x in inputs[1:]],
        out_specs=[
            pl.BlockSpec((1, rows) + row_shape, lambda *_: (1, 0, 0, 0)),
            whole((rows,) + row_shape),
        ],
        out_shape=[
            jax.ShapeDtypeStruct(features.shape, BF16),
            jax.ShapeDtypeStruct((rows,) + row_shape, F32),
        ],
        scratch_shapes=[pltpu.VMEM((3, rows + 2) + row_shape, BF16)],
        compiler_params=params,
        cost_estimate=pl.CostEstimate(
            flops=flops_conv * 14 // 9, bytes_accessed=10 * pixels * channels * 2,
            transcendentals=2 * pixels * channels,
        ),
        name="joint",
    )(*inputs)

    first = 0
    for part in arrived:
        count = part.shape[0]
        block = next(b for b in range(min(count, 4), 0, -1) if count % b == 0 and first % b == 0)
        base = first // block
        row_block = pl.BlockSpec((block,) + row_shape, lambda i, base=base: (base + i, 0, 0))
        decoded = pl.pallas_call(
            last_kernel,
            grid=(count // block,),
            in_specs=[
                pl.BlockSpec((block,) + row_shape, lambda i: (i, 0, 0)),
                row_block, row_block,
                pl.BlockSpec((1,) + time_kernel.shape[1:], lambda i: (2, 0, 0)),
                whole(time_bias.shape),
                pl.BlockSpec(memory_space=pl.ANY),
            ],
            out_specs=pl.BlockSpec((1, block) + row_shape, lambda i, base=base: (0, base + i, 0, 0)),
            out_shape=jax.ShapeDtypeStruct(features.shape, BF16),
            input_output_aliases={5: 0},
            compiler_params=params,
            cost_estimate=pl.CostEstimate(
                flops=2 * count * cols * channels * channels,
                bytes_accessed=10 * count * cols * channels, transcendentals=0,
            ),
            name="finish",
        )(part, partial, hidden_a, time_kernel, time_bias, decoded)
        first += count
    return decoded


def solution(mesh):
    return jax.shard_map(
        body,
        mesh=mesh,
        in_specs=(P(("grp", "frame"), "band", None, None), P(), P(), P(), P(), P(), P()),
        out_specs=P(("grp", "frame"), "band", None, None),
        check_vma=False,
    )
```

time: 62 us -> 51.3 us (0.83)
  the two profiles are of different devices: /device:TPU:18 before, /device:TPU:0 now
where the time goes in v1:
time: 51.3 us; the launch traced here: 50.9 us
  Pallas kernels  21.6 us (42%)
  starting transfers between devices  16.4 us (32%)
  local copies, waits for them, and re-layouts  6.39 us (12%)
  waiting for transfers between devices  6.25 us (12%)
    pallas_call x1, Pallas kernels, body(): pl.pallas_call(functools.partial(joint_kernel, step), grid=(1,), in_specs...  10.2 us
    pallas_call x2, Pallas kernels, own(): pl.pallas_call(functools.partial(own_kernel, frame, step), grid=(1,), in_...  7.11 us
    ppermute x1, starting transfers between devices, body(): inner = lax.ppermute(last[1:rows - 1], 'frame', onward)  5.44 us
    pallas_call x2, Pallas kernels, body(): pl.pallas_call(last_kernel, grid=(count // block,), in_specs=[pl.BlockSpe...  4.21 us
    ppermute x1, waiting for transfers between devices, body(): lax.ppermute(jnp.concatenate([features[:, 0], edge[:1]], axis=0), 'band',...  4.2 us
    ppermute x2, starting transfers between devices, body(): arrived = [lax.ppermute(part, 'frame', onward) for part in normed_a]  3.82 us
    ppermute x1, starting transfers between devices, body(): lax.ppermute(jnp.concatenate([features[:, rows - 1], edge[1:]], axis=0),...  3.49 us
    unnamed x26, local copies, waits for them, and re-layouts  3.16 us
  transfers between devices with their start and end apart: 6, of which 2 were waited for; matrix products, arithmetic and copies ran while one was open for 4% of the time, Pallas kernels for 40%

profile of v1, /device:TPU:0, one launch (start us, length us, event | category | flops | bytes accessed | tf_op | source)
XLA Modules:
  0.0 50.9 jit_solution(6195173215538765126)
XLA Ops:
  0.0 1.0 %slice_bitcast_fusion.4 = (bf16[1,128,256]{2,1,0:T(8,128)(2,1)S(1)}, bf16[1,128,256]{2,1,0:T(8,128)(2,1)S(1)}) fusion(bf16[2,16,128,256]{3,2,1,0:T(8,128)(2,1)} %feats.3), kind=kLoop, calls=%fused_computation.7 | loop fusion | bytes 262144 | tf_op jit(solution)/shard_map/slice | solution.py:162
  1.1 2.4 %collective-permute-start = (bf16[2,128,256]{2,1,0:T(8,128)(2,1)S(1)}, bf16[2,128,256]{2,1,0:T(8,128)(2,1)S(1)}, u32[]{:S(2)}, u32[]{:S(2)}) collective-permute-start(bf16[2,128,256]{2,1,0:T(8,128)(2,1)S(1)} %pad_maximum_fusion.2), channel_id=1, source_target_pairs={{0,4},{4,8},{8,12},{1,5},{5,9},{9,13},{2,6},{6,10},{10,14},{3,7},{... | collective-permute-start | bytes 393224 | tf_op jit(solution)/shard_map/ppermute | solution.py:162
  3.5 2.2 %slice_bitcast_fusion = bf16[14,128,256]{2,1,0:T(8,128)(2,1)} fusion(bf16[2,16,128,256]{3,2,1,0:T(8,128)(2,1)} %feats.3), kind=kLoop, calls=%fused_computation | loop fusion | bytes 1835008 | tf_op jit(solution)/shard_map/slice | solution.py:163
  5.6 5.4 %collective-permute-start.4 = (bf16[14,128,256]{2,1,0:T(8,128)(2,1)}, bf16[14,128,256]{2,1,0:T(8,128)(2,1)}, u32[]{:S(2)}, u32[]{:S(2)}) collective-permute-start(bf16[14,128,256]{2,1,0:T(8,128)(2,1)} %slice_bitcast_fusion), channel_id=1, source_target_pairs={{0,4},{4,8},{8,12},{1,5},{5,9},{9,13},{2,6},{6,10},{10,14},{3,7},{... | collective-permute-start | bytes 2752520 | tf_op jit(solution)/shard_map/ppermute | solution.py:163
  11.1 0.0 copy-done.1
  11.1 0.0 copy-done.11
  11.1 0.0 collective-permute-done.edge
  11.2 3.5 %collective-permute-start.1 = (bf16[3,128,256]{2,1,0:T(8,128)(2,1)S(1)}, bf16[3,128,256]{2,1,0:T(8,128)(2,1)S(1)}, u32[]{:S(2)}, u32[]{:S(2)}) collective-permute-start(bf16[3,128,256]{2,1,0:T(8,128)(2,1)S(1)} %pad_maximum_fusion), channel_id=1, source_target_pairs={{0,1},{1,2},{2,3},{4,5},{5,6},{6,7},{8,9},{9,10},{10,11},{12,13},{... | collective-permute-start | bytes 589832 | tf_op jit(solution)/shard_map/ppermute | solution.py:164
  14.7 1.3 %collective-permute-start.2 = (bf16[3,128,256]{2,1,0:T(8,128)(2,1)S(1)}, bf16[3,128,256]{2,1,0:T(8,128)(2,1)S(1)}, u32[]{:S(2)}, u32[]{:S(2)}) collective-permute-start(bf16[3,128,256]{2,1,0:T(8,128)(2,1)S(1)} %pad_maximum_fusion.1), channel_id=1, source_target_pairs={{1,0},{2,1},{3,2},{5,4},{6,5},{7,6},{9,8},{10,9},{11,10},{13,12},{... | collective-permute-start | bytes 589832 | tf_op jit(solution)/shard_map/ppermute | solution.py:167
  16.0 0.0 copy-done.12
  16.0 2.0 %collective-permute-done.1.above = bf16[3,128,256]{2,1,0:T(8,128)(2,1)S(1)} collective-permute-done((bf16[3,128,256]{2,1,0:T(8,128)(2,1)S(1)}, bf16[3,128,256]{2,1,0:T(8,128)(2,1)S(1)}, u32[]{:S(2)}, u32[]{:S(2)}) %collective-permute-start.1) | collective-permute-done | bytes 196640 | tf_op jit(solution)/shard_map/ppermute | solution.py:164
  18.1 4.2 %collective-permute-done.2.below = bf16[3,128,256]{2,1,0:T(8,128)(2,1)S(1)} collective-permute-done((bf16[3,128,256]{2,1,0:T(8,128)(2,1)S(1)}, bf16[3,128,256]{2,1,0:T(8,128)(2,1)S(1)}, u32[]{:S(2)}, u32[]{:S(2)}) %collective-permute-start.2) | collective-permute-done | bytes 196640 | tf_op jit(solution)/shard_map/ppermute | solution.py:167
  22.3 0.0 copy-done.10
  22.3 0.0 copy-done.3
  22.3 3.8 %own_frame_0.1 = (bf16[16,128,256]{2,1,0:T(8,128)(2,1)S(1)}, bf16[12,128,256]{2,1,0:T(8,128)(2,1)}, bf16[4,128,256]{2,1,0:T(8,128)(2,1)S(1)}) custom-call(bf16[2,16,128,256]{3,2,1,0:T(8,128)(2,1)S(1)} %copy-done.1, bf16[3,128,256]{2,1,0:T(8,128)(2,1)S(1)} %collective-permute-done.1.above, bf16[3,128,256]{2,1,0:T(8,128)(2,1)S(1)} %collective-permute-done.2.below, ...), custom_call_target="tpu_custom_call" | custom-call | flops 2415919104 | bytes 5242880 | tf_op jit(solution)/shard_map/own_frame_0/pallas_call | solution.py:170
  26.1 0.0 copy-done.8
  26.1 2.2 %collective-permute-start.5 = (bf16[12,128,256]{2,1,0:T(8,128)(2,1)}, bf16[12,128,256]{2,1,0:T(8,128)(2,1)}, u32[]{:S(2)}, u32[]{:S(2)}) collective-permute-start(bf16[12,128,256]{2,1,0:T(8,128)(2,1)} %get-tuple-element.15.rest_0_), channel_id=1, source_target_pairs={{0,4},{4,8},{8,12},{1,5},{5,9},{9,13},{2,6},{6,10},{10,14},{3,7},{... | collective-permute-start | bytes 2359304 | tf_op jit(solution)/shard_map/ppermute | solution.py:189
  28.3 1.6 %collective-permute-start.3 = (bf16[4,128,256]{2,1,0:T(8,128)(2,1)S(1)}, bf16[4,128,256]{2,1,0:T(8,128)(2,1)S(1)}, u32[]{:S(2)}, u32[]{:S(2)}) collective-permute-start(bf16[4,128,256]{2,1,0:T(8,128)(2,1)S(1)} %get-tuple-element.12.rest_1_), channel_id=1, source_target_pairs={{0,4},{4,8},{8,12},{1,5},{5,9},{9,13},{2,6},{6,10},{10,14},{3,7},{... | collective-permute-start | bytes 786440 | tf_op jit(solution)/shard_map/ppermute | solution.py:189
  30.0 0.0 copy-start.4
  30.0 1.3 %copy-done.4 = bf16[3,3,256,256]{3,2,1,0:T(8,128)(2,1)S(1)} copy-done((bf16[3,3,256,256]{3,2,1,0:T(8,128)(2,1)S(1)}, bf16[3,3,256,256]{3,2,1,0:T(8,128)(2,1)}, u32[]{:S(2)}) %copy-start.4) | copy-done | bytes 1179672
  31.2 0.9 %copy-done.7 = bf16[3,128,256]{2,1,0:T(8,128)(2,1)S(1)} copy-done((bf16[3,128,256]{2,1,0:T(8,128)(2,1)S(1)}, bf16[3,128,256]{2,1,0:T(8,128)(2,1)}, u32[]{:S(2)}) %copy-start.7) | copy-done | bytes 196632
  32.2 0.9 %copy-done.9 = bf16[3,128,256]{2,1,0:T(8,128)(2,1)S(1)} copy-done((bf16[3,128,256]{2,1,0:T(8,128)(2,1)S(1)}, bf16[3,128,256]{2,1,0:T(8,128)(2,1)}, u32[]{:S(2)}) %copy-start.9) | copy-done | bytes 196632
  33.1 3.3 %own_frame_1.1 = (bf16[16,128,256]{2,1,0:T(8,128)(2,1)S(1)}, bf16[16,128,256]{2,1,0:T(8,128)(2,1)S(1)}) custom-call(bf16[2,16,128,256]{3,2,1,0:T(8,128)(2,1)S(1)} %copy-done.1, bf16[3,128,256]{2,1,0:T(8,128)(2,1)S(1)} %copy-done.7, bf16[3,128,256]{2,1,0:T(8,128)(2,1)S(1)} %copy-done.9, bf16[3,3,256,256]{3,2,1,0:T(8,128)(2,1)S(1)} %copy-done.4, ...), custom_call_target="tpu_custom_call" | custom-call | flops 2415919104 | bytes 5242880 | tf_op jit(solution)/shard_map/own_frame_1/pallas_call | solution.py:170
  36.4 0.0 collective-permute-done.4.inner
  36.4 0.0 copy-done
  36.4 0.0 copy-done.2
  36.4 0.0 copy-done.5
  36.4 10.2 %joint.1 = (bf16[2,16,128,256]{3,2,1,0:T(8,128)(2,1)}, f32[16,128,256]{2,1,0:T(8,128)S(1)}) custom-call(s32[1]{0:T(128)} %bitcast.7.valid, bf16[2,128,256]{2,1,0:T(8,128)(2,1)S(1)} %collective-permute-done.edge, bf16[14,128,256]{2,1,0:T(8,128)(2,1)} %collective-permute-done.4.inner, bf16[3,128,256]{2,1,0:T(8,128)(2,1)S(1)} %copy-done.7, ...), custom_call_target="tpu_custom_call" | custom-call | flops 3758096384 | bytes 10485760 | tf_op jit(solution)/shard_map/joint/pallas_call | solution.py:194
  46.6 0.0 collective-permute-done.5.arrived
  46.6 3.2 %finish.2._ = bf16[2,16,128,256]{3,2,1,0:T(8,128)(2,1)} custom-call(bf16[12,128,256]{2,1,0:T(8,128)(2,1)} %collective-permute-done.5.arrived, f32[16,128,256]{2,1,0:T(8,128)S(1)} %get-tuple-element.16.partial, bf16[16,128,256]{2,1,0:T(8,128)(2,1)S(1)} %get-tuple-element.17.hidden, bf16[3,256,256]{2,1,0:T(8,128)(2,1)S(1)} %copy-done, ...), custom_call_target="tpu_custom_call", output_to_operand_aliasing={{}: (5, {})} | custom-call | flops 201326592 | bytes 3932160 | tf_op jit(solution)/shard_map/finish/pallas_call | solution.py:221
  49.9 0.0 collective-permute-done.3.arrived
  49.9 1.0 %finish.3 = bf16[2,16,128,256]{3,2,1,0:T(8,128)(2,1)} custom-call(bf16[4,128,256]{2,1,0:T(8,128)(2,1)S(1)} %collective-permute-done.3.arrived, f32[16,128,256]{2,1,0:T(8,128)S(1)} %get-tuple-element.16.partial, bf16[16,128,256]{2,1,0:T(8,128)(2,1)S(1)} %get-tuple-element.17.hidden, bf16[3,256,256]{2,1,0:T(8,128)(2,1)S(1)} %copy-done, ...), custom_call_target="tpu_custom_call", output_to_operand_aliasing={{}: (5, {})} | custom-call | flops 67108864 | bytes 1310720 | tf_op jit(solution)/shard_map/finish/pallas_call | solution.py:221
  (20 shorter events, 0.1 us)
Async XLA Ops:
  0.0 11.1 %copy-start.1 = (bf16[2,16,128,256]{3,2,1,0:T(8,128)(2,1)S(1)}, bf16[2,16,128,256]{3,2,1,0:T(8,128)(2,1)}, u32[]{:S(2)}) copy-start(bf16[2,16,128,256]{3,2,1,0:T(8,128)(2,1)} %feats.3) | copy-start | bytes 6291460
  0.0 11.1 %copy-start.11 = (f32[256]{0:T(256)S(1)}, f32[256]{0:T(256)}, u32[]{:S(2)}) copy-start(f32[256]{0:T(256)} %param.9) | copy-start | bytes 3076
  0.0 16.0 %copy-start.12 = (f32[256]{0:T(256)S(1)}, f32[256]{0:T(256)}, u32[]{:S(2)}) copy-start(f32[256]{0:T(256)} %param.12) | copy-start | bytes 3076
  0.0 22.3 %copy-start.10 = (f32[256]{0:T(256)S(1)}, f32[256]{0:T(256)}, u32[]{:S(2)}) copy-start(f32[256]{0:T(256)} %param.10) | copy-start | bytes 3076
  0.0 22.3 %copy-start.3 = (bf16[3,3,256,256]{3,2,1,0:T(8,128)(2,1)S(1)}, bf16[3,3,256,256]{3,2,1,0:T(8,128)(2,1)}, u32[]{:S(2)}) copy-start(bf16[3,3,256,256]{3,2,1,0:T(8,128)(2,1)} %kernel.5) | copy-start | bytes 3538948
  1.1 10.0 %collective-permute-start = (bf16[2,128,256]{2,1,0:T(8,128)(2,1)S(1)}, bf16[2,128,256]{2,1,0:T(8,128)(2,1)S(1)}, u32[]{:S(2)}, u32[]{:S(2)}) collective-permute-start(bf16[2,128,256]{2,1,0:T(8,128)(2,1)S(1)} %pad_maximum_fusion.2), channel_id=1, source_target_pairs={{0,4},{4,8},{8,12},{1,5},{5,9},{9,13},{2,6},{6,10},{10,14},{3,7},{... | collective-permute-start | bytes 393224 | tf_op jit(solution)/shard_map/ppermute | solution.py:162
  5.6 30.7 %collective-permute-start.4 = (bf16[14,128,256]{2,1,0:T(8,128)(2,1)}, bf16[14,128,256]{2,1,0:T(8,128)(2,1)}, u32[]{:S(2)}, u32[]{:S(2)}) collective-permute-start(bf16[14,128,256]{2,1,0:T(8,128)(2,1)} %slice_bitcast_fusion), channel_id=1, source_target_pairs={{0,4},{4,8},{8,12},{1,5},{5,9},{9,13},{2,6},{6,10},{10,14},{3,7},{... | collective-permute-start | bytes 2752520 | tf_op jit(solution)/shard_map/ppermute | solution.py:163
  11.2 6.9 %collective-permute-start.1 = (bf16[3,128,256]{2,1,0:T(8,128)(2,1)S(1)}, bf16[3,128,256]{2,1,0:T(8,128)(2,1)S(1)}, u32[]{:S(2)}, u32[]{:S(2)}) collective-permute-start(bf16[3,128,256]{2,1,0:T(8,128)(2,1)S(1)} %pad_maximum_fusion), channel_id=1, source_target_pairs={{0,1},{1,2},{2,3},{4,5},{5,6},{6,7},{8,9},{9,10},{10,11},{12,13},{... | collective-permute-start | bytes 589832 | tf_op jit(solution)/shard_map/ppermute | solution.py:164
  14.7 7.6 %collective-permute-start.2 = (bf16[3,128,256]{2,1,0:T(8,128)(2,1)S(1)}, bf16[3,128,256]{2,1,0:T(8,128)(2,1)S(1)}, u32[]{:S(2)}, u32[]{:S(2)}) collective-permute-start(bf16[3,128,256]{2,1,0:T(8,128)(2,1)S(1)} %pad_maximum_fusion.1), channel_id=1, source_target_pairs={{1,0},{2,1},{3,2},{5,4},{6,5},{7,6},{9,8},{10,9},{11,10},{13,12},{... | collective-permute-start | bytes 589832 | tf_op jit(solution)/shard_map/ppermute | solution.py:167
  18.1 8.1 %copy-start.6 = (bf16[3,128,256]{2,1,0:T(8,128)(2,1)}, bf16[3,128,256]{2,1,0:T(8,128)(2,1)S(1)}, u32[]{:S(2)}) copy-start(bf16[3,128,256]{2,1,0:T(8,128)(2,1)S(1)} %collective-permute-done.1.above) | copy-start | bytes 589828
  22.3 3.9 %copy-start.8 = (bf16[3,128,256]{2,1,0:T(8,128)(2,1)}, bf16[3,128,256]{2,1,0:T(8,128)(2,1)S(1)}, u32[]{:S(2)}) copy-start(bf16[3,128,256]{2,1,0:T(8,128)(2,1)S(1)} %collective-permute-done.2.below) | copy-start | bytes 589828
  26.1 20.5 %collective-permute-start.5 = (bf16[12,128,256]{2,1,0:T(8,128)(2,1)}, bf16[12,128,256]{2,1,0:T(8,128)(2,1)}, u32[]{:S(2)}, u32[]{:S(2)}) collective-permute-start(bf16[12,128,256]{2,1,0:T(8,128)(2,1)} %get-tuple-element.15.rest_0_), channel_id=1, source_target_pairs={{0,4},{4,8},{8,12},{1,5},{5,9},{9,13},{2,6},{6,10},{10,14},{3,7},{... | collective-permute-start | bytes 2359304 | tf_op jit(solution)/shard_map/ppermute | solution.py:189
  28.3 8.0 %copy-start = (bf16[3,256,256]{2,1,0:T(8,128)(2,1)S(1)}, bf16[3,256,256]{2,1,0:T(8,128)(2,1)}, u32[]{:S(2)}) copy-start(bf16[3,256,256]{2,1,0:T(8,128)(2,1)} %time_kernel.5) | copy-start | bytes 1179652
  28.3 8.0 %copy-start.2 = (f32[256]{0:T(256)S(1)}, f32[256]{0:T(256)}, u32[]{:S(2)}) copy-start(f32[256]{0:T(256)} %param.13) | copy-start | bytes 3076
  28.3 21.6 %collective-permute-start.3 = (bf16[4,128,256]{2,1,0:T(8,128)(2,1)S(1)}, bf16[4,128,256]{2,1,0:T(8,128)(2,1)S(1)}, u32[]{:S(2)}, u32[]{:S(2)}) collective-permute-start(bf16[4,128,256]{2,1,0:T(8,128)(2,1)S(1)} %get-tuple-element.12.rest_1_), channel_id=1, source_target_pairs={{0,4},{4,8},{8,12},{1,5},{5,9},{9,13},{2,6},{6,10},{10,14},{3,7},{... | collective-permute-start | bytes 786440 | tf_op jit(solution)/shard_map/ppermute | solution.py:189
  30.0 1.3 %copy-start.4 = (bf16[3,3,256,256]{3,2,1,0:T(8,128)(2,1)S(1)}, bf16[3,3,256,256]{3,2,1,0:T(8,128)(2,1)}, u32[]{:S(2)}) copy-start(bf16[3,3,256,256]{3,2,1,0:T(8,128)(2,1)} %kernel.5) | copy-start | bytes 3538948
  31.2 0.9 %copy-start.7 = (bf16[3,128,256]{2,1,0:T(8,128)(2,1)S(1)}, bf16[3,128,256]{2,1,0:T(8,128)(2,1)}, u32[]{:S(2)}) copy-start(bf16[3,128,256]{2,1,0:T(8,128)(2,1)} %copy-done.6) | copy-start | bytes 589828
  32.2 0.9 %copy-start.9 = (bf16[3,128,256]{2,1,0:T(8,128)(2,1)S(1)}, bf16[3,128,256]{2,1,0:T(8,128)(2,1)}, u32[]{:S(2)}) copy-start(bf16[3,128,256]{2,1,0:T(8,128)(2,1)} %copy-done.8) | copy-start | bytes 589828
  33.1 3.3 %copy-start.5 = (bf16[3,3,256,256]{3,2,1,0:T(8,128)(2,1)S(1)}, bf16[3,3,256,256]{3,2,1,0:T(8,128)(2,1)}, u32[]{:S(2)}) copy-start(bf16[3,3,256,256]{3,2,1,0:T(8,128)(2,1)} %kernel.5) | copy-start | bytes 3538948

commit v2 on v0

v2 whole, which is shorter than its diff:
```python
import functools

import jax
import jax.numpy as jnp
from jax import lax
from jax.experimental import pallas as pl
from jax.experimental.pallas import tpu as pltpu
from jax.sharding import PartitionSpec as P

F32 = jnp.float32
BF16 = jnp.bfloat16
VMEM = pl.BlockSpec(memory_space=pltpu.VMEM)
SMEM = pl.BlockSpec(memory_space=pltpu.SMEM)
ANY = pl.BlockSpec(memory_space=pl.ANY)
HBM = pl.BlockSpec(memory_space=pltpu.HBM)
STEP = 2


def blocks(first, last):
    return [(r, min(STEP, last - r)) for r in range(first, last, STEP)]


def half_silu(values, half_gain):
    mean_square = jnp.mean(values * values, axis=-1, keepdims=True)
    u = values * lax.rsqrt(mean_square + 1e-06) * half_gain
    return u + u * jnp.tanh(u)


def norm_into(shifted, place, row, half_gain):
    normed = half_silu(row.astype(F32), half_gain)
    cols = normed.shape[0]
    column = lax.broadcasted_iota(jnp.int32, normed.shape, 0)
    before = jnp.where(column == 0, 0.0, pltpu.roll(normed, 1, 0))
    after = jnp.where(column == cols - 1, 0.0, pltpu.roll(normed, cols - 1, 0))
    shifted[0, place] = before.astype(BF16)
    shifted[1, place] = normed.astype(BF16)
    shifted[2, place] = after.astype(BF16)


def conv_rows(shifted, kernel, place, count):
    cols, channels = shifted.shape[2:]
    total = None
    for i in range(3):
        for j in range(3):
            window = shifted[j, place + i : place + i + count].reshape(count * cols, channels)
            product = jnp.dot(window, kernel[i, j], preferred_element_type=F32)
            total = product if total is None else total + product
    return total


def spatial_jobs(get_row, row_blocks, offset, shifted, sums, slot0, kernel, weights, emit, after=None):
    space_half, space_bias, time_half = weights
    ready = set()
    jobs = []

    def norm_stage(first, count):
        for r in range(first - 1, first + count + 1):
            if r not in ready:
                ready.add(r)
                norm_into(shifted, r + offset, get_row(r), space_half[...])

    def conv_stage(slot, first, count):
        total = conv_rows(shifted, kernel, first - 1 + offset, count)
        sums[slot, : total.shape[0]] = total

    def emit_stage(slot, first, count):
        own = jnp.concatenate([get_row(r) for r in range(first, first + count)], axis=0)
        hidden = own.astype(F32) + sums[slot, : own.shape[0]] + space_bias[...]
        emit(first, count, hidden, half_silu(hidden, time_half[...]))

    for n, (first, count) in enumerate(row_blocks):
        slot = (slot0 + n) % sums.shape[0]
        jobs.append([
            functools.partial(norm_stage, first, count),
            functools.partial(conv_stage, slot, first, count),
            functools.partial(emit_stage, slot, first, count),
            functools.partial(after, first, count) if after else None,
        ])
    return jobs


def run(jobs):
    for n in range(len(jobs) + 3):
        for stage in range(4):
            if 0 <= n - stage < len(jobs) and jobs[n - stage][stage] is not None:
                jobs[n - stage][stage]()


def split_kernel(feats, edge, inner, tops, bottoms, sems):
    rows = feats.shape[1]
    pairs = [
        (feats.at[1, pl.ds(0, 1)], edge.at[pl.ds(0, 1)]),
        (feats.at[1, pl.ds(rows - 1, 1)], edge.at[pl.ds(1, 1)]),
        (feats.at[pl.ds(0, 2), 0], tops),
        (feats.at[pl.ds(0, 2), rows - 1], bottoms),
        (feats.at[1, pl.ds(1, rows - 2)], inner),
    ]
    copies = [pltpu.make_async_copy(a, b, sems.at[n]) for n, (a, b) in enumerate(pairs)]
    for copy in copies:
        copy.start()
    for copy in copies:
        copy.wait()


def interior_kernel(feats, kernel, time_kernel, space_half, space_bias, time_half,
                    hidden_ref, normed_ref, raw, kernel_out, time_out, shifted, sums, sems):
    rows, cols, channels = raw.shape
    half = rows // 2
    pairs = [
        (feats.at[0, pl.ds(0, half)], raw.at[pl.ds(0, half)]),
        (kernel, kernel_out),
        (feats.at[0, pl.ds(half, rows - half)], raw.at[pl.ds(half, rows - half)]),
        (time_kernel, time_out),
    ]
    copies = [pltpu.make_async_copy(a, b, sems.at[n]) for n, (a, b) in enumerate(pairs)]
    for copy in copies:
        copy.start()

    def emit(first, count, hidden, normed):
        shape = (count, cols, channels)
        hidden_ref[first - 1 : first - 1 + count] = hidden.astype(BF16).reshape(shape)
        normed_ref[first - 1 : first - 1 + count] = normed.astype(BF16).reshape(shape)

    jobs = spatial_jobs(lambda r: raw[r], blocks(1, rows - 1), 0, shifted, sums, 0, kernel_out,
                        (space_half, space_bias, time_half), emit)
    copies[0].wait()
    jobs[0][0]()
    jobs[0][0] = None
    for copy in copies[1:]:
        copy.wait()
    run(jobs)


def main_kernel(valid, raw_a, own_edge, own_inner, edge, inner, above, below, kernel, space_half, space_bias, time_half,
                time_kernel, time_bias, hidden_a, normed_a,
                out_ref, base, edge_normed,
                shift_a, shift_b, shift_p, sums, hidden_b, normed_b, normed_p, hidden_e, decoded, sems):
    rows, cols, channels = raw_a.shape
    keep = valid[0]
    weights = (space_half, space_bias, time_half)

    def a_row(r):
        return above[0] if r < 0 else below[0] if r >= rows else raw_a[r]

    def framed(upper, edges, inners, lower):
        def get_row(r):
            if r < 0 or r >= rows:
                return (upper if r < 0 else lower)[...]
            return edges[0] if r == 0 else edges[1] if r == rows - 1 else inners[r - 1]
        return get_row

    def emit_a(first, count, hidden, normed):
        which = 0 if first == 0 else 1
        hidden_e[which] = hidden
        edge_normed[which] = normed.astype(BF16)

    def emit_b(first, count, hidden, normed):
        hidden_b[first : first + count] = hidden.reshape(count, cols, channels)
        normed_b[first : first + count] = normed.astype(BF16).reshape(count, cols, channels)

    def emit_p(first, count, hidden, normed):
        normed_p[first : first + count] = (normed * keep).astype(BF16).reshape(count, cols, channels)

    def rows_of(first, count, of_edge, of_inner):
        parts = []
        for r in range(first, first + count):
            parts.append(of_edge[0] if r == 0 else of_edge[1] if r == rows - 1 else of_inner[r - 1])
        return jnp.concatenate(parts, axis=0)

    def out_rows(first, count):
        size = count * cols
        before = rows_of(first, count, edge_normed, normed_a)
        mine = normed_b[first : first + count].reshape(size, channels)
        prior = normed_p[first : first + count].reshape(size, channels)
        total = hidden_b[first : first + count].reshape(size, channels) + time_bias[...]
        total += (
            jnp.dot(mine, time_kernel[0], preferred_element_type=F32)
            + jnp.dot(before, time_kernel[1], preferred_element_type=F32)
            + jnp.dot(prior, time_kernel[2], preferred_element_type=F32)
        )
        decoded[first : first + count] = total.astype(BF16).reshape(count, cols, channels)

    def base_rows(first, count):
        before = rows_of(first, count, edge_normed, normed_a)
        prior = normed_p[first : first + count].reshape(count * cols, channels)
        other = rows_of(first, count, hidden_e, hidden_a).astype(F32) + time_bias[...]
        other += (
            jnp.dot(before, time_kernel[0], preferred_element_type=F32)
            + jnp.dot(prior, time_kernel[1], preferred_element_type=F32)
        )
        base[first : first + count] = other.reshape(count, cols, channels)

    b_row = framed(above.at[1], own_edge, own_inner, below.at[1])
    p_row = framed(above.at[2], edge, inner, below.at[2])
    top = spatial_jobs(a_row, [(0, 1)], 1, shift_a.at[0], sums, 0, kernel, weights, emit_a)
    bottom = spatial_jobs(a_row, [(rows - 1, 1)], 2 - rows, shift_a.at[1], sums, 1, kernel,
                          weights, emit_a)
    mine = spatial_jobs(b_row, blocks(0, rows), 1, shift_b, sums, 2, kernel, weights, emit_b)
    prior = spatial_jobs(p_row, blocks(0, rows), 1, shift_p, sums, 2 + len(mine), kernel,
                         weights, emit_p)
    run(top + bottom + mine + prior)
    copies = []
    for n, (first, count) in enumerate(blocks(0, rows)):
        out_rows(first, count)
        copies.append(pltpu.make_async_copy(
            decoded.at[pl.ds(first, count)], out_ref.at[1, pl.ds(first, count)], sems.at[n]))
        copies[-1].start()
    for first, count in blocks(0, rows):
        base_rows(first, count)
    for copy in copies:
        copy.wait()


def finish_kernel(places, arrived, base, time_kernel, _, out_ref, decoded, sems):
    cols, channels = arrived.shape[1:]
    copies = []
    for n, (at, row, count) in enumerate(places):
        total = base[row : row + count].reshape(count * cols, channels)
        total += jnp.dot(arrived[at : at + count].reshape(count * cols, channels), time_kernel[2],
                         preferred_element_type=F32)
        decoded[at : at + count] = total.astype(BF16).reshape(count, cols, channels)
        copies.append(pltpu.make_async_copy(
            decoded.at[pl.ds(at, count)], out_ref.at[0, pl.ds(row, count)], sems.at[n]))
        copies[-1].start()
    for copy in copies:
        copy.wait()


def cost(pixels, taps, channels, arrays):
    return pl.CostEstimate(
        flops=2 * pixels * taps * channels * channels,
        bytes_accessed=2 * arrays * pixels * channels,
        transcendentals=2 * pixels * channels,
    )


def body(features, space_kernel, space_gain, space_bias, time_kernel, time_gain, time_bias):
    frames, rows, cols, channels = features.shape
    row = (cols, channels)
    count_f, count_b = lax.axis_size("frame"), lax.axis_size("band")
    onward = [(i, i + 1) for i in range(count_f - 1)]
    up = [(i, i + 1) for i in range(count_b - 1)]
    down = [(j, i) for i, j in up]

    def params(mebibytes):
        return pltpu.CompilerParams(vmem_limit_bytes=mebibytes * 1024 * 1024)

    def shape(*lead, dtype=BF16):
        return jax.ShapeDtypeStruct(tuple(lead) + row, dtype)

    def room(*lead, dtype=BF16):
        return pltpu.VMEM(tuple(lead) + row, dtype)

    space_half = (0.5 * space_gain).reshape(1, channels)
    time_half = (0.5 * time_gain).reshape(1, channels)
    space_bias = space_bias.reshape(1, channels)
    time_bias = time_bias.reshape(1, channels)
    valid = (lax.axis_index("frame") > 0).astype(F32).reshape(1)
    sums = pltpu.VMEM((4, STEP * cols, channels), F32)

    edge_out, inner_out, tops, bottoms = pl.pallas_call(
        split_kernel,
        in_specs=[HBM],
        out_specs=[VMEM] * 4,
        out_shape=[shape(2), shape(rows - 2), shape(2), shape(2)],
        scratch_shapes=[pltpu.SemaphoreType.DMA((5,))],
        compiler_params=params(2),
        name="split",
    )(pltpu.with_memory_space_constraint(features, pltpu.HBM))
    edge = lax.ppermute(edge_out, "frame", onward)
    inner = lax.ppermute(inner_out, "frame", onward)
    up_rows = jnp.concatenate([bottoms, edge[1:]], axis=0)
    down_rows = jnp.concatenate([tops, edge[:1]], axis=0)

    up_rows, down_rows, features = lax.optimization_barrier((up_rows, down_rows, features))
    above = lax.ppermute(up_rows, "band", up)
    below = lax.ppermute(down_rows, "band", down)
    hidden_a, normed_a, raw_a, space_kernel, time_kernel = pl.pallas_call(
        interior_kernel,
        in_specs=[HBM] * 3 + [VMEM] * 3,
        out_specs=[VMEM] * 5,
        out_shape=[shape(rows - 2), shape(rows - 2), shape(rows),
                   jax.ShapeDtypeStruct(space_kernel.shape, BF16),
                   jax.ShapeDtypeStruct(time_kernel.shape, BF16)],
        scratch_shapes=[room(3, rows), sums, pltpu.SemaphoreType.DMA((4,))],
        compiler_params=params(6),
        cost_estimate=cost(rows * cols, 9 * 4, channels, 3),
        name="interior",
    )(*(pltpu.with_memory_space_constraint(x, pltpu.HBM) for x in (features, space_kernel, time_kernel)),
      space_half, space_bias, time_half)
    arrived = lax.ppermute(normed_a, "frame", onward)

    inputs = [valid, raw_a, edge_out, inner_out, edge, inner, above, below, space_kernel, space_half, space_bias,
              time_half, time_kernel, time_bias, hidden_a, normed_a]
    decoded, base, edge_normed = pl.pallas_call(
        main_kernel,
        in_specs=[SMEM] + [VMEM] * (len(inputs) - 1),
        out_specs=[ANY, VMEM, VMEM],
        out_shape=[jax.ShapeDtypeStruct(features.shape, BF16), shape(rows, dtype=F32), shape(2)],
        scratch_shapes=[
            room(2, 3, 3), room(3, rows + 2), room(3, rows + 2), sums, room(rows, dtype=F32),
            room(rows), room(rows), room(2, dtype=F32), room(rows),
            pltpu.SemaphoreType.DMA((len(blocks(0, rows)),)),
        ],
        compiler_params=params(18),
        cost_estimate=cost(rows * cols, 23 * 8, channels, 10),
        name="main",
    )(*inputs)
    edge_arrived = lax.ppermute(edge_normed, "frame", onward)

    inner_places = [(r - 1, r, n) for r, n in blocks(1, rows - 1)]
    edge_places = [(0, 0, 1), (1, rows - 1, 1)]
    for part, places in ((arrived, inner_places), (edge_arrived, edge_places)):
        decoded = pl.pallas_call(
            functools.partial(finish_kernel, places),
            in_specs=[VMEM] * 3 + [ANY],
            out_specs=ANY,
            out_shape=jax.ShapeDtypeStruct(features.shape, BF16),
            scratch_shapes=[room(part.shape[0]), pltpu.SemaphoreType.DMA((len(places),))],
            input_output_aliases={3: 0},
            compiler_params=params(3),
            cost_estimate=cost(part.shape[0] * cols, 1, channels, 4),
            name="finish",
        )(part, base, time_kernel, decoded)
    return decoded


def solution(mesh):
    return jax.shard_map(
        body,
        mesh=mesh,
        in_specs=(P(("grp", "frame"), "band", None, None), P(), P(), P(), P(), P(), P()),
        out_specs=P(("grp", "frame"), "band", None, None),
        check_vma=False,
    )
```

time: 62 us -> 36.3 us (0.59)
  waiting for transfers between devices: 28.6 us -> 5.53 us
  Pallas kernels: 0 us -> 16.7 us
  other arithmetic: 10.1 us -> 0.04 us
  matrix products: 9.43 us -> 0 us
  starting transfers between devices: 7.94 us -> 13.5 us
  local copies, waits for them, and re-layouts: 5.29 us -> 0.03 us
    ppermute x3 -> x6, waiting for transfers between devices: 28.6 us -> 5.53 us  [the longest x1 2.38 us: body(): edge = lax.ppermute(edge_out, 'frame', onward)]
    pallas_call x0 -> x5, Pallas kernels: none -> 16.7 us  [the longest x1 8.58 us: body(): pl.pallas_call(main_kernel, in_specs=[SMEM] + [VMEM] * (len(inputs) - 1),...]
    dot_general x13 -> x0, matrix products: 9.43 us -> none  [the longest x9 6.97 us: body(): jnp.dot(window, space_kernel[tap_row, tap_col], preferred_element_type=jn...]
    convert_element_type x4 -> x0, other arithmetic: 5.81 us -> none  [the longest x2 2.78 us: rms_silu(): return jax.nn.silu(scaled).astype(jnp.bfloat16)]
    ppermute x3 -> x6, starting transfers between devices: 7.94 us -> 13.5 us  [the longest x1 3.48 us: body(): above = lax.ppermute(up_rows, 'band', up)]
    slice x2 -> x1, local copies, waits for them, and re-layouts: 5.23 us -> 0.01 us  [body(): down_rows = jnp.concatenate([tops, edge[:1]], axis=0)]
    reduce_sum x2 -> x0, other arithmetic: 2.97 us -> none  [rms_silu(): jnp.mean(widened * widened, axis=-1, keepdims=True) + 1e-06]
    concatenate x2 -> x1, other arithmetic: 1.34 us -> 0.04 us  [body(): up_rows = jnp.concatenate([bottoms, edge[1:]], axis=0)]
  transfers between devices with their start and end apart: 3 -> 6, of which waited for: 3 -> 3; matrix products, arithmetic and copies ran while one was open for 2% -> 0% of each run, Pallas kernels for 0% -> 40%
where the time goes in v2:
time: 36.3 us; the launch traced here: 36 us
  Pallas kernels  16.7 us (46%)
  starting transfers between devices  13.5 us (37%)
  waiting for transfers between devices  5.53 us (15%)
    pallas_call x1, Pallas kernels, body(): pl.pallas_call(main_kernel, in_specs=[SMEM] + [VMEM] * (len(inputs) - 1),...  8.58 us
    pallas_call x1, Pallas kernels, body(): pl.pallas_call(interior_kernel, in_specs=[HBM] * 3 + [VMEM] * 3, out_spec...  4.56 us
    ppermute x1, starting transfers between devices, body(): above = lax.ppermute(up_rows, 'band', up)  3.48 us
    ppermute x1, waiting for transfers between devices, body(): edge = lax.ppermute(edge_out, 'frame', onward)  2.38 us
    ppermute x1, starting transfers between devices, body(): below = lax.ppermute(down_rows, 'band', down)  2.36 us
    ppermute x1, waiting for transfers between devices, body(): arrived = lax.ppermute(normed_a, 'frame', onward)  2.23 us
    pallas_call x2, Pallas kernels, body(): pl.pallas_call(functools.partial(finish_kernel, places), in_specs=[VMEM]...  2.07 us
    ppermute x1, starting transfers between devices, body(): inner = lax.ppermute(inner_out, 'frame', onward)  1.92 us
  transfers between devices with their start and end apart: 6, of which 3 were waited for; matrix products, arithmetic and copies ran while one was open for 0% of the time, Pallas kernels for 40%

profile of v2, /device:TPU:18, one launch (start us, length us, event | category | flops | bytes accessed | tf_op | source)
XLA Modules:
  0.0 36.0 jit_solution(10039263941509339320)
XLA Ops:
  0.0 0.0 copy-start.2
  0.0 0.0 copy-start.3
  0.0 0.0 copy-start
  0.0 1.5 %split.1 = (bf16[2,128,256]{2,1,0:T(8,128)(2,1)S(1)}, bf16[14,128,256]{2,1,0:T(8,128)(2,1)S(1)}, bf16[2,128,256]{2,1,0:T(8,128)(2,1)S(1)}, bf16[2,128,256]{2,1,0:T(8,128)(2,1)S(1)}) custom-call(bf16[2,16,128,256]{3,2,1,0:T(8,128)(2,1)} %feats.2), custom_call_target="tpu_custom_call" | custom-call | tf_op jit(solution)/shard_map/split/pallas_call | solution.py:261
  1.5 1.9 %collective-permute-start = (bf16[2,128,256]{2,1,0:T(8,128)(2,1)S(1)}, bf16[2,128,256]{2,1,0:T(8,128)(2,1)S(1)}, u32[]{:S(2)}, u32[]{:S(2)}) collective-permute-start(bf16[2,128,256]{2,1,0:T(8,128)(2,1)S(1)} %get-tuple-element.21.own_edge), channel_id=1, source_target_pairs={{0,4},{4,8},{8,12},{1,5},{5,9},{9,13},{2,6},{6,10},{10,14},{3,7},{... | collective-permute-start | bytes 393224 | tf_op jit(solution)/shard_map/ppermute | solution.py:270
  3.4 1.9 %collective-permute-start.1 = (bf16[14,128,256]{2,1,0:T(8,128)(2,1)S(1)}, bf16[14,128,256]{2,1,0:T(8,128)(2,1)S(1)}, u32[]{:S(2)}, u32[]{:S(2)}) collective-permute-start(bf16[14,128,256]{2,1,0:T(8,128)(2,1)S(1)} %get-tuple-element.25.own_inner), channel_id=1, source_target_pairs={{0,4},{4,8},{8,12},{1,5},{5,9},{9,13},{2,6},{6,10},{10,14},{3,7},{... | collective-permute-start | bytes 2752520 | tf_op jit(solution)/shard_map/ppermute | solution.py:271
  5.3 0.0 copy-done.2
  5.4 0.0 copy-done.3
  5.4 2.4 %collective-permute-done.edge = bf16[2,128,256]{2,1,0:T(8,128)(2,1)S(1)} collective-permute-done((bf16[2,128,256]{2,1,0:T(8,128)(2,1)S(1)}, bf16[2,128,256]{2,1,0:T(8,128)(2,1)S(1)}, u32[]{:S(2)}, u32[]{:S(2)}) %collective-permute-start) | collective-permute-done | bytes 131104 | tf_op jit(solution)/shard_map/ppermute | solution.py:270
  7.8 3.5 %collective-permute-start.2 = (bf16[3,128,256]{2,1,0:T(8,128)(2,1)S(1)}, bf16[3,128,256]{2,1,0:T(8,128)(2,1)S(1)}, u32[]{:S(2)}, u32[]{:S(2)}) collective-permute-start(bf16[3,128,256]{2,1,0:T(8,128)(2,1)S(1)} %get-tuple-element.26), channel_id=1, source_target_pairs={{0,1},{1,2},{2,3},{4,5},{5,6},{6,7},{8,9},{9,10},{10,11},{12,13},{... | collective-permute-start | bytes 589832 | tf_op jit(solution)/shard_map/ppermute | solution.py:276
  11.3 2.4 %collective-permute-start.3 = (bf16[3,128,256]{2,1,0:T(8,128)(2,1)S(1)}, bf16[3,128,256]{2,1,0:T(8,128)(2,1)S(1)}, u32[]{:S(2)}, u32[]{:S(2)}) collective-permute-start(bf16[3,128,256]{2,1,0:T(8,128)(2,1)S(1)} %get-tuple-element.27), channel_id=1, source_target_pairs={{1,0},{2,1},{3,2},{5,4},{6,5},{7,6},{9,8},{10,9},{11,10},{13,12},{... | collective-permute-start | bytes 589832 | tf_op jit(solution)/shard_map/ppermute | solution.py:277
  13.7 0.0 copy-done
  13.7 0.0 copy-start.1
  13.7 4.6 %interior.1 = (bf16[14,128,256]{2,1,0:T(8,128)(2,1)S(1)}, bf16[14,128,256]{2,1,0:T(8,128)(2,1)S(1)}, bf16[16,128,256]{2,1,0:T(8,128)(2,1)S(1)}, bf16[3,3,256,256...) custom-call(bf16[2,16,128,256]{3,2,1,0:T(8,128)(2,1)} %feats.2, bf16[3,3,256,256]{3,2,1,0:T(8,128)(2,1)} %kernel.1, ...), custom_call_target="tpu_custom_call" | custom-call | flops 9663676416 | bytes 3145728 | tf_op jit(solution)/shard_map/interior/pallas_call | solution.py:278
  18.3 1.9 %collective-permute-start.5 = (bf16[14,128,256]{2,1,0:T(8,128)(2,1)S(1)}, bf16[14,128,256]{2,1,0:T(8,128)(2,1)S(1)}, u32[]{:S(2)}, u32[]{:S(2)}) collective-permute-start(bf16[14,128,256]{2,1,0:T(8,128)(2,1)S(1)} %get-tuple-element.31.normed_a), channel_id=1, source_target_pairs={{0,4},{4,8},{8,12},{1,5},{5,9},{9,13},{2,6},{6,10},{10,14},{3,7},{... | collective-permute-start | bytes 2752520 | tf_op jit(solution)/shard_map/ppermute | solution.py:291
  20.2 0.0 collective-permute-done.2.above
  20.2 0.0 collective-permute-done.3.below
  20.2 0.0 collective-permute-done.1.inner
  20.2 0.0 copy-done.1
  20.2 8.6 %main.1 = (bf16[2,16,128,256]{3,2,1,0:T(8,128)(2,1)}, f32[16,128,256]{2,1,0:T(8,128)S(1)}, bf16[2,128,256]{2,1,0:T(8,128)(2,1)S(1)}) custom-call(f32[1]{0:T(128)} %bitcast.valid, bf16[16,128,256]{2,1,0:T(8,128)(2,1)S(1)} %get-tuple-element.24.raw_a, bf16[2,128,256]{2,1,0:T(8,128)(2,1)S(1)} %get-tuple-element.21.own_edge, ...), custom_call_target="tpu_custom_call" | custom-call | flops 49392123904 | bytes 10485760 | tf_op jit(solution)/shard_map/main/pallas_call | solution.py:295
  28.8 1.9 %collective-permute-start.4 = (bf16[2,128,256]{2,1,0:T(8,128)(2,1)S(1)}, bf16[2,128,256]{2,1,0:T(8,128)(2,1)S(1)}, u32[]{:S(2)}, u32[]{:S(2)}) collective-permute-start(bf16[2,128,256]{2,1,0:T(8,128)(2,1)S(1)} %get-tuple-element.32), channel_id=1, source_target_pairs={{0,4},{4,8},{8,12},{1,5},{5,9},{9,13},{2,6},{6,10},{10,14},{3,7},{... | collective-permute-start | bytes 393224 | tf_op jit(solution)/shard_map/ppermute | solution.py:309
  30.8 2.2 %collective-permute-done.5.arrived = bf16[14,128,256]{2,1,0:T(8,128)(2,1)S(1)} collective-permute-done((bf16[14,128,256]{2,1,0:T(8,128)(2,1)S(1)}, bf16[14,128,256]{2,1,0:T(8,128)(2,1)S(1)}, u32[]{:S(2)}, u32[]{:S(2)}) %collective-permute-start.5) | collective-permute-done | bytes 917536 | tf_op jit(solution)/shard_map/ppermute | solution.py:291
  33.0 1.2 %finish.2._ = bf16[2,16,128,256]{3,2,1,0:T(8,128)(2,1)} custom-call(bf16[14,128,256]{2,1,0:T(8,128)(2,1)S(1)} %collective-permute-done.5.arrived, f32[16,128,256]{2,1,0:T(8,128)S(1)} %get-tuple-element.33.base, bf16[3,256,256]{2,1,0:T(8,128)(2,1)S(1)} %get-tuple-element.29.time_kernel, ...), custom_call_target="tpu_custom_call", output_to_operand_aliasing={{}: (3, {})} | custom-call | flops 234881024 | bytes 3670016 | tf_op jit(solution)/shard_map/finish/pallas_call | solution.py:314
  34.2 0.9 %collective-permute-done.4.arrived = bf16[2,128,256]{2,1,0:T(8,128)(2,1)S(1)} collective-permute-done((bf16[2,128,256]{2,1,0:T(8,128)(2,1)S(1)}, bf16[2,128,256]{2,1,0:T(8,128)(2,1)S(1)}, u32[]{:S(2)}, u32[]{:S(2)}) %collective-permute-start.4) | collective-permute-done | bytes 131104 | tf_op jit(solution)/shard_map/ppermute | solution.py:309
  35.1 0.9 %finish.3 = bf16[2,16,128,256]{3,2,1,0:T(8,128)(2,1)} custom-call(bf16[2,128,256]{2,1,0:T(8,128)(2,1)S(1)} %collective-permute-done.4.arrived, f32[16,128,256]{2,1,0:T(8,128)S(1)} %get-tuple-element.33.base, bf16[3,256,256]{2,1,0:T(8,128)(2,1)S(1)} %get-tuple-element.29.time_kernel, bf16[2,16,128,256]{3,2,1,0:T(8,128)(2,1)} %finish.2._), custom_call_target="tpu_custom_call", output_to_operand_aliasing={{}: (3, {})} | custom-call | flops 33554432 | bytes 524288 | tf_op jit(solution)/shard_map/finish/pallas_call | solution.py:314
  (4 shorter events, 0.1 us)
Async XLA Ops:
  0.0 5.3 %copy-start.2 = (f32[256]{0:T(256)S(1)}, f32[256]{0:T(256)}, u32[]{:S(2)}) copy-start(f32[256]{0:T(256)} %param.9) | copy-start | bytes 3076
  0.0 5.4 %copy-start.3 = (f32[256]{0:T(256)S(1)}, f32[256]{0:T(256)}, u32[]{:S(2)}) copy-start(f32[256]{0:T(256)} %param.12) | copy-start | bytes 3076
  0.0 13.7 %copy-start = (f32[256]{0:T(256)S(1)}, f32[256]{0:T(256)}, u32[]{:S(2)}) copy-start(f32[256]{0:T(256)} %param.10) | copy-start | bytes 3076
  1.5 6.3 %collective-permute-start = (bf16[2,128,256]{2,1,0:T(8,128)(2,1)S(1)}, bf16[2,128,256]{2,1,0:T(8,128)(2,1)S(1)}, u32[]{:S(2)}, u32[]{:S(2)}) collective-permute-start(bf16[2,128,256]{2,1,0:T(8,128)(2,1)S(1)} %get-tuple-element.21.own_edge), channel_id=1, source_target_pairs={{0,4},{4,8},{8,12},{1,5},{5,9},{9,13},{2,6},{6,10},{10,14},{3,7},{... | collective-permute-start | bytes 393224 | tf_op jit(solution)/shard_map/ppermute | solution.py:270
  3.4 16.8 %collective-permute-start.1 = (bf16[14,128,256]{2,1,0:T(8,128)(2,1)S(1)}, bf16[14,128,256]{2,1,0:T(8,128)(2,1)S(1)}, u32[]{:S(2)}, u32[]{:S(2)}) collective-permute-start(bf16[14,128,256]{2,1,0:T(8,128)(2,1)S(1)} %get-tuple-element.25.own_inner), channel_id=1, source_target_pairs={{0,4},{4,8},{8,12},{1,5},{5,9},{9,13},{2,6},{6,10},{10,14},{3,7},{... | collective-permute-start | bytes 2752520 | tf_op jit(solution)/shard_map/ppermute | solution.py:271
  7.8 12.4 %collective-permute-start.2 = (bf16[3,128,256]{2,1,0:T(8,128)(2,1)S(1)}, bf16[3,128,256]{2,1,0:T(8,128)(2,1)S(1)}, u32[]{:S(2)}, u32[]{:S(2)}) collective-permute-start(bf16[3,128,256]{2,1,0:T(8,128)(2,1)S(1)} %get-tuple-element.26), channel_id=1, source_target_pairs={{0,1},{1,2},{2,3},{4,5},{5,6},{6,7},{8,9},{9,10},{10,11},{12,13},{... | collective-permute-start | bytes 589832 | tf_op jit(solution)/shard_map/ppermute | solution.py:276
  11.3 8.9 %collective-permute-start.3 = (bf16[3,128,256]{2,1,0:T(8,128)(2,1)S(1)}, bf16[3,128,256]{2,1,0:T(8,128)(2,1)S(1)}, u32[]{:S(2)}, u32[]{:S(2)}) collective-permute-start(bf16[3,128,256]{2,1,0:T(8,128)(2,1)S(1)} %get-tuple-element.27), channel_id=1, source_target_pairs={{1,0},{2,1},{3,2},{5,4},{6,5},{7,6},{9,8},{10,9},{11,10},{13,12},{... | collective-permute-start | bytes 589832 | tf_op jit(solution)/shard_map/ppermute | solution.py:277
  13.7 6.5 %copy-start.1 = (f32[256]{0:T(256)S(1)}, f32[256]{0:T(256)}, u32[]{:S(2)}) copy-start(f32[256]{0:T(256)} %param.13) | copy-start | bytes 3076
  18.3 14.7 %collective-permute-start.5 = (bf16[14,128,256]{2,1,0:T(8,128)(2,1)S(1)}, bf16[14,128,256]{2,1,0:T(8,128)(2,1)S(1)}, u32[]{:S(2)}, u32[]{:S(2)}) collective-permute-start(bf16[14,128,256]{2,1,0:T(8,128)(2,1)S(1)} %get-tuple-element.31.normed_a), channel_id=1, source_target_pairs={{0,4},{4,8},{8,12},{1,5},{5,9},{9,13},{2,6},{6,10},{10,14},{3,7},{... | collective-permute-start | bytes 2752520 | tf_op jit(solution)/shard_map/ppermute | solution.py:291
  28.8 6.3 %collective-permute-start.4 = (bf16[2,128,256]{2,1,0:T(8,128)(2,1)S(1)}, bf16[2,128,256]{2,1,0:T(8,128)(2,1)S(1)}, u32[]{:S(2)}, u32[]{:S(2)}) collective-permute-start(bf16[2,128,256]{2,1,0:T(8,128)(2,1)S(1)} %get-tuple-element.32), channel_id=1, source_target_pairs={{0,4},{4,8},{8,12},{1,5},{5,9},{9,13},{2,6},{6,10},{10,14},{3,7},{... | collective-permute-start | bytes 393224 | tf_op jit(solution)/shard_map/ppermute | solution.py:309

commit v3 on v2

v3 whole, which is shorter than its diff:
```python
import functools

import jax
import jax.numpy as jnp
from jax import lax
from jax.experimental import pallas as pl
from jax.experimental.pallas import tpu as pltpu
from jax.sharding import PartitionSpec as P

F32 = jnp.float32
BF16 = jnp.bfloat16
VMEM = pl.BlockSpec(memory_space=pltpu.VMEM)
ANY = pl.BlockSpec(memory_space=pl.ANY)
HBM = pl.BlockSpec(memory_space=pltpu.HBM)
STEP = 2


def blocks(first, last):
    return [(r, min(STEP, last - r)) for r in range(first, last, STEP)]


def rms_silu(values, gain):
    mean_square = jnp.mean(values * values, axis=-1, keepdims=True)
    u = values * lax.rsqrt(mean_square + 1e-06) * (0.5 * gain)
    return u + u * jnp.tanh(u)


def norm_into(shifted, place, row, gain):
    row, scale = row if isinstance(row, tuple) else (row, None)
    normed = rms_silu(row.astype(F32), gain)
    normed = normed if scale is None else normed * scale
    cols = normed.shape[0]
    column = lax.broadcasted_iota(jnp.int32, normed.shape, 0)
    before = jnp.where(column == 0, 0.0, pltpu.roll(normed, 1, 0))
    after = jnp.where(column == cols - 1, 0.0, pltpu.roll(normed, cols - 1, 0))
    shifted[0, place] = before.astype(BF16)
    shifted[1, place] = normed.astype(BF16)
    shifted[2, place] = after.astype(BF16)


def conv_rows(shifted, kernel, place, count):
    cols, channels = shifted.shape[2:]
    total = None
    for i in range(3):
        for j in range(3):
            window = shifted[j, place + i : place + i + count].reshape(count * cols, channels)
            product = jnp.dot(window, kernel[i, j], preferred_element_type=F32)
            total = product if total is None else total + product
    return total


def spatial_jobs(get_row, row_blocks, offset, shifted, sums, slot0, kernel, weights, emit, after=None):
    space_gain, space_bias, time_gain = weights
    ready = set()
    jobs = []

    def norm_stage(first, count):
        for r in range(first - 1, first + count + 1):
            if r not in ready:
                ready.add(r)
                norm_into(shifted, r + offset, get_row(r), space_gain[...])

    def conv_stage(slot, first, count):
        total = conv_rows(shifted, kernel, first - 1 + offset, count)
        sums[slot, : total.shape[0]] = total

    def emit_stage(slot, first, count):
        own = jnp.concatenate([get_row(r) for r in range(first, first + count)], axis=0)
        hidden = own.astype(F32) + sums[slot, : own.shape[0]] + space_bias[...]
        emit(first, count, hidden, rms_silu(hidden, time_gain[...]))

    for n, (first, count) in enumerate(row_blocks):
        slot = (slot0 + n) % sums.shape[0]
        jobs.append([
            functools.partial(norm_stage, first, count),
            functools.partial(conv_stage, slot, first, count),
            functools.partial(emit_stage, slot, first, count),
            functools.partial(after, first, count) if after else None,
        ])
    return jobs


def run(jobs):
    for n in range(len(jobs) + 3):
        for stage in range(4):
            if 0 <= n - stage < len(jobs) and jobs[n - stage][stage] is not None:
                jobs[n - stage][stage]()


def split_kernel(first, feats, out, sems):
    rows = feats.shape[1]
    places = [(first, rows - first, 0)] if first else [(0, 1, 0), (rows - 1, rows, 1)]
    copies = [
        pltpu.make_async_copy(feats.at[1, pl.ds(a, b - a)], out.at[pl.ds(at, b - a)], sems.at[n])
        for n, (a, b, at) in enumerate(places)
    ]
    for copy in copies:
        copy.start()
    for copy in copies:
        copy.wait()


def goes_up(index, count):
    return index % 2 == 0 or count % 2 == 1


def halo_ring(frames, bands):
    paired = frames % 2 == 0
    pairs = []
    for f in range(frames):
        for b in range(bands):
            to = (f, b + 1) if goes_up(f, frames) else (f, b - 1)
            if not 0 <= to[1] < bands:
                if not paired:
                    continue
                to = (f ^ 1, b)
            pairs.append((f * bands + b, to[0] * bands + to[1]))
    return pairs


def up_first(count):
    index = lax.axis_index("frame")
    return lax.rem(index, 2) == 0 if count % 2 == 0 else index >= 0


def halo_kernel(count, raw_a, edges_b, edges, send_0, send_1):
    rows = raw_a.shape[0]

    def fill(up_rows, down_rows):
        for n, (first, last) in enumerate((
            (raw_a.at[0], raw_a.at[rows - 1]), (edges_b.at[0], edges_b.at[1]), (edges.at[0], edges.at[1])
        )):
            up_rows[n] = last[...]
            down_rows[n] = first[...]

    up = up_first(count)
    pl.when(up)(lambda: fill(send_0, send_1))
    pl.when(jnp.logical_not(up))(lambda: fill(send_1, send_0))


def halo_row(counts, got_0, got_1, n, is_above):
    frames, bands = counts
    band = lax.axis_index("band")
    take = up_first(frames) if is_above else jnp.logical_not(up_first(frames))
    row = jnp.where(take, got_0[n].astype(F32), got_1[n].astype(F32))
    there = band > 0 if is_above else band < bands - 1
    return row, jnp.where(there, 1.0, 0.0)


def framed(upper, edges, inners, lower):
    rows = inners.shape[0] + 2

    def get_row(r):
        if r < 0 or r >= rows:
            return upper() if r < 0 else lower()
        return edges[0] if r == 0 else edges[1] if r == rows - 1 else inners[r - 1]

    return get_row


def inner_emit(hidden_ref, normed_ref):
    def emit(first, count, hidden, normed):
        at = pl.ds(first - 1, count)
        shape = (count,) + hidden_ref.shape[1:]
        hidden_ref[at] = hidden.astype(hidden_ref.dtype).reshape(shape)
        normed_ref[at] = normed.astype(BF16).reshape(shape)
    return emit


def edge_emit(hidden_ref, normed_ref):
    def emit(first, count, hidden, normed):
        which = 0 if first == 0 else 1
        hidden_ref[which] = hidden
        normed_ref[which] = normed.astype(BF16)
    return emit


def inner_a_kernel(feats, kernel, time_kernel, space_gain, space_bias, time_gain,
                   hidden_ref, normed_ref, raw, kernel_out, time_out, shifted, sums, sems):
    rows = raw.shape[0]
    half = rows // 2
    pairs = [
        (feats.at[0, pl.ds(0, half)], raw.at[pl.ds(0, half)]),
        (kernel, kernel_out),
        (feats.at[0, pl.ds(half, rows - half)], raw.at[pl.ds(half, rows - half)]),
        (time_kernel, time_out),
    ]
    copies = [pltpu.make_async_copy(a, b, sems.at[n]) for n, (a, b) in enumerate(pairs)]
    for copy in copies:
        copy.start()
    jobs = spatial_jobs(lambda r: raw[r], blocks(1, rows - 1), 0, shifted, sums, 0, kernel_out,
                        (space_gain, space_bias, time_gain), inner_emit(hidden_ref, normed_ref))
    copies[0].wait()
    jobs[0][0]()
    jobs[0][0] = None
    for copy in copies[1:]:
        copy.wait()
    run(jobs)


def inner_b_kernel(edges, inners, kernel, space_gain, space_bias, time_gain,
                   hidden_ref, normed_ref, shifted, sums):
    rows = inners.shape[0] + 2
    run(spatial_jobs(framed(None, edges, inners, None), blocks(1, rows - 1), 0, shifted, sums, 0,
                     kernel, (space_gain, space_bias, time_gain), inner_emit(hidden_ref, normed_ref)))


def edges_kernel(counts, raw_a, edges_b, inners_b, got_0, got_1, kernel, space_gain, space_bias, time_gain,
                 hidden_a, normed_a, hidden_b, normed_b, shifted, sums):
    rows = raw_a.shape[0]
    weights = (space_gain, space_bias, time_gain)

    halo = functools.partial(halo_row, counts, got_0, got_1)

    def row_a(r):
        return halo(0, r < 0) if r < 0 or r >= rows else raw_a[r]

    row_b = framed(lambda: halo(1, True), edges_b, inners_b, lambda: halo(1, False))
    jobs = []
    for n, (get_row, emit) in enumerate((
        (row_a, edge_emit(hidden_a, normed_a)), (row_b, edge_emit(hidden_b, normed_b))
    )):
        for m, (r, offset) in enumerate(((0, 1), (rows - 1, 2 - rows))):
            jobs += spatial_jobs(get_row, [(r, 1)], offset, shifted.at[2 * n + m], sums, 2 * n + m,
                                 kernel, weights, emit)
    run(jobs)


def main_kernel(counts, edges, inners, got_0, got_1, kernel, space_gain, space_bias, time_gain,
                time_kernel, time_bias, hidden_ae, hidden_ai, normed_ae, normed_ai,
                hidden_be, hidden_bi, normed_be, normed_bi,
                out_ref, base, shifted, sums, normed_p, decoded, sems):
    rows, cols, channels = base.shape
    keep = jnp.where(lax.axis_index("frame") > 0, 1.0, 0.0)

    def emit(first, count, hidden, normed):
        normed_p[first : first + count] = (normed * keep).astype(BF16).reshape(count, cols, channels)

    def rows_of(first, count, *parts):
        get_row = framed(None, *parts, None)
        return jnp.concatenate([get_row(r) for r in range(first, first + count)], axis=0)

    def out_rows(first, count):
        prior = normed_p[first : first + count].reshape(count * cols, channels)
        total = rows_of(first, count, hidden_be, hidden_bi) + time_bias[...]
        total += (
            jnp.dot(rows_of(first, count, normed_be, normed_bi), time_kernel[0], preferred_element_type=F32)
            + jnp.dot(rows_of(first, count, normed_ae, normed_ai), time_kernel[1], preferred_element_type=F32)
            + jnp.dot(prior, time_kernel[2], preferred_element_type=F32)
        )
        decoded[first : first + count] = total.astype(BF16).reshape(count, cols, channels)

    def base_rows(first, count):
        prior = normed_p[first : first + count].reshape(count * cols, channels)
        total = rows_of(first, count, hidden_ae, hidden_ai) + time_bias[...]
        total += (
            jnp.dot(rows_of(first, count, normed_ae, normed_ai), time_kernel[0], preferred_element_type=F32)
            + jnp.dot(prior, time_kernel[1], preferred_element_type=F32)
        )
        base[first : first + count] = total.reshape(count, cols, channels)

    halo = functools.partial(halo_row, counts, got_0, got_1, 2)
    get_row = framed(lambda: halo(True), edges, inners, lambda: halo(False))
    run(spatial_jobs(get_row, blocks(0, rows), 1, shifted, sums, 0, kernel,
                     (space_gain, space_bias, time_gain), emit))
    copies = []
    for n, (first, count) in enumerate(blocks(0, rows)):
        out_rows(first, count)
        copies.append(pltpu.make_async_copy(
            decoded.at[pl.ds(first, count)], out_ref.at[1, pl.ds(first, count)], sems.at[n]))
        copies[-1].start()
    for first, count in blocks(0, rows):
        base_rows(first, count)
    for copy in copies:
        copy.wait()


def finish_kernel(places, arrived, base, time_kernel, _, out_ref, decoded, sems):
    cols, channels = base.shape[1:]
    keep = jnp.where(lax.axis_index("frame") > 0, 1.0, 0.0)
    kernel = (time_kernel[2].astype(F32) * keep).astype(BF16)
    copies = []
    for n, (at, row, count) in enumerate(places):
        total = base[row : row + count].reshape(count * cols, channels)
        total += jnp.dot(arrived[at : at + count].reshape(count * cols, channels), kernel,
                         preferred_element_type=F32)
        decoded[at : at + count] = total.astype(BF16).reshape(count, cols, channels)
        copies.append(pltpu.make_async_copy(
            decoded.at[pl.ds(at, count)], out_ref.at[0, pl.ds(row, count)], sems.at[n]))
        copies[-1].start()
    for copy in copies:
        copy.wait()


def cost(pixels, taps, channels, arrays):
    return pl.CostEstimate(
        flops=2 * pixels * taps * channels * channels,
        bytes_accessed=2 * arrays * pixels * channels,
        transcendentals=2 * pixels * channels,
    )


def body(features, space_kernel, space_gain, space_bias, time_kernel, time_gain, time_bias):
    frames, rows, cols, channels = features.shape
    row = (cols, channels)
    count_f, count_b = lax.axis_size("frame"), lax.axis_size("band")
    counts = (count_f, count_b)
    onward = [(i, (i + 1) % count_f) for i in range(count_f)]
    ring = halo_ring(count_f, count_b)

    def shape(*lead, dtype=BF16):
        return jax.ShapeDtypeStruct(tuple(lead) + row, dtype)

    def room(*lead, dtype=BF16):
        return pltpu.VMEM(tuple(lead) + row, dtype)

    space_gain = space_gain.reshape(1, channels)
    time_gain = time_gain.reshape(1, channels)
    space_bias = space_bias.reshape(1, channels)
    time_bias = time_bias.reshape(1, channels)
    sums = pltpu.VMEM((4, STEP * cols, channels), F32)

    weights = (space_gain, space_bias, time_gain)
    count = len(blocks(0, rows))

    def call(kernel, inputs, outs, scratch, mebibytes, name, **more):
        inputs = [x if isinstance(x, tuple) else (VMEM, x) for x in inputs]
        specs, arrays = zip(*inputs)
        out_specs, out_shape = zip(*((VMEM, o) if not isinstance(o, tuple) else o for o in outs))
        arrays = [x if x.ndim < 3 or s is ANY else pltpu.with_memory_space_constraint(x, s.memory_space)
                  for s, x in zip(specs, arrays)]
        out_shape = [pltpu.VMEM(o.shape, o.dtype) if s is VMEM else o for s, o in zip(out_specs, out_shape)]
        return pl.pallas_call(
            kernel, in_specs=list(specs), out_specs=list(out_specs), out_shape=out_shape,
            scratch_shapes=scratch, name=name,
            compiler_params=pltpu.CompilerParams(vmem_limit_bytes=mebibytes * 1024 * 1024), **more,
        )(*arrays)

    def split(first, feats, n):
        return call(
            functools.partial(split_kernel, first), [(HBM, feats)], [shape(n)],
            [pltpu.SemaphoreType.DMA((2,))], 1, "split",
        )[0]

    edge_out = split(0, features, 2)
    edge = lax.ppermute(edge_out, "frame", onward)
    inner_out = split(1, features, rows - 2)
    inner = lax.ppermute(inner_out, "frame", onward)

    hidden_ai, normed_ai, raw_a, space_kernel, time_kernel = call(
        inner_a_kernel,
        [(HBM, features), (HBM, space_kernel), (HBM, time_kernel), *weights],
        [shape(rows - 2, dtype=F32), shape(rows - 2), shape(rows),
         jax.ShapeDtypeStruct(space_kernel.shape, BF16), jax.ShapeDtypeStruct(time_kernel.shape, BF16)],
        [room(3, rows), sums, pltpu.SemaphoreType.DMA((4,))],
        6, "inner_a", cost_estimate=cost(rows * cols, 9, channels, 3),
    )
    arrived = lax.ppermute(normed_ai, "frame", onward)

    send_0, send_1 = call(
        functools.partial(halo_kernel, count_f), [raw_a, edge_out, edge], [shape(3), shape(3)], [], 1, "halo",
    )
    got_0 = lax.ppermute(send_0, ("frame", "band"), ring)
    got_1 = lax.ppermute(send_1, ("frame", "band"), [(t, s) for s, t in ring])
    send_0, send_1, edge_b = lax.optimization_barrier((send_0, send_1, edge_out))
    hidden_bi, normed_bi = call(
        inner_b_kernel, [edge_b, inner_out, space_kernel, *weights],
        [shape(rows - 2, dtype=F32), shape(rows - 2)], [room(3, rows), sums],
        6, "inner_b", cost_estimate=cost(rows * cols, 9 * 8, channels, 3),
    )
    hidden_ae, normed_ae, hidden_be, normed_be = call(
        functools.partial(edges_kernel, counts), [raw_a, edge_out, inner_out, got_0, got_1, space_kernel, *weights],
        [shape(2, dtype=F32), shape(2)] * 2, [room(4, 3, 3), sums],
        4, "edges", cost_estimate=cost(4 * cols, 9, channels, 3),
    )
    edge_arrived = lax.ppermute(normed_ae, "frame", onward)

    decoded, base = call(
        functools.partial(main_kernel, counts),
        [edge, inner, got_0, got_1, space_kernel, *weights, time_kernel, time_bias,
         hidden_ae, hidden_ai, normed_ae, normed_ai, hidden_be, hidden_bi, normed_be, normed_bi],
        [(ANY, jax.ShapeDtypeStruct(features.shape, BF16)), shape(rows, dtype=F32)],
        [room(3, rows + 2), sums, room(rows), room(rows), pltpu.SemaphoreType.DMA((count,))],
        9, "main", cost_estimate=cost(rows * cols, 14, channels, 10),
    )
    inner_places = [(r - 1, r, n) for r, n in blocks(1, rows - 1)]
    edge_places = [(0, 0, 1), (1, rows - 1, 1)]
    for part, places in ((arrived, inner_places), (edge_arrived, edge_places)):
        decoded = call(
            functools.partial(finish_kernel, places), [part, base, time_kernel, (ANY, decoded)],
            [(ANY, jax.ShapeDtypeStruct(features.shape, BF16))],
            [room(part.shape[0]), pltpu.SemaphoreType.DMA((len(places),))],
            3, "finish", input_output_aliases={3: 0},
            cost_estimate=cost(part.shape[0] * cols, 1, channels, 4),
        )[0]
    return decoded


def solution(mesh):
    return jax.shard_map(
        body,
        mesh=mesh,
        in_specs=(P(("grp", "frame"), "band", None, None), P(), P(), P(), P(), P(), P()),
        out_specs=P(("grp", "frame"), "band", None, None),
        check_vma=False,
    )
```

time: 36.3 us -> 28.4 us (0.78)
  the two profiles are of different devices: /device:TPU:18 before, /device:TPU:0 now
where the time goes in v3:
time: 28.4 us; the launch traced here: 28.1 us
  Pallas kernels  17.5 us (62%)
  waiting for transfers between devices  5.22 us (18%)
  starting transfers between devices  5.08 us (18%)
    pallas_call x9, Pallas kernels, call(): pl.pallas_call(kernel, in_specs=list(specs), out_specs=list(out_specs), o...  17.5 us
    ppermute x1, starting transfers between devices, body(): inner = lax.ppermute(inner_out, 'frame', onward)  2.65 us
    ppermute x1, waiting for transfers between devices, body(): arrived = lax.ppermute(normed_ai, 'frame', onward)  2.27 us
    ppermute x1, waiting for transfers between devices, body(): got_0 = lax.ppermute(send_0, ('frame', 'band'), ring)  2.05 us
    ppermute x1, starting transfers between devices, body(): got_0 = lax.ppermute(send_0, ('frame', 'band'), ring)  1.59 us
    ppermute x1, waiting for transfers between devices, body(): got_1 = lax.ppermute(send_1, ('frame', 'band'), [(t, s) for s, t in ring])  0.71 us
  transfers between devices with their start and end apart: 6, of which 4 were waited for; matrix products, arithmetic and copies ran while one was open for 0% of the time, Pallas kernels for 56%

profile of v3, /device:TPU:0, one launch (start us, length us, event | category | flops | bytes accessed | tf_op | source)
XLA Modules:
  0.0 28.1 jit_solution(9860081311140497119)
XLA Ops:
  0.0 0.0 copy-start
  0.0 0.0 copy-start.1
  0.0 0.0 copy-start.2
  0.0 0.9 %split.2.edges_b.edges = bf16[2,128,256]{2,1,0:T(8,128)(2,1)S(1)} custom-call(bf16[2,16,128,256]{3,2,1,0:T(8,128)(2,1)} %feats.5), custom_call_target="tpu_custom_call" | custom-call | tf_op jit(solution)/shard_map/split/pallas_call | solution.py:333
  0.9 0.5 %collective-permute-start = (bf16[2,128,256]{2,1,0:T(8,128)(2,1)S(1)}, bf16[2,128,256]{2,1,0:T(8,128)(2,1)S(1)}, u32[]{:S(2)}, u32[]{:S(2)}) collective-permute-start(bf16[2,128,256]{2,1,0:T(8,128)(2,1)S(1)} %split.2.edges_b.edges), channel_id=1, source_target_pairs={{0,4},{4,8},{8,12},{12,0},{1,5},{5,9},{9,13},{13,1},{2,6},{6,10},{... | collective-permute-start | bytes 393224 | tf_op jit(solution)/shard_map/ppermute | solution.py:346
  1.4 1.2 %split.3.inners_b.inners = bf16[14,128,256]{2,1,0:T(8,128)(2,1)S(1)} custom-call(bf16[2,16,128,256]{3,2,1,0:T(8,128)(2,1)} %feats.5), custom_call_target="tpu_custom_call" | custom-call | tf_op jit(solution)/shard_map/split/pallas_call | solution.py:333
  2.7 2.7 %collective-permute-start.4 = (bf16[14,128,256]{2,1,0:T(8,128)(2,1)S(1)}, bf16[14,128,256]{2,1,0:T(8,128)(2,1)S(1)}, u32[]{:S(2)}, u32[]{:S(2)}) collective-permute-start(bf16[14,128,256]{2,1,0:T(8,128)(2,1)S(1)} %split.3.inners_b.inners), channel_id=1, source_target_pairs={{0,4},{4,8},{8,12},{12,0},{1,5},{5,9},{9,13},{13,1},{2,6},{6,10},{... | collective-permute-start | bytes 2752520 | tf_op jit(solution)/shard_map/ppermute | solution.py:348
  5.3 0.0 copy-done
  5.3 0.0 copy-done.1
  5.3 0.0 copy-done.2
  5.3 4.4 %inner_a.1 = (f32[14,128,256]{2,1,0:T(8,128)S(1)}, bf16[14,128,256]{2,1,0:T(8,128)(2,1)S(1)}, bf16[16,128,256]{2,1,0:T(8,128)(2,1)S(1)}, bf16[3,3,256,256]{3,2,1,0:T(8,128)(2,1)S(1)}, bf16[3,256,256]{2,1,0:T(8,128)(2,1)S(1)}) custom-call(bf16[2,16,128,256]{3,2,1,0:T(8,128)(2,1)} %feats.5, bf16[3,3,256,256]{3,2,1,0:T(8,128)(2,1)} %kernel.1, ...), custom_call_target="tpu_custom_call" | custom-call | flops 2415919104 | bytes 3145728 | tf_op jit(solution)/shard_map/inner_a/pallas_call | solution.py:333
  9.8 0.1 collective-permute-start.5
  9.9 0.0 collective-permute-done.edges
  9.9 1.6 %collective-permute-start.1 = (bf16[3,128,256]{2,1,0:T(8,128)(2,1)S(1)}, bf16[3,128,256]{2,1,0:T(8,128)(2,1)S(1)}, u32[]{:S(2)}, u32[]{:S(2)}) collective-permute-start(bf16[3,128,256]{2,1,0:T(8,128)(2,1)S(1)} %get-tuple-element.22), channel_id=1, source_target_pairs={{0,1},{1,2},{2,3},{3,7},{4,0},{5,4},{6,5},{7,6},{8,9},{9,10},{10,1... | collective-permute-start | bytes 589832 | tf_op jit(solution)/shard_map/ppermute | solution.py:363
  11.5 0.0 collective-permute-start.2
  11.5 2.9 %inner_b.1 = (f32[14,128,256]{2,1,0:T(8,128)S(1)}, bf16[14,128,256]{2,1,0:T(8,128)(2,1)S(1)}) custom-call(bf16[2,128,256]{2,1,0:T(8,128)(2,1)S(1)} %split.2.edges_b.edges, bf16[14,128,256]{2,1,0:T(8,128)(2,1)S(1)} %split.3.inners_b.inners, bf16[3,3,256,256]{3,2,1,0:T(8,128)(2,1)S(1)} %get-tuple-element.24.kernel, f32[1,256]{1,0:T(1,128)S(1)} %bitcast.5, ...), custom_call_target="tpu_custom_call" | custom-call | flops 19327352832 | bytes 3145728 | tf_op jit(solution)/shard_map/inner_b/pallas_call | solution.py:333
  14.4 0.0 copy-start.3
  14.4 2.1 %collective-permute-done.1.got_0 = bf16[3,128,256]{2,1,0:T(8,128)(2,1)S(1)} collective-permute-done((bf16[3,128,256]{2,1,0:T(8,128)(2,1)S(1)}, bf16[3,128,256]{2,1,0:T(8,128)(2,1)S(1)}, u32[]{:S(2)}, u32[]{:S(2)}) %collective-permute-start.1) | collective-permute-done | bytes 196640 | tf_op jit(solution)/shard_map/ppermute | solution.py:363
  16.4 0.7 %collective-permute-done.2.got_1 = bf16[3,128,256]{2,1,0:T(8,128)(2,1)S(1)} collective-permute-done((bf16[3,128,256]{2,1,0:T(8,128)(2,1)S(1)}, bf16[3,128,256]{2,1,0:T(8,128)(2,1)S(1)}, u32[]{:S(2)}, u32[]{:S(2)}) %collective-permute-start.2) | collective-permute-done | bytes 196640 | tf_op jit(solution)/shard_map/ppermute | solution.py:364
  17.2 1.3 %edges.1 = (f32[2,128,256]{2,1,0:T(8,128)S(1)}, bf16[2,128,256]{2,1,0:T(8,128)(2,1)S(1)}, f32[2,128,256]{2,1,0:T(8,128)S(1)}, bf16[2,128,256]{2,1,0:T(8,128)(2,1)S(1)}) custom-call(bf16[16,128,256]{2,1,0:T(8,128)(2,1)S(1)} %get-tuple-element.21.raw_a, bf16[2,128,256]{2,1,0:T(8,128)(2,1)S(1)} %split.2.edges_b.edges, ...), custom_call_target="tpu_custom_call" | custom-call | flops 603979776 | bytes 786432 | tf_op jit(solution)/shard_map/edges/pallas_call | solution.py:333
  18.5 0.2 collective-permute-start.3
  18.7 0.0 collective-permute-done.4.inners
  18.8 0.0 copy-done.3
  18.8 4.6 %main.1 = (bf16[2,16,128,256]{3,2,1,0:T(8,128)(2,1)}, f32[16,128,256]{2,1,0:T(8,128)S(1)}) custom-call(bf16[2,128,256]{2,1,0:T(8,128)(2,1)S(1)} %collective-permute-done.edges, bf16[14,128,256]{2,1,0:T(8,128)(2,1)S(1)} %collective-permute-done.4.inners, bf16[3,128,256]{2,1,0:T(8,128)(2,1)S(1)} %collective-permute-done.1.got_0, ...), custom_call_target="tpu_custom_call" | custom-call | flops 3758096384 | bytes 10485760 | tf_op jit(solution)/shard_map/main/pallas_call | solution.py:333
  23.4 2.3 %collective-permute-done.5.arrived = bf16[14,128,256]{2,1,0:T(8,128)(2,1)S(1)} collective-permute-done((bf16[14,128,256]{2,1,0:T(8,128)(2,1)S(1)}, bf16[14,128,256]{2,1,0:T(8,128)(2,1)S(1)}, u32[]{:S(2)}, u32[]{:S(2)}) %collective-permute-start.5) | collective-permute-done | bytes 917536 | tf_op jit(solution)/shard_map/ppermute | solution.py:358
  25.7 1.2 %finish.2._ = bf16[2,16,128,256]{3,2,1,0:T(8,128)(2,1)} custom-call(bf16[14,128,256]{2,1,0:T(8,128)(2,1)S(1)} %collective-permute-done.5.arrived, f32[16,128,256]{2,1,0:T(8,128)S(1)} %get-tuple-element.35.base, bf16[3,256,256]{2,1,0:T(8,128)(2,1)S(1)} %get-tuple-element.26.time_kernel, ...), custom_call_target="tpu_custom_call", output_to_operand_aliasing={{}: (3, {})} | custom-call | flops 234881024 | bytes 3670016 | tf_op jit(solution)/shard_map/finish/pallas_call | solution.py:333
  26.9 0.2 collective-permute-done.3.arrived
  27.1 0.9 %finish.3 = bf16[2,16,128,256]{3,2,1,0:T(8,128)(2,1)} custom-call(bf16[2,128,256]{2,1,0:T(8,128)(2,1)S(1)} %collective-permute-done.3.arrived, f32[16,128,256]{2,1,0:T(8,128)S(1)} %get-tuple-element.35.base, bf16[3,256,256]{2,1,0:T(8,128)(2,1)S(1)} %get-tuple-element.26.time_kernel, bf16[2,16,128,256]{3,2,1,0:T(8,128)(2,1)} %finish.2._), custom_call_target="tpu_custom_call", output_to_operand_aliasing={{}: (3, {})} | custom-call | flops 33554432 | bytes 524288 | tf_op jit(solution)/shard_map/finish/pallas_call | solution.py:333
  (1 shorter events, 0.0 us)
Async XLA Ops:
  0.0 5.3 %copy-start = (f32[256]{0:T(256)S(1)}, f32[256]{0:T(256)}, u32[]{:S(2)}) copy-start(f32[256]{0:T(256)} %param.9) | copy-start | bytes 3076
  0.0 5.3 %copy-start.1 = (f32[256]{0:T(256)S(1)}, f32[256]{0:T(256)}, u32[]{:S(2)}) copy-start(f32[256]{0:T(256)} %param.10) | copy-start | bytes 3076
  0.0 5.3 %copy-start.2 = (f32[256]{0:T(256)S(1)}, f32[256]{0:T(256)}, u32[]{:S(2)}) copy-start(f32[256]{0:T(256)} %param.12) | copy-start | bytes 3076
  0.9 8.9 %collective-permute-start = (bf16[2,128,256]{2,1,0:T(8,128)(2,1)S(1)}, bf16[2,128,256]{2,1,0:T(8,128)(2,1)S(1)}, u32[]{:S(2)}, u32[]{:S(2)}) collective-permute-start(bf16[2,128,256]{2,1,0:T(8,128)(2,1)S(1)} %split.2.edges_b.edges), channel_id=1, source_target_pairs={{0,4},{4,8},{8,12},{12,0},{1,5},{5,9},{9,13},{13,1},{2,6},{6,10},{... | collective-permute-start | bytes 393224 | tf_op jit(solution)/shard_map/ppermute | solution.py:346
  2.7 16.1 %collective-permute-start.4 = (bf16[14,128,256]{2,1,0:T(8,128)(2,1)S(1)}, bf16[14,128,256]{2,1,0:T(8,128)(2,1)S(1)}, u32[]{:S(2)}, u32[]{:S(2)}) collective-permute-start(bf16[14,128,256]{2,1,0:T(8,128)(2,1)S(1)} %split.3.inners_b.inners), channel_id=1, source_target_pairs={{0,4},{4,8},{8,12},{12,0},{1,5},{5,9},{9,13},{13,1},{2,6},{6,10},{... | collective-permute-start | bytes 2752520 | tf_op jit(solution)/shard_map/ppermute | solution.py:348
  9.8 15.9 %collective-permute-start.5 = (bf16[14,128,256]{2,1,0:T(8,128)(2,1)S(1)}, bf16[14,128,256]{2,1,0:T(8,128)(2,1)S(1)}, u32[]{:S(2)}, u32[]{:S(2)}) collective-permute-start(bf16[14,128,256]{2,1,0:T(8,128)(2,1)S(1)} %get-tuple-element.29.normed_ai), channel_id=1, source_target_pairs={{0,4},{4,8},{8,12},{12,0},{1,5},{5,9},{9,13},{13,1},{2,6},{6,10},{... | collective-permute-start | bytes 2752520 | tf_op jit(solution)/shard_map/ppermute | solution.py:358
  9.9 6.6 %collective-permute-start.1 = (bf16[3,128,256]{2,1,0:T(8,128)(2,1)S(1)}, bf16[3,128,256]{2,1,0:T(8,128)(2,1)S(1)}, u32[]{:S(2)}, u32[]{:S(2)}) collective-permute-start(bf16[3,128,256]{2,1,0:T(8,128)(2,1)S(1)} %get-tuple-element.22), channel_id=1, source_target_pairs={{0,1},{1,2},{2,3},{3,7},{4,0},{5,4},{6,5},{7,6},{8,9},{9,10},{10,1... | collective-permute-start | bytes 589832 | tf_op jit(solution)/shard_map/ppermute | solution.py:363
  11.5 5.7 %collective-permute-start.2 = (bf16[3,128,256]{2,1,0:T(8,128)(2,1)S(1)}, bf16[3,128,256]{2,1,0:T(8,128)(2,1)S(1)}, u32[]{:S(2)}, u32[]{:S(2)}) collective-permute-start(bf16[3,128,256]{2,1,0:T(8,128)(2,1)S(1)} %get-tuple-element.23), channel_id=1, source_target_pairs={{1,0},{2,1},{3,2},{7,3},{0,4},{4,5},{5,6},{6,7},{9,8},{10,9},{11,1... | collective-permute-start | bytes 589832 | tf_op jit(solution)/shard_map/ppermute | solution.py:364
  14.4 4.4 %copy-start.3 = (f32[256]{0:T(256)S(1)}, f32[256]{0:T(256)}, u32[]{:S(2)}) copy-start(f32[256]{0:T(256)} %param.13) | copy-start | bytes 3076
  18.5 8.6 %collective-permute-start.3 = (bf16[2,128,256]{2,1,0:T(8,128)(2,1)S(1)}, bf16[2,128,256]{2,1,0:T(8,128)(2,1)S(1)}, u32[]{:S(2)}, u32[]{:S(2)}) collective-permute-start(bf16[2,128,256]{2,1,0:T(8,128)(2,1)S(1)} %get-tuple-element.25.normed_ae), channel_id=1, source_target_pairs={{0,4},{4,8},{8,12},{12,0},{1,5},{5,9},{9,13},{13,1},{2,6},{6,10},{... | collective-permute-start | bytes 393224 | tf_op jit(solution)/shard_map/ppermute | solution.py:376

commit v4 on v3

--- a/solution.py
+++ b/solution.py
@@ -87,17 +87,42 @@
                 jobs[n - stage][stage]()
 
 
-def split_kernel(first, feats, out, sems):
-    rows = feats.shape[1]
-    places = [(first, rows - first, 0)] if first else [(0, 1, 0), (rows - 1, rows, 1)]
-    copies = [
-        pltpu.make_async_copy(feats.at[1, pl.ds(a, b - a)], out.at[pl.ds(at, b - a)], sems.at[n])
-        for n, (a, b, at) in enumerate(places)
-    ]
+def wait_all(pairs, sems):
+    copies = [pltpu.make_async_copy(a, b, sems.at[n]) for n, (a, b) in enumerate(pairs)]
     for copy in copies:
         copy.start()
     for copy in copies:
         copy.wait()
+
+
+def end_pairs(feats, ends):
+    rows, lower = feats.shape[1], ends.shape[0] // 2
+    upper = ends.shape[0] - lower
+    return [
+        (feats.at[1, pl.ds(0, upper)], ends.at[pl.ds(0, upper)]),
+        (feats.at[1, pl.ds(rows - lower, lower)], ends.at[pl.ds(upper, lower)]),
+    ]
+
+
+def ends_kernel(count, feats, ends, sems):
+    first = first_of_pair(count)
+
+    @pl.when(first)
+    def _():
+        ends[...] = jnp.zeros_like(ends)
+
+    @pl.when(jnp.logical_not(first))
+    def _():
+        wait_all(end_pairs(feats, ends), sems)
+
+
+def load_kernel(_, feats, ends, middle, sems):
+    upper = ends.shape[0] - ends.shape[0] // 2
+    wait_all(end_pairs(feats, ends) + [(feats.at[1, pl.ds(upper, middle.shape[0])], middle)], sems)
+
+
+def load_rest_kernel(_, feats, kernel, time_kernel, raw_a, kernel_out, time_out, sems):
+    wait_all([(feats.at[0], raw_a), (kernel, kernel_out), (time_kernel, time_out)], sems)
 
 
 def goes_up(index, count):
@@ -123,15 +148,35 @@
     return lax.rem(index, 2) == 0 if count % 2 == 0 else index >= 0
 
 
-def halo_kernel(count, raw_a, edges_b, edges, send_0, send_1):
+def first_of_pair(count):
+    index = lax.axis_index("frame")
+    return lax.rem(index, 2) == 0 if count % 2 == 0 else index < 0
+
+
+def halo_kernel(count, raw_a, edges_b, *refs):
+    *arrived, edges, send_0, send_1 = refs
     rows = raw_a.shape[0]
+    if len(arrived) == 1:
+        edges[...] = arrived[0][...]
+    else:
+        first = first_of_pair(count)
+
+        @pl.when(first)
+        def _():
+            edges[...] = arrived[0][...]
+
+        @pl.when(jnp.logical_not(first))
+        def _():
+            edges[...] = arrived[1][...]
+
+    last = edges.shape[0] - 1
 
     def fill(up_rows, down_rows):
-        for n, (first, last) in enumerate((
-            (raw_a.at[0], raw_a.at[rows - 1]), (edges_b.at[0], edges_b.at[1]), (edges.at[0], edges.at[1])
+        for n, (upper, lower) in enumerate((
+            (raw_a.at[0], raw_a.at[rows - 1]), (edges_b.at[0], edges_b.at[last]), (edges.at[0], edges.at[last])
         )):
-            up_rows[n] = last[...]
-            down_rows[n] = first[...]
+            up_rows[n] = lower[...]
+            down_rows[n] = upper[...]
 
     up = up_first(count)
     pl.when(up)(lambda: fill(send_0, send_1))
@@ -147,13 +192,17 @@
     return row, jnp.where(there, 1.0, 0.0)
 
 
-def framed(upper, edges, inners, lower):
-    rows = inners.shape[0] + 2
+def framed(upper, ends, middle, lower):
+    lower_ends, count = ends.shape[0] // 2, middle.shape[0]
+    upper_ends = ends.shape[0] - lower_ends
+    rows = ends.shape[0] + count
 
     def get_row(r):
         if r < 0 or r >= rows:
             return upper() if r < 0 else lower()
-        return edges[0] if r == 0 else edges[1] if r == rows - 1 else inners[r - 1]
+        if r < upper_ends or r >= rows - lower_ends:
+            return ends[r if r < upper_ends else r - count]
+        return middle[r - upper_ends]
 
     return get_row
 
@@ -175,38 +224,15 @@
     return emit
 
 
-def inner_a_kernel(feats, kernel, time_kernel, space_gain, space_bias, time_gain,
-                   hidden_ref, normed_ref, raw, kernel_out, time_out, shifted, sums, sems):
-    rows = raw.shape[0]
-    half = rows // 2
-    pairs = [
-        (feats.at[0, pl.ds(0, half)], raw.at[pl.ds(0, half)]),
-        (kernel, kernel_out),
-        (feats.at[0, pl.ds(half, rows - half)], raw.at[pl.ds(half, rows - half)]),
-        (time_kernel, time_out),
-    ]
-    copies = [pltpu.make_async_copy(a, b, sems.at[n]) for n, (a, b) in enumerate(pairs)]
-    for copy in copies:
-        copy.start()
-    jobs = spatial_jobs(lambda r: raw[r], blocks(1, rows - 1), 0, shifted, sums, 0, kernel_out,
-                        (space_gain, space_bias, time_gain), inner_emit(hidden_ref, normed_ref))
-    copies[0].wait()
-    jobs[0][0]()
-    jobs[0][0] = None
-    for copy in copies[1:]:
-        copy.wait()
-    run(jobs)
-
-
-def inner_b_kernel(edges, inners, kernel, space_gain, space_bias, time_gain,
-                   hidden_ref, normed_ref, shifted, sums):
-    rows = inners.shape[0] + 2
-    run(spatial_jobs(framed(None, edges, inners, None), blocks(1, rows - 1), 0, shifted, sums, 0,
-                     kernel, (space_gain, space_bias, time_gain), inner_emit(hidden_ref, normed_ref)))
+def inner_kernel(_, *refs):
+    *raw, kernel, space_gain, space_bias, time_gain, hidden_ref, normed_ref, shifted, sums = refs
+    get_row = framed(None, *raw, None) if len(raw) == 2 else lambda r: raw[0][r]
+    run(spatial_jobs(get_row, blocks(1, hidden_ref.shape[0] + 1), 0, shifted, sums, 0, kernel,
+                     (space_gain, space_bias, time_gain), inner_emit(hidden_ref, normed_ref)))
 
 
 def edges_kernel(counts, raw_a, edges_b, inners_b, got_0, got_1, kernel, space_gain, space_bias, time_gain,
-                 hidden_a, normed_a, hidden_b, normed_b, shifted, sums):
+                 time_kernel, hidden_a, normed_a, hidden_b, normed_b, product_a, shifted, sums):
     rows = raw_a.shape[0]
     weights = (space_gain, space_bias, time_gain)
 
@@ -224,6 +250,9 @@
             jobs += spatial_jobs(get_row, [(r, 1)], offset, shifted.at[2 * n + m], sums, 2 * n + m,
                                  kernel, weights, emit)
     run(jobs)
+    product = jnp.dot(normed_a[...].reshape(-1, normed_a.shape[-1]), time_kernel[2],
+                      preferred_element_type=F32)
+    product_a[...] = product.astype(BF16).reshape(product_a.shape)
 
 
 def main_kernel(counts, edges, inners, got_0, got_1, kernel, space_gain, space_bias, time_gain,
@@ -275,18 +304,29 @@
         copy.wait()
 
 
-def finish_kernel(places, arrived, base, time_kernel, _, out_ref, decoded, sems):
+def inner_finish_kernel(arrived, base, time_kernel, _, out_ref, decoded, sems):
     cols, channels = base.shape[1:]
     keep = jnp.where(lax.axis_index("frame") > 0, 1.0, 0.0)
     kernel = (time_kernel[2].astype(F32) * keep).astype(BF16)
     copies = []
-    for n, (at, row, count) in enumerate(places):
+    for n, (row, count) in enumerate(blocks(1, arrived.shape[0] + 1)):
+        at = pl.ds(row - 1, count)
         total = base[row : row + count].reshape(count * cols, channels)
-        total += jnp.dot(arrived[at : at + count].reshape(count * cols, channels), kernel,
-                         preferred_element_type=F32)
-        decoded[at : at + count] = total.astype(BF16).reshape(count, cols, channels)
-        copies.append(pltpu.make_async_copy(
-            decoded.at[pl.ds(at, count)], out_ref.at[0, pl.ds(row, count)], sems.at[n]))
+        total += jnp.dot(arrived[at].reshape(count * cols, channels), kernel, preferred_element_type=F32)
+        decoded[at] = total.astype(BF16).reshape(count, cols, channels)
+        copies.append(pltpu.make_async_copy(decoded.at[at], out_ref.at[0, pl.ds(row, count)], sems.at[n]))
+        copies[-1].start()
+    for copy in copies:
+        copy.wait()
+
+
+def edge_finish_kernel(products, base, _, out_ref, decoded, sems):
+    rows = base.shape[0]
+    keep = jnp.where(lax.axis_index("frame") > 0, 1.0, 0.0)
+    copies = []
+    for n, row in enumerate((0, rows - 1)):
+        decoded[n] = (base[row] + products[n].astype(F32) * keep).astype(BF16)
+        copies.append(pltpu.make_async_copy(decoded.at[pl.ds(n, 1)], out_ref.at[0, pl.ds(row, 1)], sems.at[n]))
         copies[-1].start()
     for copy in copies:
         copy.wait()
@@ -336,44 +376,49 @@
             compiler_params=pltpu.CompilerParams(vmem_limit_bytes=mebibytes * 1024 * 1024), **more,
         )(*arrays)
 
-    def split(first, feats, n):
+    def inner_rows(raw, scale, name, after):
         return call(
-            functools.partial(split_kernel, first), [(HBM, feats)], [shape(n)],
-            [pltpu.SemaphoreType.DMA((2,))], 1, "split",
-        )[0]
-
-    edge_out = split(0, features, 2)
-    edge = lax.ppermute(edge_out, "frame", onward)
-    inner_out = split(1, features, rows - 2)
+            inner_kernel, [(ANY, after), *raw, space_kernel, *weights],
+            [shape(rows - 2, dtype=F32), shape(rows - 2)], [room(3, rows), sums],
+            6, name, cost_estimate=cost(rows * cols, 9 * scale, channels, 3),
+        )
+
+    held = 3 if rows >= 6 else 2
+    (ends,) = call(
+        functools.partial(ends_kernel, count_f), [(HBM, features)], [shape(held)],
+        [pltpu.SemaphoreType.DMA((2,))], 1, "ends",
+    )
+    edge = [lax.ppermute(ends, "frame", onward)]
+    edge_out, inner_out = call(
+        load_kernel, [(ANY, ends), (HBM, features)], [shape(held), shape(rows - held)],
+        [pltpu.SemaphoreType.DMA((3,))], 1, "load",
+    )
+    raw_a, space_kernel, time_kernel = call(
+        load_rest_kernel, [(ANY, inner_out), (HBM, features), (HBM, space_kernel), (HBM, time_kernel)],
+        [shape(rows), jax.ShapeDtypeStruct(space_kernel.shape, BF16),
+         jax.ShapeDtypeStruct(time_kernel.shape, BF16)],
+        [pltpu.SemaphoreType.DMA((3,))], 1, "load_rest",
+    )
     inner = lax.ppermute(inner_out, "frame", onward)
-
-    hidden_ai, normed_ai, raw_a, space_kernel, time_kernel = call(
-        inner_a_kernel,
-        [(HBM, features), (HBM, space_kernel), (HBM, time_kernel), *weights],
-        [shape(rows - 2, dtype=F32), shape(rows - 2), shape(rows),
-         jax.ShapeDtypeStruct(space_kernel.shape, BF16), jax.ShapeDtypeStruct(time_kernel.shape, BF16)],
-        [room(3, rows), sums, pltpu.SemaphoreType.DMA((4,))],
-        6, "inner_a", cost_estimate=cost(rows * cols, 9, channels, 3),
-    )
-    arrived = lax.ppermute(normed_ai, "frame", onward)
-
-    send_0, send_1 = call(
-        functools.partial(halo_kernel, count_f), [raw_a, edge_out, edge], [shape(3), shape(3)], [], 1, "halo",
-    )
+    if count_f % 2 == 0:
+        edge.append(lax.ppermute(edge_out, "frame", [(f, f ^ 1) for f in range(count_f)]))
+
+    edge, send_0, send_1 = call(
+        functools.partial(halo_kernel, count_f), [raw_a, edge_out, *edge],
+        [shape(held), shape(3), shape(3)], [], 1, "halo",
+    )
+    hidden_ai, normed_ai = inner_rows([raw_a], 8, "inner_a", send_0)
     got_0 = lax.ppermute(send_0, ("frame", "band"), ring)
     got_1 = lax.ppermute(send_1, ("frame", "band"), [(t, s) for s, t in ring])
-    send_0, send_1, edge_b = lax.optimization_barrier((send_0, send_1, edge_out))
-    hidden_bi, normed_bi = call(
-        inner_b_kernel, [edge_b, inner_out, space_kernel, *weights],
-        [shape(rows - 2, dtype=F32), shape(rows - 2)], [room(3, rows), sums],
-        6, "inner_b", cost_estimate=cost(rows * cols, 9 * 8, channels, 3),
-    )
-    hidden_ae, normed_ae, hidden_be, normed_be = call(
-        functools.partial(edges_kernel, counts), [raw_a, edge_out, inner_out, got_0, got_1, space_kernel, *weights],
-        [shape(2, dtype=F32), shape(2)] * 2, [room(4, 3, 3), sums],
+    arrived = lax.ppermute(normed_ai, "frame", onward[:-1])
+    hidden_bi, normed_bi = inner_rows([edge_out, inner_out], 1, "inner_b", normed_ai)
+    hidden_ae, normed_ae, hidden_be, normed_be, product_ae = call(
+        functools.partial(edges_kernel, counts), [raw_a, edge_out, inner_out, got_0, got_1, space_kernel, *weights,
+         time_kernel],
+        [shape(2, dtype=F32), shape(2)] * 2 + [shape(2)], [room(4, 3, 3), sums],
         4, "edges", cost_estimate=cost(4 * cols, 9, channels, 3),
     )
-    edge_arrived = lax.ppermute(normed_ae, "frame", onward)
+    edge_arrived = lax.ppermute(product_ae, "frame", onward)
 
     decoded, base = call(
         functools.partial(main_kernel, counts),
@@ -381,18 +426,18 @@
          hidden_ae, hidden_ai, normed_ae, normed_ai, hidden_be, hidden_bi, normed_be, normed_bi],
         [(ANY, jax.ShapeDtypeStruct(features.shape, BF16)), shape(rows, dtype=F32)],
         [room(3, rows + 2), sums, room(rows), room(rows), pltpu.SemaphoreType.DMA((count,))],
-        9, "main", cost_estimate=cost(rows * cols, 14, channels, 10),
-    )
-    inner_places = [(r - 1, r, n) for r, n in blocks(1, rows - 1)]
-    edge_places = [(0, 0, 1), (1, rows - 1, 1)]
-    for part, places in ((arrived, inner_places), (edge_arrived, edge_places)):
-        decoded = call(
-            functools.partial(finish_kernel, places), [part, base, time_kernel, (ANY, decoded)],
-            [(ANY, jax.ShapeDtypeStruct(features.shape, BF16))],
-            [room(part.shape[0]), pltpu.SemaphoreType.DMA((len(places),))],
-            3, "finish", input_output_aliases={3: 0},
-            cost_estimate=cost(part.shape[0] * cols, 1, channels, 4),
-        )[0]
+        9, "main", cost_estimate=cost(rows * cols, 14 * 8, channels, 10),
+    )
+    for kernel, inputs, n in (
+        (inner_finish_kernel, [arrived, base, time_kernel], len(blocks(1, rows - 1))),
+        (edge_finish_kernel, [edge_arrived, base], 2),
+    ):
+        (decoded,) = call(
+            kernel, [*inputs, (ANY, decoded)], [(ANY, jax.ShapeDtypeStruct(features.shape, BF16))],
+            [room(inputs[0].shape[0]), pltpu.SemaphoreType.DMA((n,))],
+            3, "finish", input_output_aliases={len(inputs): 0},
+            cost_estimate=cost(inputs[0].shape[0] * cols, 1, channels, 4),
+        )
     return decoded
 
 

time: 28.4 us -> 27.4 us (0.965)
  the two profiles are of different devices: /device:TPU:0 before, /device:TPU:18 now
where the time goes in v4:
time: 27.4 us; the launch traced here: 27.2 us
  Pallas kernels  16.7 us (61%)
  starting transfers between devices  5.53 us (20%)
  waiting for transfers between devices  4.55 us (17%)
  between operations  0.31 us (1%)
    pallas_call x10, Pallas kernels, call(): pl.pallas_call(kernel, in_specs=list(specs), out_specs=list(out_specs), o...  16.7 us
    ppermute x1, waiting for transfers between devices, body(): arrived = lax.ppermute(normed_ai, 'frame', onward[:-1])  3.58 us
    ppermute x1, starting transfers between devices, body(): arrived = lax.ppermute(normed_ai, 'frame', onward[:-1])  1.92 us
    ppermute x1, starting transfers between devices, body(): got_0 = lax.ppermute(send_0, ('frame', 'band'), ring)  1.59 us
    ppermute x1, waiting for transfers between devices, body(): edge = [lax.ppermute(ends, 'frame', onward)]  0.78 us
    ppermute x1, starting transfers between devices, body(): edge = [lax.ppermute(ends, 'frame', onward)]  0.78 us
  transfers between devices with their start and end apart: 7, of which 3 were waited for; matrix products, arithmetic and copies ran while one was open for 0% of the time, Pallas kernels for 59%

profile of v4, /device:TPU:18, one launch (start us, length us, event | category | flops | bytes accessed | tf_op | source)
XLA Modules:
  0.0 27.2 jit_solution(18190599370841868313)
XLA Ops:
  0.0 0.8 %collective-permute-start = (bf16[3,128,256]{2,1,0:T(8,128)(2,1)S(1)}, bf16[3,128,256]{2,1,0:T(8,128)(2,1)S(1)}, u32[]{:S(2)}, u32[]{:S(2)}) collective-permute-start(bf16[3,128,256]{2,1,0:T(8,128)(2,1)S(1)} %ends.1._), channel_id=1, source_target_pairs={{0,4},{4,8},{8,12},{12,0},{1,5},{5,9},{9,13},{13,1},{2,6},{6,10},{... | collective-permute-start | bytes 589832 | tf_op jit(solution)/shard_map/ppermute | solution.py:391
  0.8 1.3 %load.1 = (bf16[3,128,256]{2,1,0:T(8,128)(2,1)S(1)}, bf16[13,128,256]{2,1,0:T(8,128)(2,1)S(1)}) custom-call(bf16[3,128,256]{2,1,0:T(8,128)(2,1)S(1)} %ends.1._, bf16[2,16,128,256]{3,2,1,0:T(8,128)(2,1)} %feats.5), custom_call_target="tpu_custom_call" | custom-call | tf_op jit(solution)/shard_map/load/pallas_call | solution.py:373
  2.1 0.1 collective-permute-start.1
  2.2 0.0 copy-start
  2.2 0.0 copy-start.1
  2.2 0.0 copy-start.2
  2.2 0.5 %collective-permute-start.5 = (bf16[13,128,256]{2,1,0:T(8,128)(2,1)S(1)}, bf16[13,128,256]{2,1,0:T(8,128)(2,1)S(1)}, u32[]{:S(2)}, u32[]{:S(2)}) collective-permute-start(bf16[13,128,256]{2,1,0:T(8,128)(2,1)S(1)} %get-tuple-element.24._.inners_b.refs_1_), channel_id=1, source_target_pairs={{0,4},{4,8},{8,12},{12,0},{1,5},{5,9},{9,13},{13,1},{2,6},{6,10},{... | collective-permute-start | bytes 2555912 | tf_op jit(solution)/shard_map/ppermute | solution.py:402
  2.7 1.7 %load_rest.1 = (bf16[16,128,256]{2,1,0:T(8,128)(2,1)S(1)}, bf16[3,3,256,256]{3,2,1,0:T(8,128)(2,1)S(1)}, bf16[3,256,256]{2,1,0:T(8,128)(2,1)S(1)}) custom-call(bf16[13,128,256]{2,1,0:T(8,128)(2,1)S(1)} %get-tuple-element.24._.inners_b.refs_1_, bf16[2,16,128,256]{3,2,1,0:T(8,128)(2,1)} %feats.5, bf16[3,3,256,256]{3,2,1,0:T(8,128)(2,1)} %kernel.1, ...), custom_call_target="tpu_custom_call" | custom-call | tf_op jit(solution)/shard_map/load_rest/pallas_call | solution.py:373
  4.4 0.8 %collective-permute-done.refs_0_ = bf16[3,128,256]{2,1,0:T(8,128)(2,1)S(1)} collective-permute-done((bf16[3,128,256]{2,1,0:T(8,128)(2,1)S(1)}, bf16[3,128,256]{2,1,0:T(8,128)(2,1)S(1)}, u32[]{:S(2)}, u32[]{:S(2)}) %collective-permute-start) | collective-permute-done | bytes 196640 | tf_op jit(solution)/shard_map/ppermute | solution.py:391
  5.2 0.0 collective-permute-done.1.refs_1_
  5.2 1.6 %collective-permute-start.2 = (bf16[3,128,256]{2,1,0:T(8,128)(2,1)S(1)}, bf16[3,128,256]{2,1,0:T(8,128)(2,1)S(1)}, u32[]{:S(2)}, u32[]{:S(2)}) collective-permute-start(bf16[3,128,256]{2,1,0:T(8,128)(2,1)S(1)} %get-tuple-element.27._), channel_id=1, source_target_pairs={{0,1},{1,2},{2,3},{3,7},{4,0},{5,4},{6,5},{7,6},{8,9},{9,10},{10,1... | collective-permute-start | bytes 589832 | tf_op jit(solution)/shard_map/ppermute | solution.py:411
  6.8 0.4 %collective-permute-start.3 = (bf16[3,128,256]{2,1,0:T(8,128)(2,1)S(1)}, bf16[3,128,256]{2,1,0:T(8,128)(2,1)S(1)}, u32[]{:S(2)}, u32[]{:S(2)}) collective-permute-start(bf16[3,128,256]{2,1,0:T(8,128)(2,1)S(1)} %get-tuple-element.28), channel_id=1, source_target_pairs={{1,0},{2,1},{3,2},{7,3},{0,4},{4,5},{5,6},{6,7},{9,8},{10,9},{11,1... | collective-permute-start | bytes 589832 | tf_op jit(solution)/shard_map/ppermute | solution.py:412
  7.3 0.0 copy-done
  7.3 0.0 copy-done.1
  7.3 0.0 copy-done.2
  7.3 2.9 %inner_a.1 = (f32[14,128,256]{2,1,0:T(8,128)S(1)}, bf16[14,128,256]{2,1,0:T(8,128)(2,1)S(1)}) custom-call(bf16[3,128,256]{2,1,0:T(8,128)(2,1)S(1)} %get-tuple-element.27._, bf16[16,128,256]{2,1,0:T(8,128)(2,1)S(1)} %get-tuple-element.25.raw_a.refs_0_, bf16[3,3,256,256]{3,2,1,0:T(8,128)(2,1)S(1)} %get-tuple-element.29.kernel.refs_1_.refs_2_, ...), custom_call_target="tpu_custom_call" | custom-call | flops 19327352832 | bytes 3145728 | tf_op jit(solution)/shard_map/inner_a/pallas_call | solution.py:373
  10.2 1.9 %collective-permute-start.6 = (bf16[14,128,256]{2,1,0:T(8,128)(2,1)S(1)}, bf16[14,128,256]{2,1,0:T(8,128)(2,1)S(1)}, u32[]{:S(2)}, u32[]{:S(2)}) collective-permute-start(bf16[14,128,256]{2,1,0:T(8,128)(2,1)S(1)} %get-tuple-element.36._.normed_ai), channel_id=1, source_target_pairs={{0,4},{4,8},{8,12},{1,5},{5,9},{9,13},{2,6},{6,10},{10,14},{3,7},{... | collective-permute-start | bytes 2752520 | tf_op jit(solution)/shard_map/ppermute | solution.py:413
  12.1 2.9 %inner_b.1 = (f32[14,128,256]{2,1,0:T(8,128)S(1)}, bf16[14,128,256]{2,1,0:T(8,128)(2,1)S(1)}) custom-call(bf16[14,128,256]{2,1,0:T(8,128)(2,1)S(1)} %get-tuple-element.36._.normed_ai, bf16[3,128,256]{2,1,0:T(8,128)(2,1)S(1)} %get-tuple-element.26.edges_b.refs_0_, bf16[13,128,256]{2,1,0:T(8,128)(2,1)S(1)} %get-tuple-element.24._.inners_b.refs_1_, ...), custom_call_target="tpu_custom_call" | custom-call | flops 2415919104 | bytes 3145728 | tf_op jit(solution)/shard_map/inner_b/pallas_call | solution.py:373
  15.0 0.0 copy-start.3
  15.0 0.0 collective-permute-done.2.got_0
  15.1 0.0 collective-permute-done.3.got_1
  15.1 1.3 %edges.1 = (f32[2,128,256]{2,1,0:T(8,128)S(1)}, bf16[2,128,256]{2,1,0:T(8,128)(2,1)S(1)}, f32[2,128,256]{2,1,0:T(8,128)S(1)}, bf16[2,128,256]{2,1,0:T(8,128)(2,1)S(1)}, bf16[2,128,256]{2,1,0:T(8,128)(2,1)S(1)}) custom-call(bf16[16,128,256]{2,1,0:T(8,128)(2,1)S(1)} %get-tuple-element.25.raw_a.refs_0_, ...), custom_call_target="tpu_custom_call" | custom-call | flops 603979776 | bytes 786432 | tf_op jit(solution)/shard_map/edges/pallas_call | solution.py:373
  16.4 0.2 collective-permute-start.4
  16.6 0.0 collective-permute-done.5.inners
  16.6 0.0 copy-done.3
  16.6 4.7 %main.1 = (bf16[2,16,128,256]{3,2,1,0:T(8,128)(2,1)}, f32[16,128,256]{2,1,0:T(8,128)S(1)}) custom-call(bf16[3,128,256]{2,1,0:T(8,128)(2,1)S(1)} %get-tuple-element.32.edges, bf16[13,128,256]{2,1,0:T(8,128)(2,1)S(1)} %collective-permute-done.5.inners, bf16[3,128,256]{2,1,0:T(8,128)(2,1)S(1)} %collective-permute-done.2.got_0, ...), custom_call_target="tpu_custom_call" | custom-call | flops 30064771072 | bytes 10485760 | tf_op jit(solution)/shard_map/main/pallas_call | solution.py:373
  21.3 3.6 %collective-permute-done.6.arrived = bf16[14,128,256]{2,1,0:T(8,128)(2,1)S(1)} collective-permute-done((bf16[14,128,256]{2,1,0:T(8,128)(2,1)S(1)}, bf16[14,128,256]{2,1,0:T(8,128)(2,1)S(1)}, u32[]{:S(2)}, u32[]{:S(2)}) %collective-permute-start.6) | collective-permute-done | bytes 917536 | tf_op jit(solution)/shard_map/ppermute | solution.py:413
  24.9 1.2 %finish.2._ = bf16[2,16,128,256]{3,2,1,0:T(8,128)(2,1)} custom-call(bf16[14,128,256]{2,1,0:T(8,128)(2,1)S(1)} %collective-permute-done.6.arrived, f32[16,128,256]{2,1,0:T(8,128)S(1)} %get-tuple-element.41.base, bf16[3,256,256]{2,1,0:T(8,128)(2,1)S(1)} %get-tuple-element.30.time_kernel, ...), custom_call_target="tpu_custom_call", output_to_operand_aliasing={{}: (3, {})} | custom-call | flops 234881024 | bytes 3670016 | tf_op jit(solution)/shard_map/finish/pallas_call | solution.py:373
  26.1 0.2 collective-permute-done.4.products
  26.3 0.7 %finish.3 = bf16[2,16,128,256]{3,2,1,0:T(8,128)(2,1)} custom-call(bf16[2,128,256]{2,1,0:T(8,128)(2,1)S(1)} %collective-permute-done.4.products, f32[16,128,256]{2,1,0:T(8,128)S(1)} %get-tuple-element.41.base, bf16[2,16,128,256]{3,2,1,0:T(8,128)(2,1)} %finish.2._), custom_call_target="tpu_custom_call", output_to_operand_aliasing={{}: (2, {})} | custom-call | flops 33554432 | bytes 524288 | tf_op jit(solution)/shard_map/finish/pallas_call | solution.py:373
  (2 shorter events, 0.1 us)
Async XLA Ops:
  0.0 5.1 %collective-permute-start = (bf16[3,128,256]{2,1,0:T(8,128)(2,1)S(1)}, bf16[3,128,256]{2,1,0:T(8,128)(2,1)S(1)}, u32[]{:S(2)}, u32[]{:S(2)}) collective-permute-start(bf16[3,128,256]{2,1,0:T(8,128)(2,1)S(1)} %ends.1._), channel_id=1, source_target_pairs={{0,4},{4,8},{8,12},{12,0},{1,5},{5,9},{9,13},{13,1},{2,6},{6,10},{... | collective-permute-start | bytes 589832 | tf_op jit(solution)/shard_map/ppermute | solution.py:391
  2.1 3.1 %collective-permute-start.1 = (bf16[3,128,256]{2,1,0:T(8,128)(2,1)S(1)}, bf16[3,128,256]{2,1,0:T(8,128)(2,1)S(1)}, u32[]{:S(2)}, u32[]{:S(2)}) collective-permute-start(bf16[3,128,256]{2,1,0:T(8,128)(2,1)S(1)} %get-tuple-element.26.edges_b.refs_0_), channel_id=1, source_target_pairs={{0,4},{4,0},{8,12},{12,8},{1,5},{5,1},{9,13},{13,9},{2,6},{6,2},{1... | collective-permute-start | bytes 589832 | tf_op jit(solution)/shard_map/ppermute | solution.py:404
  2.2 5.1 %copy-start = (f32[256]{0:T(256)S(1)}, f32[256]{0:T(256)}, u32[]{:S(2)}) copy-start(f32[256]{0:T(256)} %param.9) | copy-start | bytes 3076
  2.2 5.1 %copy-start.1 = (f32[256]{0:T(256)S(1)}, f32[256]{0:T(256)}, u32[]{:S(2)}) copy-start(f32[256]{0:T(256)} %param.10) | copy-start | bytes 3076
  2.2 5.1 %copy-start.2 = (f32[256]{0:T(256)S(1)}, f32[256]{0:T(256)}, u32[]{:S(2)}) copy-start(f32[256]{0:T(256)} %param.12) | copy-start | bytes 3076
  2.2 14.4 %collective-permute-start.5 = (bf16[13,128,256]{2,1,0:T(8,128)(2,1)S(1)}, bf16[13,128,256]{2,1,0:T(8,128)(2,1)S(1)}, u32[]{:S(2)}, u32[]{:S(2)}) collective-permute-start(bf16[13,128,256]{2,1,0:T(8,128)(2,1)S(1)} %get-tuple-element.24._.inners_b.refs_1_), channel_id=1, source_target_pairs={{0,4},{4,8},{8,12},{12,0},{1,5},{5,9},{9,13},{13,1},{2,6},{6,10},{... | collective-permute-start | bytes 2555912 | tf_op jit(solution)/shard_map/ppermute | solution.py:402
  5.2 9.8 %collective-permute-start.2 = (bf16[3,128,256]{2,1,0:T(8,128)(2,1)S(1)}, bf16[3,128,256]{2,1,0:T(8,128)(2,1)S(1)}, u32[]{:S(2)}, u32[]{:S(2)}) collective-permute-start(bf16[3,128,256]{2,1,0:T(8,128)(2,1)S(1)} %get-tuple-element.27._), channel_id=1, source_target_pairs={{0,1},{1,2},{2,3},{3,7},{4,0},{5,4},{6,5},{7,6},{8,9},{9,10},{10,1... | collective-permute-start | bytes 589832 | tf_op jit(solution)/shard_map/ppermute | solution.py:411
  6.8 8.2 %collective-permute-start.3 = (bf16[3,128,256]{2,1,0:T(8,128)(2,1)S(1)}, bf16[3,128,256]{2,1,0:T(8,128)(2,1)S(1)}, u32[]{:S(2)}, u32[]{:S(2)}) collective-permute-start(bf16[3,128,256]{2,1,0:T(8,128)(2,1)S(1)} %get-tuple-element.28), channel_id=1, source_target_pairs={{1,0},{2,1},{3,2},{7,3},{0,4},{4,5},{5,6},{6,7},{9,8},{10,9},{11,1... | collective-permute-start | bytes 589832 | tf_op jit(solution)/shard_map/ppermute | solution.py:412
  10.2 14.7 %collective-permute-start.6 = (bf16[14,128,256]{2,1,0:T(8,128)(2,1)S(1)}, bf16[14,128,256]{2,1,0:T(8,128)(2,1)S(1)}, u32[]{:S(2)}, u32[]{:S(2)}) collective-permute-start(bf16[14,128,256]{2,1,0:T(8,128)(2,1)S(1)} %get-tuple-element.36._.normed_ai), channel_id=1, source_target_pairs={{0,4},{4,8},{8,12},{1,5},{5,9},{9,13},{2,6},{6,10},{10,14},{3,7},{... | collective-permute-start | bytes 2752520 | tf_op jit(solution)/shard_map/ppermute | solution.py:413
  15.0 1.6 %copy-start.3 = (f32[256]{0:T(256)S(1)}, f32[256]{0:T(256)}, u32[]{:S(2)}) copy-start(f32[256]{0:T(256)} %param.13) | copy-start | bytes 3076
  16.4 9.9 %collective-permute-start.4 = (bf16[2,128,256]{2,1,0:T(8,128)(2,1)S(1)}, bf16[2,128,256]{2,1,0:T(8,128)(2,1)S(1)}, u32[]{:S(2)}, u32[]{:S(2)}) collective-permute-start(bf16[2,128,256]{2,1,0:T(8,128)(2,1)S(1)} %get-tuple-element.31), channel_id=1, source_target_pairs={{0,4},{4,8},{8,12},{12,0},{1,5},{5,9},{9,13},{13,1},{2,6},{6,10},{... | collective-permute-start | bytes 393224 | tf_op jit(solution)/shard_map/ppermute | solution.py:421

commit v5 on v4

--- a/solution.py
+++ b/solution.py
@@ -13,6 +13,7 @@
 ANY = pl.BlockSpec(memory_space=pl.ANY)
 HBM = pl.BlockSpec(memory_space=pltpu.HBM)
 STEP = 2
+RING_ROWS = 4
 
 
 def blocks(first, last):
@@ -153,6 +154,10 @@
     return lax.rem(index, 2) == 0 if count % 2 == 0 else index < 0
 
 
+def copy_kernel(source, target):
+    target[...] = source[...]
+
+
 def halo_kernel(count, raw_a, edges_b, *refs):
     *arrived, edges, send_0, send_1 = refs
     rows = raw_a.shape[0]
@@ -193,7 +198,8 @@
 
 
 def framed(upper, ends, middle, lower):
-    lower_ends, count = ends.shape[0] // 2, middle.shape[0]
+    middle = middle if isinstance(middle, list) else [middle]
+    lower_ends, count = ends.shape[0] // 2, sum(part.shape[0] for part in middle)
     upper_ends = ends.shape[0] - lower_ends
     rows = ends.shape[0] + count
 
@@ -202,14 +208,22 @@
             return upper() if r < 0 else lower()
         if r < upper_ends or r >= rows - lower_ends:
             return ends[r if r < upper_ends else r - count]
-        return middle[r - upper_ends]
+        part, at = part_of(middle, r - upper_ends)
+        return part[at]
 
     return get_row
 
 
-def inner_emit(hidden_ref, normed_ref):
+def part_of(parts, row):
+    for part in parts:
+        if row < part.shape[0]:
+            return part, row
+        row -= part.shape[0]
+
+
+def inner_emit(start, hidden_ref, normed_ref):
     def emit(first, count, hidden, normed):
-        at = pl.ds(first - 1, count)
+        at = pl.ds(first - start, count)
         shape = (count,) + hidden_ref.shape[1:]
         hidden_ref[at] = hidden.astype(hidden_ref.dtype).reshape(shape)
         normed_ref[at] = normed.astype(BF16).reshape(shape)
@@ -224,11 +238,11 @@
     return emit
 
 
-def inner_kernel(_, *refs):
+def inner_kernel(start, _, *refs):
     *raw, kernel, space_gain, space_bias, time_gain, hidden_ref, normed_ref, shifted, sums = refs
     get_row = framed(None, *raw, None) if len(raw) == 2 else lambda r: raw[0][r]
-    run(spatial_jobs(get_row, blocks(1, hidden_ref.shape[0] + 1), 0, shifted, sums, 0, kernel,
-                     (space_gain, space_bias, time_gain), inner_emit(hidden_ref, normed_ref)))
+    run(spatial_jobs(get_row, blocks(start, start + hidden_ref.shape[0]), 1 - start, shifted, sums, 0, kernel,
+                     (space_gain, space_bias, time_gain), inner_emit(start, hidden_ref, normed_ref)))
 
 
 def edges_kernel(counts, raw_a, edges_b, inners_b, got_0, got_1, kernel, space_gain, space_bias, time_gain,
@@ -255,10 +269,11 @@
     product_a[...] = product.astype(BF16).reshape(product_a.shape)
 
 
-def main_kernel(counts, edges, inners, got_0, got_1, kernel, space_gain, space_bias, time_gain,
-                time_kernel, time_bias, hidden_ae, hidden_ai, normed_ae, normed_ai,
-                hidden_be, hidden_bi, normed_be, normed_bi,
-                out_ref, base, shifted, sums, normed_p, decoded, sems):
+def main_kernel(counts, ring_start, edges, inners, got_0, got_1, kernel, space_gain, space_bias, time_gain,
+                time_kernel, time_bias, hidden_be, hidden_bi, normed_be, normed_bi, hidden_ae, normed_ae, *refs):
+    *refs, out_ref, base, shifted, sums, normed_p, decoded, decoded_ring, sems = refs
+    inner_a, arrived = (refs[:4], refs[4]) if len(refs) > 4 else (refs, None)
+    hidden_ai, normed_ai = inner_a[::2], inner_a[1::2]
     rows, cols, channels = base.shape
     keep = jnp.where(lax.axis_index("frame") > 0, 1.0, 0.0)
 
@@ -286,50 +301,70 @@
             jnp.dot(rows_of(first, count, normed_ae, normed_ai), time_kernel[0], preferred_element_type=F32)
             + jnp.dot(prior, time_kernel[1], preferred_element_type=F32)
         )
-        base[first : first + count] = total.reshape(count, cols, channels)
+        return total
 
     halo = functools.partial(halo_row, counts, got_0, got_1, 2)
     get_row = framed(lambda: halo(True), edges, inners, lambda: halo(False))
     run(spatial_jobs(get_row, blocks(0, rows), 1, shifted, sums, 0, kernel,
                      (space_gain, space_bias, time_gain), emit))
     copies = []
-    for n, (first, count) in enumerate(blocks(0, rows)):
+
+    def write(frame, row, held, at):
+        copies.append(pltpu.make_async_copy(held.at[at], out_ref.at[frame, row], sems.at[len(copies)]))
+        copies[-1].start()
+
+    for first, count in blocks(0, rows):
         out_rows(first, count)
-        copies.append(pltpu.make_async_copy(
-            decoded.at[pl.ds(first, count)], out_ref.at[1, pl.ds(first, count)], sems.at[n]))
-        copies[-1].start()
-    for first, count in blocks(0, rows):
-        base_rows(first, count)
+        write(1, pl.ds(first, count), decoded, pl.ds(first, count))
+    ring_end = ring_start + (0 if arrived is None else arrived.shape[0])
+    lag_kernel = (time_kernel[2].astype(F32) * keep).astype(BF16)
+    for first, count in blocks(ring_start, ring_end):
+        at = pl.ds(first - ring_start, count)
+        total = base_rows(first, count)
+        total += jnp.dot(arrived[at].reshape(count * cols, channels), lag_kernel, preferred_element_type=F32)
+        decoded_ring[at] = total.astype(BF16).reshape(count, cols, channels)
+        write(0, pl.ds(first, count), decoded_ring, at)
+    for first, count in blocks(0, ring_start) + blocks(ring_end, rows):
+        base[first : first + count] = base_rows(first, count).reshape(count, cols, channels)
     for copy in copies:
         copy.wait()
 
 
-def inner_finish_kernel(arrived, base, time_kernel, _, out_ref, decoded, sems):
+def waits_at_end(count):
+    return jnp.logical_and(first_of_pair(count), lax.axis_index("frame") > 0)
+
+
+def inner_finish_kernel(frames, arrived, base, time_kernel, _, decoded, out_ref, sems):
     cols, channels = base.shape[1:]
     keep = jnp.where(lax.axis_index("frame") > 0, 1.0, 0.0)
     kernel = (time_kernel[2].astype(F32) * keep).astype(BF16)
-    copies = []
-    for n, (row, count) in enumerate(blocks(1, arrived.shape[0] + 1)):
+    for row, count in blocks(1, arrived.shape[0] + 1):
         at = pl.ds(row - 1, count)
         total = base[row : row + count].reshape(count * cols, channels)
         total += jnp.dot(arrived[at].reshape(count * cols, channels), kernel, preferred_element_type=F32)
         decoded[at] = total.astype(BF16).reshape(count, cols, channels)
-        copies.append(pltpu.make_async_copy(decoded.at[at], out_ref.at[0, pl.ds(row, count)], sems.at[n]))
+    copy = pltpu.make_async_copy(decoded, out_ref.at[0, pl.ds(1, decoded.shape[0])], sems.at[0])
+
+    @pl.when(waits_at_end(frames))
+    def _():
+        copy.start()
+        copy.wait()
+
+
+def finish_kernel(frames, decoded, products, base, _, out_ref, edges, sems):
+    rows, count = base.shape[0], decoded.shape[0]
+    keep = jnp.where(lax.axis_index("frame") > 0, 1.0, 0.0)
+    second = jnp.logical_not(waits_at_end(frames))
+    inner = pltpu.make_async_copy(decoded, out_ref.at[0, pl.ds(1, count)], sems.at[2])
+    pl.when(second)(inner.start)
+    copies = []
+    for n, row in enumerate((0, rows - 1)):
+        edges[n] = (base[row] + products[n].astype(F32) * keep).astype(BF16)
+        copies.append(pltpu.make_async_copy(edges.at[pl.ds(n, 1)], out_ref.at[0, pl.ds(row, 1)], sems.at[n]))
         copies[-1].start()
     for copy in copies:
         copy.wait()
-
-
-def edge_finish_kernel(products, base, _, out_ref, decoded, sems):
-    rows = base.shape[0]
-    keep = jnp.where(lax.axis_index("frame") > 0, 1.0, 0.0)
-    copies = []
-    for n, row in enumerate((0, rows - 1)):
-        decoded[n] = (base[row] + products[n].astype(F32) * keep).astype(BF16)
-        copies.append(pltpu.make_async_copy(decoded.at[pl.ds(n, 1)], out_ref.at[0, pl.ds(row, 1)], sems.at[n]))
-        copies[-1].start()
-    for copy in copies:
-        copy.wait()
+    pl.when(second)(inner.wait)
 
 
 def cost(pixels, taps, channels, arrays):
@@ -376,11 +411,11 @@
             compiler_params=pltpu.CompilerParams(vmem_limit_bytes=mebibytes * 1024 * 1024), **more,
         )(*arrays)
 
-    def inner_rows(raw, scale, name, after):
+    def inner_rows(raw, start, n, scale, name, after):
         return call(
-            inner_kernel, [(ANY, after), *raw, space_kernel, *weights],
-            [shape(rows - 2, dtype=F32), shape(rows - 2)], [room(3, rows), sums],
-            6, name, cost_estimate=cost(rows * cols, 9 * scale, channels, 3),
+            functools.partial(inner_kernel, start), [(ANY, after), *raw, space_kernel, *weights],
+            [shape(n, dtype=F32), shape(n)], [room(3, n + 2), sums],
+            6, name, cost_estimate=cost(n * cols, 9 * scale, channels, 3),
         )
 
     held = 3 if rows >= 6 else 2
@@ -403,15 +438,23 @@
     if count_f % 2 == 0:
         edge.append(lax.ppermute(edge_out, "frame", [(f, f ^ 1) for f in range(count_f)]))
 
+    ring_rows = min(RING_ROWS, (rows - 2) // STEP // 2 * STEP)
+    parts = [rows - 2 - ring_rows] + [ring_rows] * (ring_rows > 0)
+    inner_a = []
+    if ring_rows:
+        inner_a = inner_rows([raw_a], 1 + parts[0], ring_rows, 1, "inner_a_ring", raw_a)
+    (edge[0],) = call(copy_kernel, [edge[0]], [shape(held)], [], 1, "arrived")
     edge, send_0, send_1 = call(
         functools.partial(halo_kernel, count_f), [raw_a, edge_out, *edge],
         [shape(held), shape(3), shape(3)], [], 1, "halo",
     )
-    hidden_ai, normed_ai = inner_rows([raw_a], 8, "inner_a", send_0)
+    inner_a = [*inner_rows([raw_a], 1, parts[0], 8, "inner_a", send_0), *inner_a]
+    normed_ai = inner_a[1::2]
     got_0 = lax.ppermute(send_0, ("frame", "band"), ring)
     got_1 = lax.ppermute(send_1, ("frame", "band"), [(t, s) for s, t in ring])
-    arrived = lax.ppermute(normed_ai, "frame", onward[:-1])
-    hidden_bi, normed_bi = inner_rows([edge_out, inner_out], 1, "inner_b", normed_ai)
+    arrived = [lax.ppermute(normed_ai[0], "frame", onward[:-1])]
+    arrived += [lax.ppermute(part, "frame", onward) for part in normed_ai[1:]]
+    hidden_bi, normed_bi = inner_rows([edge_out, inner_out], 1, rows - 2, 1, "inner_b", normed_ai[0])
     hidden_ae, normed_ae, hidden_be, normed_be, product_ae = call(
         functools.partial(edges_kernel, counts), [raw_a, edge_out, inner_out, got_0, got_1, space_kernel, *weights,
          time_kernel],
@@ -421,23 +464,24 @@
     edge_arrived = lax.ppermute(product_ae, "frame", onward)
 
     decoded, base = call(
-        functools.partial(main_kernel, counts),
+        functools.partial(main_kernel, counts, 1 + parts[0]),
         [edge, inner, got_0, got_1, space_kernel, *weights, time_kernel, time_bias,
-         hidden_ae, hidden_ai, normed_ae, normed_ai, hidden_be, hidden_bi, normed_be, normed_bi],
+         hidden_be, hidden_bi, normed_be, normed_bi, hidden_ae, normed_ae, *inner_a, *arrived[1:]],
         [(ANY, jax.ShapeDtypeStruct(features.shape, BF16)), shape(rows, dtype=F32)],
-        [room(3, rows + 2), sums, room(rows), room(rows), pltpu.SemaphoreType.DMA((count,))],
+        [room(3, rows + 2), sums, room(rows), room(rows), room(max(ring_rows, 1)),
+         pltpu.SemaphoreType.DMA((2 * count,))],
         9, "main", cost_estimate=cost(rows * cols, 14 * 8, channels, 10),
     )
-    for kernel, inputs, n in (
-        (inner_finish_kernel, [arrived, base, time_kernel], len(blocks(1, rows - 1))),
-        (edge_finish_kernel, [edge_arrived, base], 2),
-    ):
-        (decoded,) = call(
-            kernel, [*inputs, (ANY, decoded)], [(ANY, jax.ShapeDtypeStruct(features.shape, BF16))],
-            [room(inputs[0].shape[0]), pltpu.SemaphoreType.DMA((n,))],
-            3, "finish", input_output_aliases={len(inputs): 0},
-            cost_estimate=cost(inputs[0].shape[0] * cols, 1, channels, 4),
-        )
+    decoded_a, decoded = call(
+        functools.partial(inner_finish_kernel, count_f), [arrived[0], base, time_kernel, (ANY, decoded)],
+        [shape(parts[0]), (ANY, jax.ShapeDtypeStruct(features.shape, BF16))], [pltpu.SemaphoreType.DMA((1,))],
+        3, "inner_finish", input_output_aliases={3: 1}, cost_estimate=cost(parts[0] * cols, 1, channels, 4),
+    )
+    (decoded,) = call(
+        functools.partial(finish_kernel, count_f), [decoded_a, edge_arrived, base, (ANY, decoded)],
+        [(ANY, jax.ShapeDtypeStruct(features.shape, BF16))], [room(2), pltpu.SemaphoreType.DMA((3,))],
+        3, "finish", input_output_aliases={3: 0}, cost_estimate=cost(2 * cols, 1, channels, 4),
+    )
     return decoded
 
 

time: 27.4 us -> 27 us (0.985)
  waiting for transfers between devices: 4.55 us -> 2.23 us
  starting transfers between devices: 5.53 us -> 6.59 us
  Pallas kernels: 16.7 us -> 17.3 us
    ppermute x1 -> x2, waiting for transfers between devices: 3.58 us -> 1.64 us  [the longest x1 1.64 us: body(): arrived = [lax.ppermute(normed_ai[0], 'frame', onward[:-1])]]
    ppermute x1 -> x2, starting transfers between devices: 1.92 us -> 2.98 us  [the longest x1 1.91 us: body(): arrived = [lax.ppermute(normed_ai[0], 'frame', onward[:-1])]]
    ppermute x1, waiting for transfers between devices: 0.78 us -> 0.01 us  [body(): edge = [lax.ppermute(ends, 'frame', onward)]]
    pallas_call x10 -> x12, Pallas kernels: 16.7 us -> 17.3 us  [call(): pl.pallas_call(kernel, in_specs=list(specs), out_specs=list(out_specs), o...]
  transfers between devices with their start and end apart: 7 -> 8, of which waited for: 3 -> 4; matrix products, arithmetic and copies ran while one was open for 0% -> 0% of each run, Pallas kernels for 59% -> 63%
where the time goes in v5:
time: 27 us; the launch traced here: 26.5 us
  Pallas kernels  17.3 us (64%)
  starting transfers between devices  6.59 us (24%)
  waiting for transfers between devices  2.23 us (8%)
  between operations  0.35 us (1%)
    pallas_call x12, Pallas kernels, call(): pl.pallas_call(kernel, in_specs=list(specs), out_specs=list(out_specs), o...  17.3 us
    ppermute x1, starting transfers between devices, body(): arrived = [lax.ppermute(normed_ai[0], 'frame', onward[:-1])]  1.91 us
    ppermute x1, waiting for transfers between devices, body(): arrived = [lax.ppermute(normed_ai[0], 'frame', onward[:-1])]  1.64 us
    ppermute x1, starting transfers between devices, body(): got_0 = lax.ppermute(send_0, ('frame', 'band'), ring)  1.59 us
    ppermute x1, starting transfers between devices, body(): arrived += [lax.ppermute(part, 'frame', onward) for part in normed_ai[1:]]  1.07 us
    ppermute x1, starting transfers between devices, body(): edge = [lax.ppermute(ends, 'frame', onward)]  0.78 us
  transfers between devices with their start and end apart: 8, of which 4 were waited for; matrix products, arithmetic and copies ran while one was open for 0% of the time, Pallas kernels for 63%

profile of v5, /device:TPU:18, one launch (start us, length us, event | category | flops | bytes accessed | tf_op | source)
XLA Modules:
  0.0 26.5 jit_solution(3287197888681427464)
XLA Ops:
  0.0 0.8 %collective-permute-start = (bf16[3,128,256]{2,1,0:T(8,128)(2,1)S(1)}, bf16[3,128,256]{2,1,0:T(8,128)(2,1)S(1)}, u32[]{:S(2)}, u32[]{:S(2)}) collective-permute-start(bf16[3,128,256]{2,1,0:T(8,128)(2,1)S(1)} %ends.1._), channel_id=1, source_target_pairs={{0,4},{4,8},{8,12},{12,0},{1,5},{5,9},{9,13},{13,1},{2,6},{6,10},{... | collective-permute-start | bytes 589832 | tf_op jit(solution)/shard_map/ppermute | solution.py:426
  0.8 1.3 %load.1 = (bf16[3,128,256]{2,1,0:T(8,128)(2,1)S(1)}, bf16[13,128,256]{2,1,0:T(8,128)(2,1)S(1)}) custom-call(bf16[3,128,256]{2,1,0:T(8,128)(2,1)S(1)} %ends.1._, bf16[2,16,128,256]{3,2,1,0:T(8,128)(2,1)} %feats.5), custom_call_target="tpu_custom_call" | custom-call | tf_op jit(solution)/shard_map/load/pallas_call | solution.py:408
  2.1 0.1 collective-permute-start.1
  2.2 0.0 copy-start.1
  2.2 0.0 copy-start.2
  2.2 0.5 %collective-permute-start.3 = (bf16[13,128,256]{2,1,0:T(8,128)(2,1)S(1)}, bf16[13,128,256]{2,1,0:T(8,128)(2,1)S(1)}, u32[]{:S(2)}, u32[]{:S(2)}) collective-permute-start(bf16[13,128,256]{2,1,0:T(8,128)(2,1)S(1)} %get-tuple-element.28._.inners_b.refs_1_), channel_id=1, source_target_pairs={{0,4},{4,8},{8,12},{12,0},{1,5},{5,9},{9,13},{13,1},{2,6},{6,10},{... | collective-permute-start | bytes 2555912 | tf_op jit(solution)/shard_map/ppermute | solution.py:437
  2.7 1.7 %load_rest.1 = (bf16[16,128,256]{2,1,0:T(8,128)(2,1)S(1)}, bf16[3,3,256,256]{3,2,1,0:T(8,128)(2,1)S(1)}, bf16[3,256,256]{2,1,0:T(8,128)(2,1)S(1)}) custom-call(bf16[13,128,256]{2,1,0:T(8,128)(2,1)S(1)} %get-tuple-element.28._.inners_b.refs_1_, bf16[2,16,128,256]{3,2,1,0:T(8,128)(2,1)} %feats.5, bf16[3,3,256,256]{3,2,1,0:T(8,128)(2,1)} %kernel.1, ...), custom_call_target="tpu_custom_call" | custom-call | tf_op jit(solution)/shard_map/load_rest/pallas_call | solution.py:408
  4.4 0.0 copy-done
  4.4 0.0 copy-done.1
  4.4 0.0 copy-done.2
  4.4 1.0 %inner_a_ring.1 = (f32[4,128,256]{2,1,0:T(8,128)S(1)}, bf16[4,128,256]{2,1,0:T(8,128)(2,1)S(1)}) custom-call(bf16[16,128,256]{2,1,0:T(8,128)(2,1)S(1)} %get-tuple-element.29.raw_a.refs_0_._, bf16[16,128,256]{2,1,0:T(8,128)(2,1)S(1)} %get-tuple-element.29.raw_a.refs_0_._, bf16[3,3,256,256]{3,2,1,0:T(8,128)(2,1)S(1)} %get-tuple-element.32.refs_1_.kernel.refs_2_, ...), custom_call_target="tpu_custom_call" | custom-call | flops 603979776 | bytes 786432 | tf_op jit(solution)/shard_map/inner_a_ring/pallas_call | solution.py:408
  5.5 1.1 %collective-permute-start.6 = (bf16[4,128,256]{2,1,0:T(8,128)(2,1)S(1)}, bf16[4,128,256]{2,1,0:T(8,128)(2,1)S(1)}, u32[]{:S(2)}, u32[]{:S(2)}) collective-permute-start(bf16[4,128,256]{2,1,0:T(8,128)(2,1)S(1)} %get-tuple-element.45.refs_3_), channel_id=1, source_target_pairs={{0,4},{4,8},{8,12},{12,0},{1,5},{5,9},{9,13},{13,1},{2,6},{6,10},{... | collective-permute-start | bytes 786440 | tf_op jit(solution)/shard_map/ppermute | solution.py:456
  6.5 0.0 collective-permute-done.source
  6.6 0.0 collective-permute-done.1.refs_1_
  6.6 0.1 halo.1
  6.6 2.1 %inner_a.1 = (f32[10,128,256]{2,1,0:T(8,128)S(1)}, bf16[10,128,256]{2,1,0:T(8,128)(2,1)S(1)}) custom-call(bf16[3,128,256]{2,1,0:T(8,128)(2,1)S(1)} %get-tuple-element.31._, bf16[16,128,256]{2,1,0:T(8,128)(2,1)S(1)} %get-tuple-element.29.raw_a.refs_0_._, bf16[3,3,256,256]{3,2,1,0:T(8,128)(2,1)S(1)} %get-tuple-element.32.refs_1_.kernel.refs_2_, ...), custom_call_target="tpu_custom_call" | custom-call | flops 12079595520 | bytes 1966080 | tf_op jit(solution)/shard_map/inner_a/pallas_call | solution.py:408
  8.8 1.6 %collective-permute-start.4 = (bf16[3,128,256]{2,1,0:T(8,128)(2,1)S(1)}, bf16[3,128,256]{2,1,0:T(8,128)(2,1)S(1)}, u32[]{:S(2)}, u32[]{:S(2)}) collective-permute-start(bf16[3,128,256]{2,1,0:T(8,128)(2,1)S(1)} %get-tuple-element.31._), channel_id=1, source_target_pairs={{0,1},{1,2},{2,3},{3,7},{4,0},{5,4},{6,5},{7,6},{8,9},{9,10},{10,1... | collective-permute-start | bytes 589832 | tf_op jit(solution)/shard_map/ppermute | solution.py:453
  10.3 0.5 %collective-permute-start.5 = (bf16[3,128,256]{2,1,0:T(8,128)(2,1)S(1)}, bf16[3,128,256]{2,1,0:T(8,128)(2,1)S(1)}, u32[]{:S(2)}, u32[]{:S(2)}) collective-permute-start(bf16[3,128,256]{2,1,0:T(8,128)(2,1)S(1)} %get-tuple-element.35), channel_id=1, source_target_pairs={{1,0},{2,1},{3,2},{7,3},{0,4},{4,5},{5,6},{6,7},{9,8},{10,9},{11,1... | collective-permute-start | bytes 589832 | tf_op jit(solution)/shard_map/ppermute | solution.py:454
  10.8 1.9 %collective-permute-start.2 = (bf16[10,128,256]{2,1,0:T(8,128)(2,1)S(1)}, bf16[10,128,256]{2,1,0:T(8,128)(2,1)S(1)}, u32[]{:S(2)}, u32[]{:S(2)}) collective-permute-start(bf16[10,128,256]{2,1,0:T(8,128)(2,1)S(1)} %get-tuple-element.33._.refs_1_), channel_id=1, source_target_pairs={{0,4},{4,8},{8,12},{1,5},{5,9},{9,13},{2,6},{6,10},{10,14},{3,7},{... | collective-permute-start | bytes 1966088 | tf_op jit(solution)/shard_map/ppermute | solution.py:455
  12.7 2.9 %inner_b.1 = (f32[14,128,256]{2,1,0:T(8,128)S(1)}, bf16[14,128,256]{2,1,0:T(8,128)(2,1)S(1)}) custom-call(bf16[10,128,256]{2,1,0:T(8,128)(2,1)S(1)} %get-tuple-element.33._.refs_1_, bf16[3,128,256]{2,1,0:T(8,128)(2,1)S(1)} %get-tuple-element.30.edges_b.refs_0_, bf16[13,128,256]{2,1,0:T(8,128)(2,1)S(1)} %get-tuple-element.28._.inners_b.refs_1_, ...), custom_call_target="tpu_custom_call" | custom-call | flops 2113929216 | bytes 2752512 | tf_op jit(solution)/shard_map/inner_b/pallas_call | solution.py:408
  15.6 0.0 copy-start.3
  15.6 0.2 collective-permute-done.4.got_0
  15.8 0.2 collective-permute-done.5.got_1
  16.0 1.3 %edges.1 = (f32[2,128,256]{2,1,0:T(8,128)S(1)}, bf16[2,128,256]{2,1,0:T(8,128)(2,1)S(1)}, f32[2,128,256]{2,1,0:T(8,128)S(1)}, bf16[2,128,256]{2,1,0:T(8,128)(2,1)S(1)}, bf16[2,128,256]{2,1,0:T(8,128)(2,1)S(1)}) custom-call(bf16[16,128,256]{2,1,0:T(8,128)(2,1)S(1)} %get-tuple-element.29.raw_a.refs_0_._, ...), custom_call_target="tpu_custom_call" | custom-call | flops 603979776 | bytes 786432 | tf_op jit(solution)/shard_map/edges/pallas_call | solution.py:408
  17.3 0.2 collective-permute-start.7
  17.6 0.0 collective-permute-done.6.refs_4_
  17.6 0.0 collective-permute-done.3.inners
  17.6 5.0 %main.1 = (bf16[2,16,128,256]{3,2,1,0:T(8,128)(2,1)}, f32[16,128,256]{2,1,0:T(8,128)S(1)}) custom-call(bf16[3,128,256]{2,1,0:T(8,128)(2,1)S(1)} %get-tuple-element.34.edges, bf16[13,128,256]{2,1,0:T(8,128)(2,1)S(1)} %collective-permute-done.3.inners, bf16[3,128,256]{2,1,0:T(8,128)(2,1)S(1)} %collective-permute-done.4.got_0, ...), custom_call_target="tpu_custom_call" | custom-call | flops 30064771072 | bytes 10485760 | tf_op jit(solution)/shard_map/main/pallas_call | solution.py:408
  22.6 1.6 %collective-permute-done.2.arrived = bf16[10,128,256]{2,1,0:T(8,128)(2,1)S(1)} collective-permute-done((bf16[10,128,256]{2,1,0:T(8,128)(2,1)S(1)}, bf16[10,128,256]{2,1,0:T(8,128)(2,1)S(1)}, u32[]{:S(2)}, u32[]{:S(2)}) %collective-permute-start.2) | collective-permute-done | bytes 655392 | tf_op jit(solution)/shard_map/ppermute | solution.py:455
  24.2 1.2 %inner_finish.1 = (bf16[10,128,256]{2,1,0:T(8,128)(2,1)S(1)}, bf16[2,16,128,256]{3,2,1,0:T(8,128)(2,1)}) custom-call(bf16[10,128,256]{2,1,0:T(8,128)(2,1)S(1)} %collective-permute-done.2.arrived, f32[16,128,256]{2,1,0:T(8,128)S(1)} %get-tuple-element.46.base, ...), custom_call_target="tpu_custom_call", output_to_operand_aliasing={{1}: (3, {})} | custom-call | flops 167772160 | bytes 2621440 | tf_op jit(solution)/shard_map/inner_finish/pallas_call | solution.py:408
  25.4 0.2 collective-permute-done.7.products
  25.6 0.7 %finish.1 = bf16[2,16,128,256]{3,2,1,0:T(8,128)(2,1)} custom-call(bf16[10,128,256]{2,1,0:T(8,128)(2,1)S(1)} %get-tuple-element.48.decoded, bf16[2,128,256]{2,1,0:T(8,128)(2,1)S(1)} %collective-permute-done.7.products, f32[16,128,256]{2,1,0:T(8,128)S(1)} %get-tuple-element.46.base, ...), custom_call_target="tpu_custom_call", output_to_operand_aliasing={{}: (3, {})} | custom-call | flops 33554432 | bytes 524288 | tf_op jit(solution)/shard_map/finish/pallas_call | solution.py:408
  (4 shorter events, 0.0 us)
Async XLA Ops:
  0.0 6.5 %collective-permute-start = (bf16[3,128,256]{2,1,0:T(8,128)(2,1)S(1)}, bf16[3,128,256]{2,1,0:T(8,128)(2,1)S(1)}, u32[]{:S(2)}, u32[]{:S(2)}) collective-permute-start(bf16[3,128,256]{2,1,0:T(8,128)(2,1)S(1)} %ends.1._), channel_id=1, source_target_pairs={{0,4},{4,8},{8,12},{12,0},{1,5},{5,9},{9,13},{13,1},{2,6},{6,10},{... | collective-permute-start | bytes 589832 | tf_op jit(solution)/shard_map/ppermute | solution.py:426
  2.1 4.4 %collective-permute-start.1 = (bf16[3,128,256]{2,1,0:T(8,128)(2,1)S(1)}, bf16[3,128,256]{2,1,0:T(8,128)(2,1)S(1)}, u32[]{:S(2)}, u32[]{:S(2)}) collective-permute-start(bf16[3,128,256]{2,1,0:T(8,128)(2,1)S(1)} %get-tuple-element.30.edges_b.refs_0_), channel_id=1, source_target_pairs={{0,4},{4,0},{8,12},{12,8},{1,5},{5,1},{9,13},{13,9},{2,6},{6,2},{1... | collective-permute-start | bytes 589832 | tf_op jit(solution)/shard_map/ppermute | solution.py:439
  2.2 2.2 %copy-start = (f32[256]{0:T(256)S(1)}, f32[256]{0:T(256)}, u32[]{:S(2)}) copy-start(f32[256]{0:T(256)} %param.9) | copy-start | bytes 3076
  2.2 2.2 %copy-start.1 = (f32[256]{0:T(256)S(1)}, f32[256]{0:T(256)}, u32[]{:S(2)}) copy-start(f32[256]{0:T(256)} %param.10) | copy-start | bytes 3076
  2.2 2.2 %copy-start.2 = (f32[256]{0:T(256)S(1)}, f32[256]{0:T(256)}, u32[]{:S(2)}) copy-start(f32[256]{0:T(256)} %param.12) | copy-start | bytes 3076
  2.2 15.4 %collective-permute-start.3 = (bf16[13,128,256]{2,1,0:T(8,128)(2,1)S(1)}, bf16[13,128,256]{2,1,0:T(8,128)(2,1)S(1)}, u32[]{:S(2)}, u32[]{:S(2)}) collective-permute-start(bf16[13,128,256]{2,1,0:T(8,128)(2,1)S(1)} %get-tuple-element.28._.inners_b.refs_1_), channel_id=1, source_target_pairs={{0,4},{4,8},{8,12},{12,0},{1,5},{5,9},{9,13},{13,1},{2,6},{6,10},{... | collective-permute-start | bytes 2555912 | tf_op jit(solution)/shard_map/ppermute | solution.py:437
  5.5 12.1 %collective-permute-start.6 = (bf16[4,128,256]{2,1,0:T(8,128)(2,1)S(1)}, bf16[4,128,256]{2,1,0:T(8,128)(2,1)S(1)}, u32[]{:S(2)}, u32[]{:S(2)}) collective-permute-start(bf16[4,128,256]{2,1,0:T(8,128)(2,1)S(1)} %get-tuple-element.45.refs_3_), channel_id=1, source_target_pairs={{0,4},{4,8},{8,12},{12,0},{1,5},{5,9},{9,13},{13,1},{2,6},{6,10},{... | collective-permute-start | bytes 786440 | tf_op jit(solution)/shard_map/ppermute | solution.py:456
  8.8 7.1 %collective-permute-start.4 = (bf16[3,128,256]{2,1,0:T(8,128)(2,1)S(1)}, bf16[3,128,256]{2,1,0:T(8,128)(2,1)S(1)}, u32[]{:S(2)}, u32[]{:S(2)}) collective-permute-start(bf16[3,128,256]{2,1,0:T(8,128)(2,1)S(1)} %get-tuple-element.31._), channel_id=1, source_target_pairs={{0,1},{1,2},{2,3},{3,7},{4,0},{5,4},{6,5},{7,6},{8,9},{9,10},{10,1... | collective-permute-start | bytes 589832 | tf_op jit(solution)/shard_map/ppermute | solution.py:453
  10.3 5.7 %collective-permute-start.5 = (bf16[3,128,256]{2,1,0:T(8,128)(2,1)S(1)}, bf16[3,128,256]{2,1,0:T(8,128)(2,1)S(1)}, u32[]{:S(2)}, u32[]{:S(2)}) collective-permute-start(bf16[3,128,256]{2,1,0:T(8,128)(2,1)S(1)} %get-tuple-element.35), channel_id=1, source_target_pairs={{1,0},{2,1},{3,2},{7,3},{0,4},{4,5},{5,6},{6,7},{9,8},{10,9},{11,1... | collective-permute-start | bytes 589832 | tf_op jit(solution)/shard_map/ppermute | solution.py:454
  10.8 13.4 %collective-permute-start.2 = (bf16[10,128,256]{2,1,0:T(8,128)(2,1)S(1)}, bf16[10,128,256]{2,1,0:T(8,128)(2,1)S(1)}, u32[]{:S(2)}, u32[]{:S(2)}) collective-permute-start(bf16[10,128,256]{2,1,0:T(8,128)(2,1)S(1)} %get-tuple-element.33._.refs_1_), channel_id=1, source_target_pairs={{0,4},{4,8},{8,12},{1,5},{5,9},{9,13},{2,6},{6,10},{10,14},{3,7},{... | collective-permute-start | bytes 1966088 | tf_op jit(solution)/shard_map/ppermute | solution.py:455
  15.6 2.0 %copy-start.3 = (f32[256]{0:T(256)S(1)}, f32[256]{0:T(256)}, u32[]{:S(2)}) copy-start(f32[256]{0:T(256)} %param.13) | copy-start | bytes 3076
  17.3 8.3 %collective-permute-start.7 = (bf16[2,128,256]{2,1,0:T(8,128)(2,1)S(1)}, bf16[2,128,256]{2,1,0:T(8,128)(2,1)S(1)}, u32[]{:S(2)}, u32[]{:S(2)}) collective-permute-start(bf16[2,128,256]{2,1,0:T(8,128)(2,1)S(1)} %get-tuple-element.49), channel_id=1, source_target_pairs={{0,4},{4,8},{8,12},{12,0},{1,5},{5,9},{9,13},{13,1},{2,6},{6,10},{... | collective-permute-start | bytes 393224 | tf_op jit(solution)/shard_map/ppermute | solution.py:464

commit v6 on v5

--- a/solution.py
+++ b/solution.py
@@ -13,7 +13,7 @@
 ANY = pl.BlockSpec(memory_space=pl.ANY)
 HBM = pl.BlockSpec(memory_space=pltpu.HBM)
 STEP = 2
-RING_ROWS = 4
+RING_ROWS = 6
 
 
 def blocks(first, last):
@@ -269,10 +269,9 @@
     product_a[...] = product.astype(BF16).reshape(product_a.shape)
 
 
-def main_kernel(counts, ring_start, edges, inners, got_0, got_1, kernel, space_gain, space_bias, time_gain,
+def main_kernel(counts, edges, inners, got_0, got_1, kernel, space_gain, space_bias, time_gain,
                 time_kernel, time_bias, hidden_be, hidden_bi, normed_be, normed_bi, hidden_ae, normed_ae, *refs):
-    *refs, out_ref, base, shifted, sums, normed_p, decoded, decoded_ring, sems = refs
-    inner_a, arrived = (refs[:4], refs[4]) if len(refs) > 4 else (refs, None)
+    *inner_a, out_ref, base, shifted, sums, normed_p, decoded, sems = refs
     hidden_ai, normed_ai = inner_a[::2], inner_a[1::2]
     rows, cols, channels = base.shape
     keep = jnp.where(lax.axis_index("frame") > 0, 1.0, 0.0)
@@ -308,55 +307,44 @@
     run(spatial_jobs(get_row, blocks(0, rows), 1, shifted, sums, 0, kernel,
                      (space_gain, space_bias, time_gain), emit))
     copies = []
-
-    def write(frame, row, held, at):
-        copies.append(pltpu.make_async_copy(held.at[at], out_ref.at[frame, row], sems.at[len(copies)]))
+    for n, (first, count) in enumerate(blocks(0, rows)):
+        out_rows(first, count)
+        copies.append(pltpu.make_async_copy(
+            decoded.at[pl.ds(first, count)], out_ref.at[1, pl.ds(first, count)], sems.at[n]))
         copies[-1].start()
-
     for first, count in blocks(0, rows):
-        out_rows(first, count)
-        write(1, pl.ds(first, count), decoded, pl.ds(first, count))
-    ring_end = ring_start + (0 if arrived is None else arrived.shape[0])
-    lag_kernel = (time_kernel[2].astype(F32) * keep).astype(BF16)
-    for first, count in blocks(ring_start, ring_end):
-        at = pl.ds(first - ring_start, count)
-        total = base_rows(first, count)
-        total += jnp.dot(arrived[at].reshape(count * cols, channels), lag_kernel, preferred_element_type=F32)
-        decoded_ring[at] = total.astype(BF16).reshape(count, cols, channels)
-        write(0, pl.ds(first, count), decoded_ring, at)
-    for first, count in blocks(0, ring_start) + blocks(ring_end, rows):
         base[first : first + count] = base_rows(first, count).reshape(count, cols, channels)
     for copy in copies:
         copy.wait()
 
 
-def waits_at_end(count):
-    return jnp.logical_and(first_of_pair(count), lax.axis_index("frame") > 0)
-
-
-def inner_finish_kernel(frames, arrived, base, time_kernel, _, decoded, out_ref, sems):
+def inner_finish_kernel(base, time_kernel, *refs):
+    *arrived, _, decoded, out_ref, sems = refs
     cols, channels = base.shape[1:]
     keep = jnp.where(lax.axis_index("frame") > 0, 1.0, 0.0)
     kernel = (time_kernel[2].astype(F32) * keep).astype(BF16)
-    for row, count in blocks(1, arrived.shape[0] + 1):
-        at = pl.ds(row - 1, count)
-        total = base[row : row + count].reshape(count * cols, channels)
-        total += jnp.dot(arrived[at].reshape(count * cols, channels), kernel, preferred_element_type=F32)
-        decoded[at] = total.astype(BF16).reshape(count, cols, channels)
+    start = 1
+    for part in arrived:
+        for row, count in blocks(start, start + part.shape[0]):
+            normed = part[pl.ds(row - start, count)].reshape(count * cols, channels)
+            total = base[row : row + count].reshape(count * cols, channels)
+            total += jnp.dot(normed, kernel, preferred_element_type=F32)
+            decoded[pl.ds(row - 1, count)] = total.astype(BF16).reshape(count, cols, channels)
+        start += part.shape[0]
     copy = pltpu.make_async_copy(decoded, out_ref.at[0, pl.ds(1, decoded.shape[0])], sems.at[0])
 
-    @pl.when(waits_at_end(frames))
+    @pl.when(lax.axis_index("frame") > 0)
     def _():
         copy.start()
         copy.wait()
 
 
-def finish_kernel(frames, decoded, products, base, _, out_ref, edges, sems):
+def finish_kernel(decoded, products, base, _, out_ref, edges, sems):
     rows, count = base.shape[0], decoded.shape[0]
     keep = jnp.where(lax.axis_index("frame") > 0, 1.0, 0.0)
-    second = jnp.logical_not(waits_at_end(frames))
+    rest = lax.axis_index("frame") == 0
     inner = pltpu.make_async_copy(decoded, out_ref.at[0, pl.ds(1, count)], sems.at[2])
-    pl.when(second)(inner.start)
+    pl.when(rest)(inner.start)
     copies = []
     for n, row in enumerate((0, rows - 1)):
         edges[n] = (base[row] + products[n].astype(F32) * keep).astype(BF16)
@@ -364,7 +352,7 @@
         copies[-1].start()
     for copy in copies:
         copy.wait()
-    pl.when(second)(inner.wait)
+    pl.when(rest)(inner.wait)
 
 
 def cost(pixels, taps, channels, arrays):
@@ -438,7 +426,7 @@
     if count_f % 2 == 0:
         edge.append(lax.ppermute(edge_out, "frame", [(f, f ^ 1) for f in range(count_f)]))
 
-    ring_rows = min(RING_ROWS, (rows - 2) // STEP // 2 * STEP)
+    ring_rows = min(RING_ROWS, (rows - 2 - STEP) // STEP * STEP)
     parts = [rows - 2 - ring_rows] + [ring_rows] * (ring_rows > 0)
     inner_a = []
     if ring_rows:
@@ -454,7 +442,7 @@
     got_1 = lax.ppermute(send_1, ("frame", "band"), [(t, s) for s, t in ring])
     arrived = [lax.ppermute(normed_ai[0], "frame", onward[:-1])]
     arrived += [lax.ppermute(part, "frame", onward) for part in normed_ai[1:]]
-    hidden_bi, normed_bi = inner_rows([edge_out, inner_out], 1, rows - 2, 1, "inner_b", normed_ai[0])
+    hidden_bi, normed_bi = inner_rows([edge_out, inner_out], 1, rows - 2, 0, "inner_b", normed_ai[0])
     hidden_ae, normed_ae, hidden_be, normed_be, product_ae = call(
         functools.partial(edges_kernel, counts), [raw_a, edge_out, inner_out, got_0, got_1, space_kernel, *weights,
          time_kernel],
@@ -464,21 +452,21 @@
     edge_arrived = lax.ppermute(product_ae, "frame", onward)
 
     decoded, base = call(
-        functools.partial(main_kernel, counts, 1 + parts[0]),
+        functools.partial(main_kernel, counts),
         [edge, inner, got_0, got_1, space_kernel, *weights, time_kernel, time_bias,
-         hidden_be, hidden_bi, normed_be, normed_bi, hidden_ae, normed_ae, *inner_a, *arrived[1:]],
+         hidden_be, hidden_bi, normed_be, normed_bi, hidden_ae, normed_ae, *inner_a],
         [(ANY, jax.ShapeDtypeStruct(features.shape, BF16)), shape(rows, dtype=F32)],
-        [room(3, rows + 2), sums, room(rows), room(rows), room(max(ring_rows, 1)),
-         pltpu.SemaphoreType.DMA((2 * count,))],
+        [room(3, rows + 2), sums, room(rows), room(rows), pltpu.SemaphoreType.DMA((count,))],
         9, "main", cost_estimate=cost(rows * cols, 14 * 8, channels, 10),
     )
     decoded_a, decoded = call(
-        functools.partial(inner_finish_kernel, count_f), [arrived[0], base, time_kernel, (ANY, decoded)],
-        [shape(parts[0]), (ANY, jax.ShapeDtypeStruct(features.shape, BF16))], [pltpu.SemaphoreType.DMA((1,))],
-        3, "inner_finish", input_output_aliases={3: 1}, cost_estimate=cost(parts[0] * cols, 1, channels, 4),
+        inner_finish_kernel, [base, time_kernel, *arrived, (ANY, decoded)],
+        [shape(rows - 2), (ANY, jax.ShapeDtypeStruct(features.shape, BF16))], [pltpu.SemaphoreType.DMA((1,))],
+        3, "inner_finish", input_output_aliases={2 + len(arrived): 1},
+        cost_estimate=cost(rows * cols, 1, channels, 4),
     )
     (decoded,) = call(
-        functools.partial(finish_kernel, count_f), [decoded_a, edge_arrived, base, (ANY, decoded)],
+        finish_kernel, [decoded_a, edge_arrived, base, (ANY, decoded)],
         [(ANY, jax.ShapeDtypeStruct(features.shape, BF16))], [room(2), pltpu.SemaphoreType.DMA((3,))],
         3, "finish", input_output_aliases={3: 0}, cost_estimate=cost(2 * cols, 1, channels, 4),
     )

time: 27 us -> 26.8 us (level)
    ppermute x1, waiting for transfers between devices: 1.64 us -> 2.32 us  [body(): arrived = [lax.ppermute(normed_ai[0], 'frame', onward[:-1])]]
  transfers between devices with their start and end apart: 8 -> 8, of which waited for: 4 -> 1; matrix products, arithmetic and copies ran while one was open for 0% -> 0% of each run, Pallas kernels for 63% -> 62%
where the time goes in v6:
time: 26.8 us; the launch traced here: 26.5 us
  Pallas kernels  17.1 us (64%)
  starting transfers between devices  6.6 us (25%)
  waiting for transfers between devices  2.38 us (9%)
  between operations  0.36 us (1%)
    pallas_call x12, Pallas kernels, call(): pl.pallas_call(kernel, in_specs=list(specs), out_specs=list(out_specs), o...  17.1 us
    ppermute x1, waiting for transfers between devices, body(): arrived = [lax.ppermute(normed_ai[0], 'frame', onward[:-1])]  2.32 us
    ppermute x1, starting transfers between devices, body(): arrived = [lax.ppermute(normed_ai[0], 'frame', onward[:-1])]  1.92 us
    ppermute x1, starting transfers between devices, body(): got_0 = lax.ppermute(send_0, ('frame', 'band'), ring)  1.59 us
    ppermute x1, starting transfers between devices, body(): arrived += [lax.ppermute(part, 'frame', onward) for part in normed_ai[1:]]  1.07 us
    ppermute x1, starting transfers between devices, body(): edge = [lax.ppermute(ends, 'frame', onward)]  0.78 us
  transfers between devices with their start and end apart: 8, of which 1 were waited for; matrix products, arithmetic and copies ran while one was open for 0% of the time, Pallas kernels for 62%

profile of v6, /device:TPU:18, one launch (start us, length us, event | category | flops | bytes accessed | tf_op | source)
XLA Modules:
  0.0 26.5 jit_solution(4751107816167672894)
XLA Ops:
  0.0 0.8 %collective-permute-start = (bf16[3,128,256]{2,1,0:T(8,128)(2,1)S(1)}, bf16[3,128,256]{2,1,0:T(8,128)(2,1)S(1)}, u32[]{:S(2)}, u32[]{:S(2)}) collective-permute-start(bf16[3,128,256]{2,1,0:T(8,128)(2,1)S(1)} %ends.1._), channel_id=1, source_target_pairs={{0,4},{4,8},{8,12},{12,0},{1,5},{5,9},{9,13},{13,1},{2,6},{6,10},{... | collective-permute-start | bytes 589832 | tf_op jit(solution)/shard_map/ppermute | solution.py:414
  0.8 1.3 %load.1 = (bf16[3,128,256]{2,1,0:T(8,128)(2,1)S(1)}, bf16[13,128,256]{2,1,0:T(8,128)(2,1)S(1)}) custom-call(bf16[3,128,256]{2,1,0:T(8,128)(2,1)S(1)} %ends.1._, bf16[2,16,128,256]{3,2,1,0:T(8,128)(2,1)} %feats.5), custom_call_target="tpu_custom_call" | custom-call | tf_op jit(solution)/shard_map/load/pallas_call | solution.py:396
  2.1 0.1 collective-permute-start.1
  2.2 0.0 copy-start.1
  2.2 0.0 copy-start.2
  2.2 0.5 %collective-permute-start.2 = (bf16[13,128,256]{2,1,0:T(8,128)(2,1)S(1)}, bf16[13,128,256]{2,1,0:T(8,128)(2,1)S(1)}, u32[]{:S(2)}, u32[]{:S(2)}) collective-permute-start(bf16[13,128,256]{2,1,0:T(8,128)(2,1)S(1)} %get-tuple-element.28._.inners_b.refs_1_), channel_id=1, source_target_pairs={{0,4},{4,8},{8,12},{12,0},{1,5},{5,9},{9,13},{13,1},{2,6},{6,10},{... | collective-permute-start | bytes 2555912 | tf_op jit(solution)/shard_map/ppermute | solution.py:425
  2.7 1.7 %load_rest.1 = (bf16[16,128,256]{2,1,0:T(8,128)(2,1)S(1)}, bf16[3,3,256,256]{3,2,1,0:T(8,128)(2,1)S(1)}, bf16[3,256,256]{2,1,0:T(8,128)(2,1)S(1)}) custom-call(bf16[13,128,256]{2,1,0:T(8,128)(2,1)S(1)} %get-tuple-element.28._.inners_b.refs_1_, bf16[2,16,128,256]{3,2,1,0:T(8,128)(2,1)} %feats.5, bf16[3,3,256,256]{3,2,1,0:T(8,128)(2,1)} %kernel.1, ...), custom_call_target="tpu_custom_call" | custom-call | tf_op jit(solution)/shard_map/load_rest/pallas_call | solution.py:396
  4.4 0.0 copy-done
  4.4 0.0 copy-done.1
  4.4 0.0 copy-done.2
  4.4 1.4 %inner_a_ring.1 = (f32[6,128,256]{2,1,0:T(8,128)S(1)}, bf16[6,128,256]{2,1,0:T(8,128)(2,1)S(1)}) custom-call(bf16[16,128,256]{2,1,0:T(8,128)(2,1)S(1)} %get-tuple-element.29.raw_a.refs_0_._, bf16[16,128,256]{2,1,0:T(8,128)(2,1)S(1)} %get-tuple-element.29.raw_a.refs_0_._, bf16[3,3,256,256]{3,2,1,0:T(8,128)(2,1)S(1)} %get-tuple-element.34.kernel.refs_1_.refs_2_, ...), custom_call_target="tpu_custom_call" | custom-call | flops 905969664 | bytes 1179648 | tf_op jit(solution)/shard_map/inner_a_ring/pallas_call | solution.py:396
  5.8 1.1 %collective-permute-start.6 = (bf16[6,128,256]{2,1,0:T(8,128)(2,1)S(1)}, bf16[6,128,256]{2,1,0:T(8,128)(2,1)S(1)}, u32[]{:S(2)}, u32[]{:S(2)}) collective-permute-start(bf16[6,128,256]{2,1,0:T(8,128)(2,1)S(1)} %get-tuple-element.45.refs_3_), channel_id=1, source_target_pairs={{0,4},{4,8},{8,12},{12,0},{1,5},{5,9},{9,13},{13,1},{2,6},{6,10},{... | collective-permute-start | bytes 1179656 | tf_op jit(solution)/shard_map/ppermute | solution.py:444
  6.9 0.0 collective-permute-done.source
  6.9 0.0 collective-permute-done.1.refs_1_
  6.9 0.1 halo.1
  7.0 1.6 %collective-permute-start.3 = (bf16[3,128,256]{2,1,0:T(8,128)(2,1)S(1)}, bf16[3,128,256]{2,1,0:T(8,128)(2,1)S(1)}, u32[]{:S(2)}, u32[]{:S(2)}) collective-permute-start(bf16[3,128,256]{2,1,0:T(8,128)(2,1)S(1)} %get-tuple-element.32._), channel_id=1, source_target_pairs={{0,1},{1,2},{2,3},{3,7},{4,0},{5,4},{6,5},{7,6},{8,9},{9,10},{10,1... | collective-permute-start | bytes 589832 | tf_op jit(solution)/shard_map/ppermute | solution.py:441
  8.6 0.4 %collective-permute-start.4 = (bf16[3,128,256]{2,1,0:T(8,128)(2,1)S(1)}, bf16[3,128,256]{2,1,0:T(8,128)(2,1)S(1)}, u32[]{:S(2)}, u32[]{:S(2)}) collective-permute-start(bf16[3,128,256]{2,1,0:T(8,128)(2,1)S(1)} %get-tuple-element.33), channel_id=1, source_target_pairs={{1,0},{2,1},{3,2},{7,3},{0,4},{4,5},{5,6},{6,7},{9,8},{10,9},{11,1... | collective-permute-start | bytes 589832 | tf_op jit(solution)/shard_map/ppermute | solution.py:442
  9.0 1.7 %inner_a.1 = (f32[8,128,256]{2,1,0:T(8,128)S(1)}, bf16[8,128,256]{2,1,0:T(8,128)(2,1)S(1)}) custom-call(bf16[3,128,256]{2,1,0:T(8,128)(2,1)S(1)} %get-tuple-element.32._, bf16[16,128,256]{2,1,0:T(8,128)(2,1)S(1)} %get-tuple-element.29.raw_a.refs_0_._, bf16[3,3,256,256]{3,2,1,0:T(8,128)(2,1)S(1)} %get-tuple-element.34.kernel.refs_1_.refs_2_, ...), custom_call_target="tpu_custom_call" | custom-call | flops 9663676416 | bytes 1572864 | tf_op jit(solution)/shard_map/inner_a/pallas_call | solution.py:396
  10.8 2.9 %inner_b.1 = (f32[14,128,256]{2,1,0:T(8,128)S(1)}, bf16[14,128,256]{2,1,0:T(8,128)(2,1)S(1)}) custom-call(bf16[8,128,256]{2,1,0:T(8,128)(2,1)S(1)} %get-tuple-element.37._.refs_1_, bf16[3,128,256]{2,1,0:T(8,128)(2,1)S(1)} %get-tuple-element.30.edges_b.refs_0_, bf16[13,128,256]{2,1,0:T(8,128)(2,1)S(1)} %get-tuple-element.28._.inners_b.refs_1_, ...), custom_call_target="tpu_custom_call" | custom-call | bytes 2752512 | tf_op jit(solution)/shard_map/inner_b/pallas_call | solution.py:396
  13.7 0.0 copy-start.3
  13.7 1.9 %collective-permute-start.5 = (bf16[8,128,256]{2,1,0:T(8,128)(2,1)S(1)}, bf16[8,128,256]{2,1,0:T(8,128)(2,1)S(1)}, u32[]{:S(2)}, u32[]{:S(2)}) collective-permute-start(bf16[8,128,256]{2,1,0:T(8,128)(2,1)S(1)} %get-tuple-element.37._.refs_1_), channel_id=1, source_target_pairs={{0,4},{4,8},{8,12},{1,5},{5,9},{9,13},{2,6},{6,10},{10,14},{3,7},{... | collective-permute-start | bytes 1572872 | tf_op jit(solution)/shard_map/ppermute | solution.py:443
  15.6 0.0 collective-permute-done.3.got_0
  15.6 0.0 collective-permute-done.4.got_1
  15.6 1.3 %edges.1 = (f32[2,128,256]{2,1,0:T(8,128)S(1)}, bf16[2,128,256]{2,1,0:T(8,128)(2,1)S(1)}, f32[2,128,256]{2,1,0:T(8,128)S(1)}, bf16[2,128,256]{2,1,0:T(8,128)(2,1)S(1)}, bf16[2,128,256]{2,1,0:T(8,128)(2,1)S(1)}) custom-call(bf16[16,128,256]{2,1,0:T(8,128)(2,1)S(1)} %get-tuple-element.29.raw_a.refs_0_._, ...), custom_call_target="tpu_custom_call" | custom-call | flops 603979776 | bytes 786432 | tf_op jit(solution)/shard_map/edges/pallas_call | solution.py:396
  17.0 0.2 collective-permute-start.7
  17.2 0.0 collective-permute-done.2.inners
  17.2 4.7 %main.1 = (bf16[2,16,128,256]{3,2,1,0:T(8,128)(2,1)}, f32[16,128,256]{2,1,0:T(8,128)S(1)}) custom-call(bf16[3,128,256]{2,1,0:T(8,128)(2,1)S(1)} %get-tuple-element.31.edges, bf16[13,128,256]{2,1,0:T(8,128)(2,1)S(1)} %collective-permute-done.2.inners, bf16[3,128,256]{2,1,0:T(8,128)(2,1)S(1)} %collective-permute-done.3.got_0, ...), custom_call_target="tpu_custom_call" | custom-call | flops 30064771072 | bytes 10485760 | tf_op jit(solution)/shard_map/main/pallas_call | solution.py:396
  21.9 0.0 collective-permute-done.6.refs_1_
  21.9 2.3 %collective-permute-done.5.refs_0_ = bf16[8,128,256]{2,1,0:T(8,128)(2,1)S(1)} collective-permute-done((bf16[8,128,256]{2,1,0:T(8,128)(2,1)S(1)}, bf16[8,128,256]{2,1,0:T(8,128)(2,1)S(1)}, u32[]{:S(2)}, u32[]{:S(2)}) %collective-permute-start.5) | collective-permute-done | bytes 524320 | tf_op jit(solution)/shard_map/ppermute | solution.py:443
  24.2 1.3 %inner_finish.1 = (bf16[14,128,256]{2,1,0:T(8,128)(2,1)S(1)}, bf16[2,16,128,256]{3,2,1,0:T(8,128)(2,1)}) custom-call(f32[16,128,256]{2,1,0:T(8,128)S(1)} %get-tuple-element.46.base, bf16[3,256,256]{2,1,0:T(8,128)(2,1)S(1)} %get-tuple-element.35.time_kernel, bf16[8,128,256]{2,1,0:T(8,128)(2,1)S(1)} %collective-permute-done.5.refs_0_, ...), custom_call_target="tpu_custom_call", output_to_operand_aliasing={{1}: (4, {})} | custom-call | flops 268435456 | bytes 4194304 | tf_op jit(solution)/shard_map/inner_finish/pallas_call | solution.py:396
  25.6 0.0 collective-permute-done.7.products
  25.6 0.7 %finish.1 = bf16[2,16,128,256]{3,2,1,0:T(8,128)(2,1)} custom-call(bf16[14,128,256]{2,1,0:T(8,128)(2,1)S(1)} %get-tuple-element.48.decoded, bf16[2,128,256]{2,1,0:T(8,128)(2,1)S(1)} %collective-permute-done.7.products, f32[16,128,256]{2,1,0:T(8,128)S(1)} %get-tuple-element.46.base, ...), custom_call_target="tpu_custom_call", output_to_operand_aliasing={{}: (3, {})} | custom-call | flops 33554432 | bytes 524288 | tf_op jit(solution)/shard_map/finish/pallas_call | solution.py:396
  (4 shorter events, 0.0 us)
Async XLA Ops:
  0.0 6.8 %collective-permute-start = (bf16[3,128,256]{2,1,0:T(8,128)(2,1)S(1)}, bf16[3,128,256]{2,1,0:T(8,128)(2,1)S(1)}, u32[]{:S(2)}, u32[]{:S(2)}) collective-permute-start(bf16[3,128,256]{2,1,0:T(8,128)(2,1)S(1)} %ends.1._), channel_id=1, source_target_pairs={{0,4},{4,8},{8,12},{12,0},{1,5},{5,9},{9,13},{13,1},{2,6},{6,10},{... | collective-permute-start | bytes 589832 | tf_op jit(solution)/shard_map/ppermute | solution.py:414
  2.1 4.8 %collective-permute-start.1 = (bf16[3,128,256]{2,1,0:T(8,128)(2,1)S(1)}, bf16[3,128,256]{2,1,0:T(8,128)(2,1)S(1)}, u32[]{:S(2)}, u32[]{:S(2)}) collective-permute-start(bf16[3,128,256]{2,1,0:T(8,128)(2,1)S(1)} %get-tuple-element.30.edges_b.refs_0_), channel_id=1, source_target_pairs={{0,4},{4,0},{8,12},{12,8},{1,5},{5,1},{9,13},{13,9},{2,6},{6,2},{1... | collective-permute-start | bytes 589832 | tf_op jit(solution)/shard_map/ppermute | solution.py:427
  2.2 2.2 %copy-start = (f32[256]{0:T(256)S(1)}, f32[256]{0:T(256)}, u32[]{:S(2)}) copy-start(f32[256]{0:T(256)} %param.9) | copy-start | bytes 3076
  2.2 2.2 %copy-start.1 = (f32[256]{0:T(256)S(1)}, f32[256]{0:T(256)}, u32[]{:S(2)}) copy-start(f32[256]{0:T(256)} %param.10) | copy-start | bytes 3076
  2.2 2.2 %copy-start.2 = (f32[256]{0:T(256)S(1)}, f32[256]{0:T(256)}, u32[]{:S(2)}) copy-start(f32[256]{0:T(256)} %param.12) | copy-start | bytes 3076
  2.2 15.0 %collective-permute-start.2 = (bf16[13,128,256]{2,1,0:T(8,128)(2,1)S(1)}, bf16[13,128,256]{2,1,0:T(8,128)(2,1)S(1)}, u32[]{:S(2)}, u32[]{:S(2)}) collective-permute-start(bf16[13,128,256]{2,1,0:T(8,128)(2,1)S(1)} %get-tuple-element.28._.inners_b.refs_1_), channel_id=1, source_target_pairs={{0,4},{4,8},{8,12},{12,0},{1,5},{5,9},{9,13},{13,1},{2,6},{6,10},{... | collective-permute-start | bytes 2555912 | tf_op jit(solution)/shard_map/ppermute | solution.py:425
  5.8 16.1 %collective-permute-start.6 = (bf16[6,128,256]{2,1,0:T(8,128)(2,1)S(1)}, bf16[6,128,256]{2,1,0:T(8,128)(2,1)S(1)}, u32[]{:S(2)}, u32[]{:S(2)}) collective-permute-start(bf16[6,128,256]{2,1,0:T(8,128)(2,1)S(1)} %get-tuple-element.45.refs_3_), channel_id=1, source_target_pairs={{0,4},{4,8},{8,12},{12,0},{1,5},{5,9},{9,13},{13,1},{2,6},{6,10},{... | collective-permute-start | bytes 1179656 | tf_op jit(solution)/shard_map/ppermute | solution.py:444
  7.0 8.6 %collective-permute-start.3 = (bf16[3,128,256]{2,1,0:T(8,128)(2,1)S(1)}, bf16[3,128,256]{2,1,0:T(8,128)(2,1)S(1)}, u32[]{:S(2)}, u32[]{:S(2)}) collective-permute-start(bf16[3,128,256]{2,1,0:T(8,128)(2,1)S(1)} %get-tuple-element.32._), channel_id=1, source_target_pairs={{0,1},{1,2},{2,3},{3,7},{4,0},{5,4},{6,5},{7,6},{8,9},{9,10},{10,1... | collective-permute-start | bytes 589832 | tf_op jit(solution)/shard_map/ppermute | solution.py:441
  8.6 7.1 %collective-permute-start.4 = (bf16[3,128,256]{2,1,0:T(8,128)(2,1)S(1)}, bf16[3,128,256]{2,1,0:T(8,128)(2,1)S(1)}, u32[]{:S(2)}, u32[]{:S(2)}) collective-permute-start(bf16[3,128,256]{2,1,0:T(8,128)(2,1)S(1)} %get-tuple-element.33), channel_id=1, source_target_pairs={{1,0},{2,1},{3,2},{7,3},{0,4},{4,5},{5,6},{6,7},{9,8},{10,9},{11,1... | collective-permute-start | bytes 589832 | tf_op jit(solution)/shard_map/ppermute | solution.py:442
  13.7 3.6 %copy-start.3 = (f32[256]{0:T(256)S(1)}, f32[256]{0:T(256)}, u32[]{:S(2)}) copy-start(f32[256]{0:T(256)} %param.13) | copy-start | bytes 3076
  13.7 10.6 %collective-permute-start.5 = (bf16[8,128,256]{2,1,0:T(8,128)(2,1)S(1)}, bf16[8,128,256]{2,1,0:T(8,128)(2,1)S(1)}, u32[]{:S(2)}, u32[]{:S(2)}) collective-permute-start(bf16[8,128,256]{2,1,0:T(8,128)(2,1)S(1)} %get-tuple-element.37._.refs_1_), channel_id=1, source_target_pairs={{0,4},{4,8},{8,12},{1,5},{5,9},{9,13},{2,6},{6,10},{10,14},{3,7},{... | collective-permute-start | bytes 1572872 | tf_op jit(solution)/shard_map/ppermute | solution.py:443
  17.0 8.7 %collective-permute-start.7 = (bf16[2,128,256]{2,1,0:T(8,128)(2,1)S(1)}, bf16[2,128,256]{2,1,0:T(8,128)(2,1)S(1)}, u32[]{:S(2)}, u32[]{:S(2)}) collective-permute-start(bf16[2,128,256]{2,1,0:T(8,128)(2,1)S(1)} %get-tuple-element.49), channel_id=1, source_target_pairs={{0,4},{4,8},{8,12},{12,0},{1,5},{5,9},{9,13},{13,1},{2,6},{6,10},{... | collective-permute-start | bytes 393224 | tf_op jit(solution)/shard_map/ppermute | solution.py:452

commit v7 on v6

--- a/solution.py
+++ b/solution.py
@@ -442,7 +442,7 @@
     got_1 = lax.ppermute(send_1, ("frame", "band"), [(t, s) for s, t in ring])
     arrived = [lax.ppermute(normed_ai[0], "frame", onward[:-1])]
     arrived += [lax.ppermute(part, "frame", onward) for part in normed_ai[1:]]
-    hidden_bi, normed_bi = inner_rows([edge_out, inner_out], 1, rows - 2, 0, "inner_b", normed_ai[0])
+    hidden_bi, normed_bi = inner_rows([edge_out, inner_out], 1, rows - 2, 1, "inner_b", normed_ai[0])
     hidden_ae, normed_ae, hidden_be, normed_be, product_ae = call(
         functools.partial(edges_kernel, counts), [raw_a, edge_out, inner_out, got_0, got_1, space_kernel, *weights,
          time_kernel],

time: 26.8 us -> 26.8 us (level)
  no operation moved by 1% of the time
where the time goes in v7:
time: 26.8 us; the launch traced here: 26.5 us
  Pallas kernels  17.1 us (64%)
  starting transfers between devices  6.6 us (25%)
  waiting for transfers between devices  2.37 us (9%)
  between operations  0.36 us (1%)
    pallas_call x12, Pallas kernels, call(): pl.pallas_call(kernel, in_specs=list(specs), out_specs=list(out_specs), o...  17.1 us
    ppermute x1, waiting for transfers between devices, body(): arrived = [lax.ppermute(normed_ai[0], 'frame', onward[:-1])]  2.31 us
    ppermute x1, starting transfers between devices, body(): arrived = [lax.ppermute(normed_ai[0], 'frame', onward[:-1])]  1.92 us
    ppermute x1, starting transfers between devices, body(): got_0 = lax.ppermute(send_0, ('frame', 'band'), ring)  1.59 us
    ppermute x1, starting transfers between devices, body(): arrived += [lax.ppermute(part, 'frame', onward) for part in normed_ai[1:]]  1.07 us
    ppermute x1, starting transfers between devices, body(): edge = [lax.ppermute(ends, 'frame', onward)]  0.78 us
  transfers between devices with their start and end apart: 8, of which 1 were waited for; matrix products, arithmetic and copies ran while one was open for 0% of the time, Pallas kernels for 62%

profile of v7, /device:TPU:18, one launch (start us, length us, event | category | flops | bytes accessed | tf_op | source)
XLA Modules:
  0.0 26.5 jit_solution(11574888592556508930)
XLA Ops:
  0.0 0.8 %collective-permute-start = (bf16[3,128,256]{2,1,0:T(8,128)(2,1)S(1)}, bf16[3,128,256]{2,1,0:T(8,128)(2,1)S(1)}, u32[]{:S(2)}, u32[]{:S(2)}) collective-permute-start(bf16[3,128,256]{2,1,0:T(8,128)(2,1)S(1)} %ends.1._), channel_id=1, source_target_pairs={{0,4},{4,8},{8,12},{12,0},{1,5},{5,9},{9,13},{13,1},{2,6},{6,10},{... | collective-permute-start | bytes 589832 | tf_op jit(solution)/shard_map/ppermute | solution.py:414
  0.8 1.3 %load.1 = (bf16[3,128,256]{2,1,0:T(8,128)(2,1)S(1)}, bf16[13,128,256]{2,1,0:T(8,128)(2,1)S(1)}) custom-call(bf16[3,128,256]{2,1,0:T(8,128)(2,1)S(1)} %ends.1._, bf16[2,16,128,256]{3,2,1,0:T(8,128)(2,1)} %feats.5), custom_call_target="tpu_custom_call" | custom-call | tf_op jit(solution)/shard_map/load/pallas_call | solution.py:396
  2.1 0.1 collective-permute-start.1
  2.2 0.0 copy-start.1
  2.2 0.0 copy-start.2
  2.2 0.5 %collective-permute-start.2 = (bf16[13,128,256]{2,1,0:T(8,128)(2,1)S(1)}, bf16[13,128,256]{2,1,0:T(8,128)(2,1)S(1)}, u32[]{:S(2)}, u32[]{:S(2)}) collective-permute-start(bf16[13,128,256]{2,1,0:T(8,128)(2,1)S(1)} %get-tuple-element.28._.inners_b.refs_1_), channel_id=1, source_target_pairs={{0,4},{4,8},{8,12},{12,0},{1,5},{5,9},{9,13},{13,1},{2,6},{6,10},{... | collective-permute-start | bytes 2555912 | tf_op jit(solution)/shard_map/ppermute | solution.py:425
  2.7 1.7 %load_rest.1 = (bf16[16,128,256]{2,1,0:T(8,128)(2,1)S(1)}, bf16[3,3,256,256]{3,2,1,0:T(8,128)(2,1)S(1)}, bf16[3,256,256]{2,1,0:T(8,128)(2,1)S(1)}) custom-call(bf16[13,128,256]{2,1,0:T(8,128)(2,1)S(1)} %get-tuple-element.28._.inners_b.refs_1_, bf16[2,16,128,256]{3,2,1,0:T(8,128)(2,1)} %feats.5, bf16[3,3,256,256]{3,2,1,0:T(8,128)(2,1)} %kernel.1, ...), custom_call_target="tpu_custom_call" | custom-call | tf_op jit(solution)/shard_map/load_rest/pallas_call | solution.py:396
  4.4 0.0 copy-done
  4.4 0.0 copy-done.1
  4.4 1.4 %inner_a_ring.1 = (f32[6,128,256]{2,1,0:T(8,128)S(1)}, bf16[6,128,256]{2,1,0:T(8,128)(2,1)S(1)}) custom-call(bf16[16,128,256]{2,1,0:T(8,128)(2,1)S(1)} %get-tuple-element.29.raw_a.refs_0_._, bf16[16,128,256]{2,1,0:T(8,128)(2,1)S(1)} %get-tuple-element.29.raw_a.refs_0_._, bf16[3,3,256,256]{3,2,1,0:T(8,128)(2,1)S(1)} %get-tuple-element.34.kernel.refs_1_.refs_2_, ...), custom_call_target="tpu_custom_call" | custom-call | flops 905969664 | bytes 1179648 | tf_op jit(solution)/shard_map/inner_a_ring/pallas_call | solution.py:396
  5.8 1.1 %collective-permute-start.6 = (bf16[6,128,256]{2,1,0:T(8,128)(2,1)S(1)}, bf16[6,128,256]{2,1,0:T(8,128)(2,1)S(1)}, u32[]{:S(2)}, u32[]{:S(2)}) collective-permute-start(bf16[6,128,256]{2,1,0:T(8,128)(2,1)S(1)} %get-tuple-element.45.refs_3_), channel_id=1, source_target_pairs={{0,4},{4,8},{8,12},{12,0},{1,5},{5,9},{9,13},{13,1},{2,6},{6,10},{... | collective-permute-start | bytes 1179656 | tf_op jit(solution)/shard_map/ppermute | solution.py:444
  6.9 0.0 collective-permute-done.source
  6.9 0.0 collective-permute-done.1.refs_1_
  6.9 0.1 halo.1
  7.0 1.6 %collective-permute-start.3 = (bf16[3,128,256]{2,1,0:T(8,128)(2,1)S(1)}, bf16[3,128,256]{2,1,0:T(8,128)(2,1)S(1)}, u32[]{:S(2)}, u32[]{:S(2)}) collective-permute-start(bf16[3,128,256]{2,1,0:T(8,128)(2,1)S(1)} %get-tuple-element.32._), channel_id=1, source_target_pairs={{0,1},{1,2},{2,3},{3,7},{4,0},{5,4},{6,5},{7,6},{8,9},{9,10},{10,1... | collective-permute-start | bytes 589832 | tf_op jit(solution)/shard_map/ppermute | solution.py:441
  8.6 0.4 %collective-permute-start.4 = (bf16[3,128,256]{2,1,0:T(8,128)(2,1)S(1)}, bf16[3,128,256]{2,1,0:T(8,128)(2,1)S(1)}, u32[]{:S(2)}, u32[]{:S(2)}) collective-permute-start(bf16[3,128,256]{2,1,0:T(8,128)(2,1)S(1)} %get-tuple-element.33), channel_id=1, source_target_pairs={{1,0},{2,1},{3,2},{7,3},{0,4},{4,5},{5,6},{6,7},{9,8},{10,9},{11,1... | collective-permute-start | bytes 589832 | tf_op jit(solution)/shard_map/ppermute | solution.py:442
  9.0 1.7 %inner_a.1 = (f32[8,128,256]{2,1,0:T(8,128)S(1)}, bf16[8,128,256]{2,1,0:T(8,128)(2,1)S(1)}) custom-call(bf16[3,128,256]{2,1,0:T(8,128)(2,1)S(1)} %get-tuple-element.32._, bf16[16,128,256]{2,1,0:T(8,128)(2,1)S(1)} %get-tuple-element.29.raw_a.refs_0_._, bf16[3,3,256,256]{3,2,1,0:T(8,128)(2,1)S(1)} %get-tuple-element.34.kernel.refs_1_.refs_2_, ...), custom_call_target="tpu_custom_call" | custom-call | flops 9663676416 | bytes 1572864 | tf_op jit(solution)/shard_map/inner_a/pallas_call | solution.py:396
  10.8 1.9 %collective-permute-start.5 = (bf16[8,128,256]{2,1,0:T(8,128)(2,1)S(1)}, bf16[8,128,256]{2,1,0:T(8,128)(2,1)S(1)}, u32[]{:S(2)}, u32[]{:S(2)}) collective-permute-start(bf16[8,128,256]{2,1,0:T(8,128)(2,1)S(1)} %get-tuple-element.37._.refs_1_), channel_id=1, source_target_pairs={{0,4},{4,8},{8,12},{1,5},{5,9},{9,13},{2,6},{6,10},{10,14},{3,7},{... | collective-permute-start | bytes 1572872 | tf_op jit(solution)/shard_map/ppermute | solution.py:443
  12.7 2.9 %inner_b.1 = (f32[14,128,256]{2,1,0:T(8,128)S(1)}, bf16[14,128,256]{2,1,0:T(8,128)(2,1)S(1)}) custom-call(bf16[8,128,256]{2,1,0:T(8,128)(2,1)S(1)} %get-tuple-element.37._.refs_1_, bf16[3,128,256]{2,1,0:T(8,128)(2,1)S(1)} %get-tuple-element.30.edges_b.refs_0_, bf16[13,128,256]{2,1,0:T(8,128)(2,1)S(1)} %get-tuple-element.28._.inners_b.refs_1_, ...), custom_call_target="tpu_custom_call" | custom-call | flops 2113929216 | bytes 2752512 | tf_op jit(solution)/shard_map/inner_b/pallas_call | solution.py:396
  15.6 0.0 copy-start.3
  15.6 0.0 collective-permute-done.3.got_0
  15.6 0.0 collective-permute-done.4.got_1
  15.6 1.3 %edges.1 = (f32[2,128,256]{2,1,0:T(8,128)S(1)}, bf16[2,128,256]{2,1,0:T(8,128)(2,1)S(1)}, f32[2,128,256]{2,1,0:T(8,128)S(1)}, bf16[2,128,256]{2,1,0:T(8,128)(2,1)S(1)}, bf16[2,128,256]{2,1,0:T(8,128)(2,1)S(1)}) custom-call(bf16[16,128,256]{2,1,0:T(8,128)(2,1)S(1)} %get-tuple-element.29.raw_a.refs_0_._, ...), custom_call_target="tpu_custom_call" | custom-call | flops 603979776 | bytes 786432 | tf_op jit(solution)/shard_map/edges/pallas_call | solution.py:396
  17.0 0.2 collective-permute-start.7
  17.2 0.0 collective-permute-done.2.inners
  17.2 0.0 copy-done.3
  17.2 4.7 %main.1 = (bf16[2,16,128,256]{3,2,1,0:T(8,128)(2,1)}, f32[16,128,256]{2,1,0:T(8,128)S(1)}) custom-call(bf16[3,128,256]{2,1,0:T(8,128)(2,1)S(1)} %get-tuple-element.31.edges, bf16[13,128,256]{2,1,0:T(8,128)(2,1)S(1)} %collective-permute-done.2.inners, bf16[3,128,256]{2,1,0:T(8,128)(2,1)S(1)} %collective-permute-done.3.got_0, ...), custom_call_target="tpu_custom_call" | custom-call | flops 30064771072 | bytes 10485760 | tf_op jit(solution)/shard_map/main/pallas_call | solution.py:396
  21.9 0.0 collective-permute-done.6.refs_1_
  21.9 2.3 %collective-permute-done.5.refs_0_ = bf16[8,128,256]{2,1,0:T(8,128)(2,1)S(1)} collective-permute-done((bf16[8,128,256]{2,1,0:T(8,128)(2,1)S(1)}, bf16[8,128,256]{2,1,0:T(8,128)(2,1)S(1)}, u32[]{:S(2)}, u32[]{:S(2)}) %collective-permute-start.5) | collective-permute-done | bytes 524320 | tf_op jit(solution)/shard_map/ppermute | solution.py:443
  24.2 1.3 %inner_finish.1 = (bf16[14,128,256]{2,1,0:T(8,128)(2,1)S(1)}, bf16[2,16,128,256]{3,2,1,0:T(8,128)(2,1)}) custom-call(f32[16,128,256]{2,1,0:T(8,128)S(1)} %get-tuple-element.46.base, bf16[3,256,256]{2,1,0:T(8,128)(2,1)S(1)} %get-tuple-element.35.time_kernel, bf16[8,128,256]{2,1,0:T(8,128)(2,1)S(1)} %collective-permute-done.5.refs_0_, ...), custom_call_target="tpu_custom_call", output_to_operand_aliasing={{1}: (4, {})} | custom-call | flops 268435456 | bytes 4194304 | tf_op jit(solution)/shard_map/inner_finish/pallas_call | solution.py:396
  25.6 0.0 collective-permute-done.7.products
  25.6 0.7 %finish.1 = bf16[2,16,128,256]{3,2,1,0:T(8,128)(2,1)} custom-call(bf16[14,128,256]{2,1,0:T(8,128)(2,1)S(1)} %get-tuple-element.48.decoded, bf16[2,128,256]{2,1,0:T(8,128)(2,1)S(1)} %collective-permute-done.7.products, f32[16,128,256]{2,1,0:T(8,128)S(1)} %get-tuple-element.46.base, ...), custom_call_target="tpu_custom_call", output_to_operand_aliasing={{}: (3, {})} | custom-call | flops 33554432 | bytes 524288 | tf_op jit(solution)/shard_map/finish/pallas_call | solution.py:396
  (4 shorter events, 0.0 us)
Async XLA Ops:
  0.0 6.8 %collective-permute-start = (bf16[3,128,256]{2,1,0:T(8,128)(2,1)S(1)}, bf16[3,128,256]{2,1,0:T(8,128)(2,1)S(1)}, u32[]{:S(2)}, u32[]{:S(2)}) collective-permute-start(bf16[3,128,256]{2,1,0:T(8,128)(2,1)S(1)} %ends.1._), channel_id=1, source_target_pairs={{0,4},{4,8},{8,12},{12,0},{1,5},{5,9},{9,13},{13,1},{2,6},{6,10},{... | collective-permute-start | bytes 589832 | tf_op jit(solution)/shard_map/ppermute | solution.py:414
  2.1 4.8 %collective-permute-start.1 = (bf16[3,128,256]{2,1,0:T(8,128)(2,1)S(1)}, bf16[3,128,256]{2,1,0:T(8,128)(2,1)S(1)}, u32[]{:S(2)}, u32[]{:S(2)}) collective-permute-start(bf16[3,128,256]{2,1,0:T(8,128)(2,1)S(1)} %get-tuple-element.30.edges_b.refs_0_), channel_id=1, source_target_pairs={{0,4},{4,0},{8,12},{12,8},{1,5},{5,1},{9,13},{13,9},{2,6},{6,2},{1... | collective-permute-start | bytes 589832 | tf_op jit(solution)/shard_map/ppermute | solution.py:427
  2.2 2.2 %copy-start = (f32[256]{0:T(256)S(1)}, f32[256]{0:T(256)}, u32[]{:S(2)}) copy-start(f32[256]{0:T(256)} %param.9) | copy-start | bytes 3076
  2.2 2.2 %copy-start.1 = (f32[256]{0:T(256)S(1)}, f32[256]{0:T(256)}, u32[]{:S(2)}) copy-start(f32[256]{0:T(256)} %param.10) | copy-start | bytes 3076
  2.2 2.2 %copy-start.2 = (f32[256]{0:T(256)S(1)}, f32[256]{0:T(256)}, u32[]{:S(2)}) copy-start(f32[256]{0:T(256)} %param.12) | copy-start | bytes 3076
  2.2 15.0 %collective-permute-start.2 = (bf16[13,128,256]{2,1,0:T(8,128)(2,1)S(1)}, bf16[13,128,256]{2,1,0:T(8,128)(2,1)S(1)}, u32[]{:S(2)}, u32[]{:S(2)}) collective-permute-start(bf16[13,128,256]{2,1,0:T(8,128)(2,1)S(1)} %get-tuple-element.28._.inners_b.refs_1_), channel_id=1, source_target_pairs={{0,4},{4,8},{8,12},{12,0},{1,5},{5,9},{9,13},{13,1},{2,6},{6,10},{... | collective-permute-start | bytes 2555912 | tf_op jit(solution)/shard_map/ppermute | solution.py:425
  5.8 16.1 %collective-permute-start.6 = (bf16[6,128,256]{2,1,0:T(8,128)(2,1)S(1)}, bf16[6,128,256]{2,1,0:T(8,128)(2,1)S(1)}, u32[]{:S(2)}, u32[]{:S(2)}) collective-permute-start(bf16[6,128,256]{2,1,0:T(8,128)(2,1)S(1)} %get-tuple-element.45.refs_3_), channel_id=1, source_target_pairs={{0,4},{4,8},{8,12},{12,0},{1,5},{5,9},{9,13},{13,1},{2,6},{6,10},{... | collective-permute-start | bytes 1179656 | tf_op jit(solution)/shard_map/ppermute | solution.py:444
  7.0 8.6 %collective-permute-start.3 = (bf16[3,128,256]{2,1,0:T(8,128)(2,1)S(1)}, bf16[3,128,256]{2,1,0:T(8,128)(2,1)S(1)}, u32[]{:S(2)}, u32[]{:S(2)}) collective-permute-start(bf16[3,128,256]{2,1,0:T(8,128)(2,1)S(1)} %get-tuple-element.32._), channel_id=1, source_target_pairs={{0,1},{1,2},{2,3},{3,7},{4,0},{5,4},{6,5},{7,6},{8,9},{9,10},{10,1... | collective-permute-start | bytes 589832 | tf_op jit(solution)/shard_map/ppermute | solution.py:441
  8.6 7.1 %collective-permute-start.4 = (bf16[3,128,256]{2,1,0:T(8,128)(2,1)S(1)}, bf16[3,128,256]{2,1,0:T(8,128)(2,1)S(1)}, u32[]{:S(2)}, u32[]{:S(2)}) collective-permute-start(bf16[3,128,256]{2,1,0:T(8,128)(2,1)S(1)} %get-tuple-element.33), channel_id=1, source_target_pairs={{1,0},{2,1},{3,2},{7,3},{0,4},{4,5},{5,6},{6,7},{9,8},{10,9},{11,1... | collective-permute-start | bytes 589832 | tf_op jit(solution)/shard_map/ppermute | solution.py:442
  10.8 13.5 %collective-permute-start.5 = (bf16[8,128,256]{2,1,0:T(8,128)(2,1)S(1)}, bf16[8,128,256]{2,1,0:T(8,128)(2,1)S(1)}, u32[]{:S(2)}, u32[]{:S(2)}) collective-permute-start(bf16[8,128,256]{2,1,0:T(8,128)(2,1)S(1)} %get-tuple-element.37._.refs_1_), channel_id=1, source_target_pairs={{0,4},{4,8},{8,12},{1,5},{5,9},{9,13},{2,6},{6,10},{10,14},{3,7},{... | collective-permute-start | bytes 1572872 | tf_op jit(solution)/shard_map/ppermute | solution.py:443
  15.6 1.6 %copy-start.3 = (f32[256]{0:T(256)S(1)}, f32[256]{0:T(256)}, u32[]{:S(2)}) copy-start(f32[256]{0:T(256)} %param.13) | copy-start | bytes 3076
  17.0 8.7 %collective-permute-start.7 = (bf16[2,128,256]{2,1,0:T(8,128)(2,1)S(1)}, bf16[2,128,256]{2,1,0:T(8,128)(2,1)S(1)}, u32[]{:S(2)}, u32[]{:S(2)}) collective-permute-start(bf16[2,128,256]{2,1,0:T(8,128)(2,1)S(1)} %get-tuple-element.49), channel_id=1, source_target_pairs={{0,4},{4,8},{8,12},{12,0},{1,5},{5,9},{9,13},{13,1},{2,6},{6,10},{... | collective-permute-start | bytes 393224 | tf_op jit(solution)/shard_map/ppermute | solution.py:452

commit v8 on v7

--- a/solution.py
+++ b/solution.py
@@ -318,8 +318,25 @@
         copy.wait()
 
 
-def inner_finish_kernel(base, time_kernel, *refs):
-    *arrived, _, decoded, out_ref, sems = refs
+def ends_late(count):
+    index = lax.axis_index("frame")
+    return jnp.logical_and(lax.rem(index, 2) == 0, index > 0) if count % 2 == 0 else index >= 0
+
+
+def write_edges(products, base, out_ref, edges, sems):
+    rows = base.shape[0]
+    keep = jnp.where(lax.axis_index("frame") > 0, 1.0, 0.0)
+    copies = []
+    for n, row in enumerate((0, rows - 1)):
+        edges[n] = (base[row] + products[n].astype(F32) * keep).astype(BF16)
+        copies.append(pltpu.make_async_copy(edges.at[pl.ds(n, 1)], out_ref.at[0, pl.ds(row, 1)], sems.at[n]))
+        copies[-1].start()
+    for copy in copies:
+        copy.wait()
+
+
+def inner_finish_kernel(frames, base, time_kernel, products, *refs):
+    *arrived, _, out_ref, decoded, edges, sems = refs
     cols, channels = base.shape[1:]
     keep = jnp.where(lax.axis_index("frame") > 0, 1.0, 0.0)
     kernel = (time_kernel[2].astype(F32) * keep).astype(BF16)
@@ -331,28 +348,14 @@
             total += jnp.dot(normed, kernel, preferred_element_type=F32)
             decoded[pl.ds(row - 1, count)] = total.astype(BF16).reshape(count, cols, channels)
         start += part.shape[0]
-    copy = pltpu.make_async_copy(decoded, out_ref.at[0, pl.ds(1, decoded.shape[0])], sems.at[0])
-
-    @pl.when(lax.axis_index("frame") > 0)
-    def _():
-        copy.start()
-        copy.wait()
-
-
-def finish_kernel(decoded, products, base, _, out_ref, edges, sems):
-    rows, count = base.shape[0], decoded.shape[0]
-    keep = jnp.where(lax.axis_index("frame") > 0, 1.0, 0.0)
-    rest = lax.axis_index("frame") == 0
-    inner = pltpu.make_async_copy(decoded, out_ref.at[0, pl.ds(1, count)], sems.at[2])
-    pl.when(rest)(inner.start)
-    copies = []
-    for n, row in enumerate((0, rows - 1)):
-        edges[n] = (base[row] + products[n].astype(F32) * keep).astype(BF16)
-        copies.append(pltpu.make_async_copy(edges.at[pl.ds(n, 1)], out_ref.at[0, pl.ds(row, 1)], sems.at[n]))
-        copies[-1].start()
-    for copy in copies:
-        copy.wait()
-    pl.when(rest)(inner.wait)
+    copy = pltpu.make_async_copy(decoded, out_ref.at[0, pl.ds(1, decoded.shape[0])], sems.at[2])
+    copy.start()
+    pl.when(jnp.logical_not(ends_late(frames)))(lambda: write_edges(products, base, out_ref, edges, sems))
+    copy.wait()
+
+
+def finish_kernel(frames, products, base, _, out_ref, edges, sems):
+    pl.when(ends_late(frames))(lambda: write_edges(products, base, out_ref, edges, sems))
 
 
 def cost(pixels, taps, channels, arrays):
@@ -450,6 +453,9 @@
         4, "edges", cost_estimate=cost(4 * cols, 9, channels, 3),
     )
     edge_arrived = lax.ppermute(product_ae, "frame", onward)
+    edge_swapped = edge_arrived
+    if count_f % 2 == 0:
+        edge_swapped = lax.ppermute(product_ae, "frame", [(f, f ^ 1) for f in range(count_f)])
 
     decoded, base = call(
         functools.partial(main_kernel, counts),
@@ -459,16 +465,18 @@
         [room(3, rows + 2), sums, room(rows), room(rows), pltpu.SemaphoreType.DMA((count,))],
         9, "main", cost_estimate=cost(rows * cols, 14 * 8, channels, 10),
     )
-    decoded_a, decoded = call(
-        inner_finish_kernel, [base, time_kernel, *arrived, (ANY, decoded)],
-        [shape(rows - 2), (ANY, jax.ShapeDtypeStruct(features.shape, BF16))], [pltpu.SemaphoreType.DMA((1,))],
-        3, "inner_finish", input_output_aliases={2 + len(arrived): 1},
+    out = (ANY, jax.ShapeDtypeStruct(features.shape, BF16))
+    (decoded,) = call(
+        functools.partial(inner_finish_kernel, count_f),
+        [base, time_kernel, edge_swapped, *arrived, (ANY, decoded)], [out],
+        [room(rows - 2), room(2), pltpu.SemaphoreType.DMA((3,))],
+        3, "inner_finish", input_output_aliases={3 + len(arrived): 0},
         cost_estimate=cost(rows * cols, 1, channels, 4),
     )
     (decoded,) = call(
-        finish_kernel, [decoded_a, edge_arrived, base, (ANY, decoded)],
-        [(ANY, jax.ShapeDtypeStruct(features.shape, BF16))], [room(2), pltpu.SemaphoreType.DMA((3,))],
-        3, "finish", input_output_aliases={3: 0}, cost_estimate=cost(2 * cols, 1, channels, 4),
+        functools.partial(finish_kernel, count_f), [edge_arrived, base, (ANY, decoded)], [out],
+        [room(2), pltpu.SemaphoreType.DMA((2,))],
+        3, "finish", input_output_aliases={2: 0}, cost_estimate=cost(2 * cols, 1, channels, 4),
     )
     return decoded
 

time: 26.8 us -> 26.7 us (level)
  starting transfers between devices: 6.6 us -> 6.93 us
  waiting for transfers between devices: 2.37 us -> 2.04 us
    ppermute x1, waiting for transfers between devices: 2.31 us -> 2 us  [body(): arrived = [lax.ppermute(normed_ai[0], 'frame', onward[:-1])]]
  transfers between devices with their start and end apart: 8 -> 9, of which waited for: 1 -> 1; matrix products, arithmetic and copies ran while one was open for 0% -> 0% of each run, Pallas kernels for 62% -> 62%
where the time goes in v8:
time: 26.7 us; the launch traced here: 26.5 us
  Pallas kernels  17.1 us (64%)
  starting transfers between devices  6.93 us (26%)
  waiting for transfers between devices  2.04 us (8%)
  between operations  0.35 us (1%)
    pallas_call x12, Pallas kernels, call(): pl.pallas_call(kernel, in_specs=list(specs), out_specs=list(out_specs), o...  17.1 us
    ppermute x1, waiting for transfers between devices, body(): arrived = [lax.ppermute(normed_ai[0], 'frame', onward[:-1])]  2 us
    ppermute x1, starting transfers between devices, body(): arrived = [lax.ppermute(normed_ai[0], 'frame', onward[:-1])]  1.92 us
    ppermute x1, starting transfers between devices, body(): got_0 = lax.ppermute(send_0, ('frame', 'band'), ring)  1.59 us
    ppermute x1, starting transfers between devices, body(): arrived += [lax.ppermute(part, 'frame', onward) for part in normed_ai[1:]]  1.07 us
    ppermute x1, starting transfers between devices, body(): edge = [lax.ppermute(ends, 'frame', onward)]  0.78 us
  transfers between devices with their start and end apart: 9, of which 1 were waited for; matrix products, arithmetic and copies ran while one was open for 0% of the time, Pallas kernels for 62%

profile of v8, /device:TPU:18, one launch (start us, length us, event | category | flops | bytes accessed | tf_op | source)
XLA Modules:
  0.0 26.5 jit_solution(1847808635872237754)
XLA Ops:
  0.0 0.8 %collective-permute-start = (bf16[3,128,256]{2,1,0:T(8,128)(2,1)S(1)}, bf16[3,128,256]{2,1,0:T(8,128)(2,1)S(1)}, u32[]{:S(2)}, u32[]{:S(2)}) collective-permute-start(bf16[3,128,256]{2,1,0:T(8,128)(2,1)S(1)} %ends.1._), channel_id=1, source_target_pairs={{0,4},{4,8},{8,12},{12,0},{1,5},{5,9},{9,13},{13,1},{2,6},{6,10},{... | collective-permute-start | bytes 589832 | tf_op jit(solution)/shard_map/ppermute | solution.py:417
  0.8 1.3 %load.1 = (bf16[3,128,256]{2,1,0:T(8,128)(2,1)S(1)}, bf16[13,128,256]{2,1,0:T(8,128)(2,1)S(1)}) custom-call(bf16[3,128,256]{2,1,0:T(8,128)(2,1)S(1)} %ends.1._, bf16[2,16,128,256]{3,2,1,0:T(8,128)(2,1)} %feats.5), custom_call_target="tpu_custom_call" | custom-call | tf_op jit(solution)/shard_map/load/pallas_call | solution.py:399
  2.1 0.1 collective-permute-start.1
  2.2 0.0 copy-start.1
  2.2 0.0 copy-start.2
  2.2 0.5 %collective-permute-start.5 = (bf16[13,128,256]{2,1,0:T(8,128)(2,1)S(1)}, bf16[13,128,256]{2,1,0:T(8,128)(2,1)S(1)}, u32[]{:S(2)}, u32[]{:S(2)}) collective-permute-start(bf16[13,128,256]{2,1,0:T(8,128)(2,1)S(1)} %get-tuple-element.26._.inners_b.refs_1_), channel_id=1, source_target_pairs={{0,4},{4,8},{8,12},{12,0},{1,5},{5,9},{9,13},{13,1},{2,6},{6,10},{... | collective-permute-start | bytes 2555912 | tf_op jit(solution)/shard_map/ppermute | solution.py:428
  2.7 1.7 %load_rest.1 = (bf16[16,128,256]{2,1,0:T(8,128)(2,1)S(1)}, bf16[3,3,256,256]{3,2,1,0:T(8,128)(2,1)S(1)}, bf16[3,256,256]{2,1,0:T(8,128)(2,1)S(1)}) custom-call(bf16[13,128,256]{2,1,0:T(8,128)(2,1)S(1)} %get-tuple-element.26._.inners_b.refs_1_, bf16[2,16,128,256]{3,2,1,0:T(8,128)(2,1)} %feats.5, bf16[3,3,256,256]{3,2,1,0:T(8,128)(2,1)} %kernel.1, ...), custom_call_target="tpu_custom_call" | custom-call | tf_op jit(solution)/shard_map/load_rest/pallas_call | solution.py:399
  4.4 0.0 copy-done
  4.4 1.4 %inner_a_ring.1 = (f32[6,128,256]{2,1,0:T(8,128)S(1)}, bf16[6,128,256]{2,1,0:T(8,128)(2,1)S(1)}) custom-call(bf16[16,128,256]{2,1,0:T(8,128)(2,1)S(1)} %get-tuple-element.27.raw_a.refs_0_._, bf16[16,128,256]{2,1,0:T(8,128)(2,1)S(1)} %get-tuple-element.27.raw_a.refs_0_._, bf16[3,3,256,256]{3,2,1,0:T(8,128)(2,1)S(1)} %get-tuple-element.31.kernel.refs_1_.refs_2_, ...), custom_call_target="tpu_custom_call" | custom-call | flops 905969664 | bytes 1179648 | tf_op jit(solution)/shard_map/inner_a_ring/pallas_call | solution.py:399
  5.8 1.1 %collective-permute-start.8 = (bf16[6,128,256]{2,1,0:T(8,128)(2,1)S(1)}, bf16[6,128,256]{2,1,0:T(8,128)(2,1)S(1)}, u32[]{:S(2)}, u32[]{:S(2)}) collective-permute-start(bf16[6,128,256]{2,1,0:T(8,128)(2,1)S(1)} %get-tuple-element.44.refs_3_), channel_id=1, source_target_pairs={{0,4},{4,8},{8,12},{12,0},{1,5},{5,9},{9,13},{13,1},{2,6},{6,10},{... | collective-permute-start | bytes 1179656 | tf_op jit(solution)/shard_map/ppermute | solution.py:447
  6.9 0.0 collective-permute-done.source
  6.9 0.0 collective-permute-done.1.refs_1_
  6.9 0.1 halo.1
  7.0 1.6 %collective-permute-start.2 = (bf16[3,128,256]{2,1,0:T(8,128)(2,1)S(1)}, bf16[3,128,256]{2,1,0:T(8,128)(2,1)S(1)}, u32[]{:S(2)}, u32[]{:S(2)}) collective-permute-start(bf16[3,128,256]{2,1,0:T(8,128)(2,1)S(1)} %get-tuple-element.29._), channel_id=1, source_target_pairs={{0,1},{1,2},{2,3},{3,7},{4,0},{5,4},{6,5},{7,6},{8,9},{9,10},{10,1... | collective-permute-start | bytes 589832 | tf_op jit(solution)/shard_map/ppermute | solution.py:444
  8.6 0.4 %collective-permute-start.3 = (bf16[3,128,256]{2,1,0:T(8,128)(2,1)S(1)}, bf16[3,128,256]{2,1,0:T(8,128)(2,1)S(1)}, u32[]{:S(2)}, u32[]{:S(2)}) collective-permute-start(bf16[3,128,256]{2,1,0:T(8,128)(2,1)S(1)} %get-tuple-element.30), channel_id=1, source_target_pairs={{1,0},{2,1},{3,2},{7,3},{0,4},{4,5},{5,6},{6,7},{9,8},{10,9},{11,1... | collective-permute-start | bytes 589832 | tf_op jit(solution)/shard_map/ppermute | solution.py:445
  9.0 1.7 %inner_a.1 = (f32[8,128,256]{2,1,0:T(8,128)S(1)}, bf16[8,128,256]{2,1,0:T(8,128)(2,1)S(1)}) custom-call(bf16[3,128,256]{2,1,0:T(8,128)(2,1)S(1)} %get-tuple-element.29._, bf16[16,128,256]{2,1,0:T(8,128)(2,1)S(1)} %get-tuple-element.27.raw_a.refs_0_._, bf16[3,3,256,256]{3,2,1,0:T(8,128)(2,1)S(1)} %get-tuple-element.31.kernel.refs_1_.refs_2_, ...), custom_call_target="tpu_custom_call" | custom-call | flops 9663676416 | bytes 1572864 | tf_op jit(solution)/shard_map/inner_a/pallas_call | solution.py:399
  10.8 1.9 %collective-permute-start.7 = (bf16[8,128,256]{2,1,0:T(8,128)(2,1)S(1)}, bf16[8,128,256]{2,1,0:T(8,128)(2,1)S(1)}, u32[]{:S(2)}, u32[]{:S(2)}) collective-permute-start(bf16[8,128,256]{2,1,0:T(8,128)(2,1)S(1)} %get-tuple-element.36._.refs_1_), channel_id=1, source_target_pairs={{0,4},{4,8},{8,12},{1,5},{5,9},{9,13},{2,6},{6,10},{10,14},{3,7},{... | collective-permute-start | bytes 1572872 | tf_op jit(solution)/shard_map/ppermute | solution.py:446
  12.7 2.9 %inner_b.1 = (f32[14,128,256]{2,1,0:T(8,128)S(1)}, bf16[14,128,256]{2,1,0:T(8,128)(2,1)S(1)}) custom-call(bf16[8,128,256]{2,1,0:T(8,128)(2,1)S(1)} %get-tuple-element.36._.refs_1_, bf16[3,128,256]{2,1,0:T(8,128)(2,1)S(1)} %get-tuple-element.28.edges_b.refs_0_, bf16[13,128,256]{2,1,0:T(8,128)(2,1)S(1)} %get-tuple-element.26._.inners_b.refs_1_, ...), custom_call_target="tpu_custom_call" | custom-call | flops 2113929216 | bytes 2752512 | tf_op jit(solution)/shard_map/inner_b/pallas_call | solution.py:399
  15.6 0.0 copy-start.3
  15.6 0.0 collective-permute-done.2.got_0
  15.6 0.0 collective-permute-done.3.got_1
  15.6 1.3 %edges.1 = (f32[2,128,256]{2,1,0:T(8,128)S(1)}, bf16[2,128,256]{2,1,0:T(8,128)(2,1)S(1)}, f32[2,128,256]{2,1,0:T(8,128)S(1)}, bf16[2,128,256]{2,1,0:T(8,128)(2,1)S(1)}, bf16[2,128,256]{2,1,0:T(8,128)(2,1)S(1)}) custom-call(bf16[16,128,256]{2,1,0:T(8,128)(2,1)S(1)} %get-tuple-element.27.raw_a.refs_0_._, ...), custom_call_target="tpu_custom_call" | custom-call | flops 603979776 | bytes 786432 | tf_op jit(solution)/shard_map/edges/pallas_call | solution.py:399
  17.0 0.1 collective-permute-start.6
  17.0 0.5 %collective-permute-start.4 = (bf16[2,128,256]{2,1,0:T(8,128)(2,1)S(1)}, bf16[2,128,256]{2,1,0:T(8,128)(2,1)S(1)}, u32[]{:S(2)}, u32[]{:S(2)}) collective-permute-start(bf16[2,128,256]{2,1,0:T(8,128)(2,1)S(1)} %get-tuple-element.33), channel_id=1, source_target_pairs={{0,4},{4,8},{8,12},{12,0},{1,5},{5,9},{9,13},{13,1},{2,6},{6,10},{... | collective-permute-start | bytes 393224 | tf_op jit(solution)/shard_map/ppermute | solution.py:455
  17.5 0.0 collective-permute-done.5.inners
  17.5 4.7 %main.1 = (bf16[2,16,128,256]{3,2,1,0:T(8,128)(2,1)}, f32[16,128,256]{2,1,0:T(8,128)S(1)}) custom-call(bf16[3,128,256]{2,1,0:T(8,128)(2,1)S(1)} %get-tuple-element.34.edges, bf16[13,128,256]{2,1,0:T(8,128)(2,1)S(1)} %collective-permute-done.5.inners, bf16[3,128,256]{2,1,0:T(8,128)(2,1)S(1)} %collective-permute-done.2.got_0, ...), custom_call_target="tpu_custom_call" | custom-call | flops 30064771072 | bytes 10485760 | tf_op jit(solution)/shard_map/main/pallas_call | solution.py:399
  22.2 0.0 collective-permute-done.8.refs_1_
  22.2 0.0 collective-permute-done.6.products
  22.2 2.0 %collective-permute-done.7.refs_0_ = bf16[8,128,256]{2,1,0:T(8,128)(2,1)S(1)} collective-permute-done((bf16[8,128,256]{2,1,0:T(8,128)(2,1)S(1)}, bf16[8,128,256]{2,1,0:T(8,128)(2,1)S(1)}, u32[]{:S(2)}, u32[]{:S(2)}) %collective-permute-start.7) | collective-permute-done | bytes 524320 | tf_op jit(solution)/shard_map/ppermute | solution.py:446
  24.2 1.4 %inner_finish.1._ = bf16[2,16,128,256]{3,2,1,0:T(8,128)(2,1)} custom-call(f32[16,128,256]{2,1,0:T(8,128)S(1)} %get-tuple-element.45.base, bf16[3,256,256]{2,1,0:T(8,128)(2,1)S(1)} %get-tuple-element.32.time_kernel, bf16[2,128,256]{2,1,0:T(8,128)(2,1)S(1)} %collective-permute-done.6.products, ...), custom_call_target="tpu_custom_call", output_to_operand_aliasing={{}: (5, {})} | custom-call | flops 268435456 | bytes 4194304 | tf_op jit(solution)/shard_map/inner_finish/pallas_call | solution.py:399
  25.6 0.0 collective-permute-done.4.products
  25.6 0.7 %finish.1 = bf16[2,16,128,256]{3,2,1,0:T(8,128)(2,1)} custom-call(bf16[2,128,256]{2,1,0:T(8,128)(2,1)S(1)} %collective-permute-done.4.products, f32[16,128,256]{2,1,0:T(8,128)S(1)} %get-tuple-element.45.base, bf16[2,16,128,256]{3,2,1,0:T(8,128)(2,1)} %inner_finish.1._), custom_call_target="tpu_custom_call", output_to_operand_aliasing={{}: (2, {})} | custom-call | flops 33554432 | bytes 524288 | tf_op jit(solution)/shard_map/finish/pallas_call | solution.py:399
  (6 shorter events, 0.1 us)
Async XLA Ops:
  0.0 6.8 %collective-permute-start = (bf16[3,128,256]{2,1,0:T(8,128)(2,1)S(1)}, bf16[3,128,256]{2,1,0:T(8,128)(2,1)S(1)}, u32[]{:S(2)}, u32[]{:S(2)}) collective-permute-start(bf16[3,128,256]{2,1,0:T(8,128)(2,1)S(1)} %ends.1._), channel_id=1, source_target_pairs={{0,4},{4,8},{8,12},{12,0},{1,5},{5,9},{9,13},{13,1},{2,6},{6,10},{... | collective-permute-start | bytes 589832 | tf_op jit(solution)/shard_map/ppermute | solution.py:417
  2.1 4.8 %collective-permute-start.1 = (bf16[3,128,256]{2,1,0:T(8,128)(2,1)S(1)}, bf16[3,128,256]{2,1,0:T(8,128)(2,1)S(1)}, u32[]{:S(2)}, u32[]{:S(2)}) collective-permute-start(bf16[3,128,256]{2,1,0:T(8,128)(2,1)S(1)} %get-tuple-element.28.edges_b.refs_0_), channel_id=1, source_target_pairs={{0,4},{4,0},{8,12},{12,8},{1,5},{5,1},{9,13},{13,9},{2,6},{6,2},{1... | collective-permute-start | bytes 589832 | tf_op jit(solution)/shard_map/ppermute | solution.py:430
  2.2 2.2 %copy-start = (f32[256]{0:T(256)S(1)}, f32[256]{0:T(256)}, u32[]{:S(2)}) copy-start(f32[256]{0:T(256)} %param.9) | copy-start | bytes 3076
  2.2 2.2 %copy-start.1 = (f32[256]{0:T(256)S(1)}, f32[256]{0:T(256)}, u32[]{:S(2)}) copy-start(f32[256]{0:T(256)} %param.10) | copy-start | bytes 3076
  2.2 2.2 %copy-start.2 = (f32[256]{0:T(256)S(1)}, f32[256]{0:T(256)}, u32[]{:S(2)}) copy-start(f32[256]{0:T(256)} %param.12) | copy-start | bytes 3076
  2.2 15.3 %collective-permute-start.5 = (bf16[13,128,256]{2,1,0:T(8,128)(2,1)S(1)}, bf16[13,128,256]{2,1,0:T(8,128)(2,1)S(1)}, u32[]{:S(2)}, u32[]{:S(2)}) collective-permute-start(bf16[13,128,256]{2,1,0:T(8,128)(2,1)S(1)} %get-tuple-element.26._.inners_b.refs_1_), channel_id=1, source_target_pairs={{0,4},{4,8},{8,12},{12,0},{1,5},{5,9},{9,13},{13,1},{2,6},{6,10},{... | collective-permute-start | bytes 2555912 | tf_op jit(solution)/shard_map/ppermute | solution.py:428
  5.8 16.4 %collective-permute-start.8 = (bf16[6,128,256]{2,1,0:T(8,128)(2,1)S(1)}, bf16[6,128,256]{2,1,0:T(8,128)(2,1)S(1)}, u32[]{:S(2)}, u32[]{:S(2)}) collective-permute-start(bf16[6,128,256]{2,1,0:T(8,128)(2,1)S(1)} %get-tuple-element.44.refs_3_), channel_id=1, source_target_pairs={{0,4},{4,8},{8,12},{12,0},{1,5},{5,9},{9,13},{13,1},{2,6},{6,10},{... | collective-permute-start | bytes 1179656 | tf_op jit(solution)/shard_map/ppermute | solution.py:447
  7.0 8.6 %collective-permute-start.2 = (bf16[3,128,256]{2,1,0:T(8,128)(2,1)S(1)}, bf16[3,128,256]{2,1,0:T(8,128)(2,1)S(1)}, u32[]{:S(2)}, u32[]{:S(2)}) collective-permute-start(bf16[3,128,256]{2,1,0:T(8,128)(2,1)S(1)} %get-tuple-element.29._), channel_id=1, source_target_pairs={{0,1},{1,2},{2,3},{3,7},{4,0},{5,4},{6,5},{7,6},{8,9},{9,10},{10,1... | collective-permute-start | bytes 589832 | tf_op jit(solution)/shard_map/ppermute | solution.py:444
  8.6 7.1 %collective-permute-start.3 = (bf16[3,128,256]{2,1,0:T(8,128)(2,1)S(1)}, bf16[3,128,256]{2,1,0:T(8,128)(2,1)S(1)}, u32[]{:S(2)}, u32[]{:S(2)}) collective-permute-start(bf16[3,128,256]{2,1,0:T(8,128)(2,1)S(1)} %get-tuple-element.30), channel_id=1, source_target_pairs={{1,0},{2,1},{3,2},{7,3},{0,4},{4,5},{5,6},{6,7},{9,8},{10,9},{11,1... | collective-permute-start | bytes 589832 | tf_op jit(solution)/shard_map/ppermute | solution.py:445
  10.8 13.5 %collective-permute-start.7 = (bf16[8,128,256]{2,1,0:T(8,128)(2,1)S(1)}, bf16[8,128,256]{2,1,0:T(8,128)(2,1)S(1)}, u32[]{:S(2)}, u32[]{:S(2)}) collective-permute-start(bf16[8,128,256]{2,1,0:T(8,128)(2,1)S(1)} %get-tuple-element.36._.refs_1_), channel_id=1, source_target_pairs={{0,4},{4,8},{8,12},{1,5},{5,9},{9,13},{2,6},{6,10},{10,14},{3,7},{... | collective-permute-start | bytes 1572872 | tf_op jit(solution)/shard_map/ppermute | solution.py:446
  15.6 1.9 %copy-start.3 = (f32[256]{0:T(256)S(1)}, f32[256]{0:T(256)}, u32[]{:S(2)}) copy-start(f32[256]{0:T(256)} %param.13) | copy-start | bytes 3076
  17.0 5.3 %collective-permute-start.6 = (bf16[2,128,256]{2,1,0:T(8,128)(2,1)S(1)}, bf16[2,128,256]{2,1,0:T(8,128)(2,1)S(1)}, u32[]{:S(2)}, u32[]{:S(2)}) collective-permute-start(bf16[2,128,256]{2,1,0:T(8,128)(2,1)S(1)} %get-tuple-element.33), channel_id=1, source_target_pairs={{0,4},{4,0},{8,12},{12,8},{1,5},{5,1},{9,13},{13,9},{2,6},{6,2},{1... | collective-permute-start | bytes 393224 | tf_op jit(solution)/shard_map/ppermute | solution.py:458
  17.0 8.6 %collective-permute-start.4 = (bf16[2,128,256]{2,1,0:T(8,128)(2,1)S(1)}, bf16[2,128,256]{2,1,0:T(8,128)(2,1)S(1)}, u32[]{:S(2)}, u32[]{:S(2)}) collective-permute-start(bf16[2,128,256]{2,1,0:T(8,128)(2,1)S(1)} %get-tuple-element.33), channel_id=1, source_target_pairs={{0,4},{4,8},{8,12},{12,0},{1,5},{5,9},{9,13},{13,1},{2,6},{6,10},{... | collective-permute-start | bytes 393224 | tf_op jit(solution)/shard_map/ppermute | solution.py:455

commit v9 on v8

--- a/solution.py
+++ b/solution.py
@@ -341,17 +341,21 @@
     keep = jnp.where(lax.axis_index("frame") > 0, 1.0, 0.0)
     kernel = (time_kernel[2].astype(F32) * keep).astype(BF16)
     start = 1
+    copies = []
     for part in arrived:
         for row, count in blocks(start, start + part.shape[0]):
             normed = part[pl.ds(row - start, count)].reshape(count * cols, channels)
             total = base[row : row + count].reshape(count * cols, channels)
             total += jnp.dot(normed, kernel, preferred_element_type=F32)
-            decoded[pl.ds(row - 1, count)] = total.astype(BF16).reshape(count, cols, channels)
+            at = pl.ds(row - 1, count)
+            decoded[at] = total.astype(BF16).reshape(count, cols, channels)
+            copies.append(pltpu.make_async_copy(
+                decoded.at[at], out_ref.at[0, pl.ds(row, count)], sems.at[2 + len(copies)]))
+            copies[-1].start()
         start += part.shape[0]
-    copy = pltpu.make_async_copy(decoded, out_ref.at[0, pl.ds(1, decoded.shape[0])], sems.at[2])
-    copy.start()
     pl.when(jnp.logical_not(ends_late(frames)))(lambda: write_edges(products, base, out_ref, edges, sems))
-    copy.wait()
+    for copy in copies:
+        copy.wait()
 
 
 def finish_kernel(frames, products, base, _, out_ref, edges, sems):
@@ -469,7 +473,7 @@
     (decoded,) = call(
         functools.partial(inner_finish_kernel, count_f),
         [base, time_kernel, edge_swapped, *arrived, (ANY, decoded)], [out],
-        [room(rows - 2), room(2), pltpu.SemaphoreType.DMA((3,))],
+        [room(rows - 2), room(2), pltpu.SemaphoreType.DMA((rows,))],
         3, "inner_finish", input_output_aliases={3 + len(arrived): 0},
         cost_estimate=cost(rows * cols, 1, channels, 4),
     )

time: 26.7 us -> 26.7 us (level)
  transfers between devices with their start and end apart: 9 -> 9, of which waited for: 1 -> 2; matrix products, arithmetic and copies ran while one was open for 0% -> 0% of each run, Pallas kernels for 62% -> 62%
where the time goes in v9:
time: 26.7 us; the launch traced here: 26.5 us
  Pallas kernels  17.1 us (64%)
  starting transfers between devices  6.93 us (26%)
  waiting for transfers between devices  2.12 us (8%)
  between operations  0.35 us (1%)
    pallas_call x12, Pallas kernels, call(): pl.pallas_call(kernel, in_specs=list(specs), out_specs=list(out_specs), o...  17.1 us
    ppermute x1, waiting for transfers between devices, body(): arrived = [lax.ppermute(normed_ai[0], 'frame', onward[:-1])]  2 us
    ppermute x1, starting transfers between devices, body(): arrived = [lax.ppermute(normed_ai[0], 'frame', onward[:-1])]  1.92 us
    ppermute x1, starting transfers between devices, body(): got_0 = lax.ppermute(send_0, ('frame', 'band'), ring)  1.59 us
    ppermute x1, starting transfers between devices, body(): arrived += [lax.ppermute(part, 'frame', onward) for part in normed_ai[1:]]  1.07 us
    ppermute x1, starting transfers between devices, body(): edge = [lax.ppermute(ends, 'frame', onward)]  0.78 us
  transfers between devices with their start and end apart: 9, of which 2 were waited for; matrix products, arithmetic and copies ran while one was open for 0% of the time, Pallas kernels for 62%

profile of v9, /device:TPU:18, one launch (start us, length us, event | category | flops | bytes accessed | tf_op | source)
XLA Modules:
  0.0 26.5 jit_solution(13709239323692016986)
XLA Ops:
  0.0 0.8 %collective-permute-start = (bf16[3,128,256]{2,1,0:T(8,128)(2,1)S(1)}, bf16[3,128,256]{2,1,0:T(8,128)(2,1)S(1)}, u32[]{:S(2)}, u32[]{:S(2)}) collective-permute-start(bf16[3,128,256]{2,1,0:T(8,128)(2,1)S(1)} %ends.1._), channel_id=1, source_target_pairs={{0,4},{4,8},{8,12},{12,0},{1,5},{5,9},{9,13},{13,1},{2,6},{6,10},{... | collective-permute-start | bytes 589832 | tf_op jit(solution)/shard_map/ppermute | solution.py:421
  0.8 1.3 %load.1 = (bf16[3,128,256]{2,1,0:T(8,128)(2,1)S(1)}, bf16[13,128,256]{2,1,0:T(8,128)(2,1)S(1)}) custom-call(bf16[3,128,256]{2,1,0:T(8,128)(2,1)S(1)} %ends.1._, bf16[2,16,128,256]{3,2,1,0:T(8,128)(2,1)} %feats.5), custom_call_target="tpu_custom_call" | custom-call | tf_op jit(solution)/shard_map/load/pallas_call | solution.py:403
  2.1 0.1 collective-permute-start.1
  2.2 0.0 copy-start.1
  2.2 0.0 copy-start.2
  2.2 0.5 %collective-permute-start.5 = (bf16[13,128,256]{2,1,0:T(8,128)(2,1)S(1)}, bf16[13,128,256]{2,1,0:T(8,128)(2,1)S(1)}, u32[]{:S(2)}, u32[]{:S(2)}) collective-permute-start(bf16[13,128,256]{2,1,0:T(8,128)(2,1)S(1)} %get-tuple-element.26._.inners_b.refs_1_), channel_id=1, source_target_pairs={{0,4},{4,8},{8,12},{12,0},{1,5},{5,9},{9,13},{13,1},{2,6},{6,10},{... | collective-permute-start | bytes 2555912 | tf_op jit(solution)/shard_map/ppermute | solution.py:432
  2.7 1.7 %load_rest.1 = (bf16[16,128,256]{2,1,0:T(8,128)(2,1)S(1)}, bf16[3,3,256,256]{3,2,1,0:T(8,128)(2,1)S(1)}, bf16[3,256,256]{2,1,0:T(8,128)(2,1)S(1)}) custom-call(bf16[13,128,256]{2,1,0:T(8,128)(2,1)S(1)} %get-tuple-element.26._.inners_b.refs_1_, bf16[2,16,128,256]{3,2,1,0:T(8,128)(2,1)} %feats.5, bf16[3,3,256,256]{3,2,1,0:T(8,128)(2,1)} %kernel.1, ...), custom_call_target="tpu_custom_call" | custom-call | tf_op jit(solution)/shard_map/load_rest/pallas_call | solution.py:403
  4.4 0.0 copy-done
  4.4 1.4 %inner_a_ring.1 = (f32[6,128,256]{2,1,0:T(8,128)S(1)}, bf16[6,128,256]{2,1,0:T(8,128)(2,1)S(1)}) custom-call(bf16[16,128,256]{2,1,0:T(8,128)(2,1)S(1)} %get-tuple-element.27.raw_a.refs_0_._, bf16[16,128,256]{2,1,0:T(8,128)(2,1)S(1)} %get-tuple-element.27.raw_a.refs_0_._, bf16[3,3,256,256]{3,2,1,0:T(8,128)(2,1)S(1)} %get-tuple-element.31.kernel.refs_1_.refs_2_, ...), custom_call_target="tpu_custom_call" | custom-call | flops 905969664 | bytes 1179648 | tf_op jit(solution)/shard_map/inner_a_ring/pallas_call | solution.py:403
  5.8 1.1 %collective-permute-start.8 = (bf16[6,128,256]{2,1,0:T(8,128)(2,1)S(1)}, bf16[6,128,256]{2,1,0:T(8,128)(2,1)S(1)}, u32[]{:S(2)}, u32[]{:S(2)}) collective-permute-start(bf16[6,128,256]{2,1,0:T(8,128)(2,1)S(1)} %get-tuple-element.44.refs_3_), channel_id=1, source_target_pairs={{0,4},{4,8},{8,12},{12,0},{1,5},{5,9},{9,13},{13,1},{2,6},{6,10},{... | collective-permute-start | bytes 1179656 | tf_op jit(solution)/shard_map/ppermute | solution.py:451
  6.9 0.0 collective-permute-done.source
  6.9 0.0 collective-permute-done.1.refs_1_
  6.9 0.1 halo.1
  7.0 1.6 %collective-permute-start.2 = (bf16[3,128,256]{2,1,0:T(8,128)(2,1)S(1)}, bf16[3,128,256]{2,1,0:T(8,128)(2,1)S(1)}, u32[]{:S(2)}, u32[]{:S(2)}) collective-permute-start(bf16[3,128,256]{2,1,0:T(8,128)(2,1)S(1)} %get-tuple-element.29._), channel_id=1, source_target_pairs={{0,1},{1,2},{2,3},{3,7},{4,0},{5,4},{6,5},{7,6},{8,9},{9,10},{10,1... | collective-permute-start | bytes 589832 | tf_op jit(solution)/shard_map/ppermute | solution.py:448
  8.6 0.4 %collective-permute-start.3 = (bf16[3,128,256]{2,1,0:T(8,128)(2,1)S(1)}, bf16[3,128,256]{2,1,0:T(8,128)(2,1)S(1)}, u32[]{:S(2)}, u32[]{:S(2)}) collective-permute-start(bf16[3,128,256]{2,1,0:T(8,128)(2,1)S(1)} %get-tuple-element.30), channel_id=1, source_target_pairs={{1,0},{2,1},{3,2},{7,3},{0,4},{4,5},{5,6},{6,7},{9,8},{10,9},{11,1... | collective-permute-start | bytes 589832 | tf_op jit(solution)/shard_map/ppermute | solution.py:449
  9.0 1.7 %inner_a.1 = (f32[8,128,256]{2,1,0:T(8,128)S(1)}, bf16[8,128,256]{2,1,0:T(8,128)(2,1)S(1)}) custom-call(bf16[3,128,256]{2,1,0:T(8,128)(2,1)S(1)} %get-tuple-element.29._, bf16[16,128,256]{2,1,0:T(8,128)(2,1)S(1)} %get-tuple-element.27.raw_a.refs_0_._, bf16[3,3,256,256]{3,2,1,0:T(8,128)(2,1)S(1)} %get-tuple-element.31.kernel.refs_1_.refs_2_, ...), custom_call_target="tpu_custom_call" | custom-call | flops 9663676416 | bytes 1572864 | tf_op jit(solution)/shard_map/inner_a/pallas_call | solution.py:403
  10.8 1.9 %collective-permute-start.7 = (bf16[8,128,256]{2,1,0:T(8,128)(2,1)S(1)}, bf16[8,128,256]{2,1,0:T(8,128)(2,1)S(1)}, u32[]{:S(2)}, u32[]{:S(2)}) collective-permute-start(bf16[8,128,256]{2,1,0:T(8,128)(2,1)S(1)} %get-tuple-element.36._.refs_1_), channel_id=1, source_target_pairs={{0,4},{4,8},{8,12},{1,5},{5,9},{9,13},{2,6},{6,10},{10,14},{3,7},{... | collective-permute-start | bytes 1572872 | tf_op jit(solution)/shard_map/ppermute | solution.py:450
  12.7 2.9 %inner_b.1 = (f32[14,128,256]{2,1,0:T(8,128)S(1)}, bf16[14,128,256]{2,1,0:T(8,128)(2,1)S(1)}) custom-call(bf16[8,128,256]{2,1,0:T(8,128)(2,1)S(1)} %get-tuple-element.36._.refs_1_, bf16[3,128,256]{2,1,0:T(8,128)(2,1)S(1)} %get-tuple-element.28.edges_b.refs_0_, bf16[13,128,256]{2,1,0:T(8,128)(2,1)S(1)} %get-tuple-element.26._.inners_b.refs_1_, ...), custom_call_target="tpu_custom_call" | custom-call | flops 2113929216 | bytes 2752512 | tf_op jit(solution)/shard_map/inner_b/pallas_call | solution.py:403
  15.6 0.0 copy-start.3
  15.6 0.0 collective-permute-done.2.got_0
  15.6 0.0 collective-permute-done.3.got_1
  15.6 1.3 %edges.1 = (f32[2,128,256]{2,1,0:T(8,128)S(1)}, bf16[2,128,256]{2,1,0:T(8,128)(2,1)S(1)}, f32[2,128,256]{2,1,0:T(8,128)S(1)}, bf16[2,128,256]{2,1,0:T(8,128)(2,1)S(1)}, bf16[2,128,256]{2,1,0:T(8,128)(2,1)S(1)}) custom-call(bf16[16,128,256]{2,1,0:T(8,128)(2,1)S(1)} %get-tuple-element.27.raw_a.refs_0_._, ...), custom_call_target="tpu_custom_call" | custom-call | flops 603979776 | bytes 786432 | tf_op jit(solution)/shard_map/edges/pallas_call | solution.py:403
  17.0 0.1 collective-permute-start.6
  17.0 0.5 %collective-permute-start.4 = (bf16[2,128,256]{2,1,0:T(8,128)(2,1)S(1)}, bf16[2,128,256]{2,1,0:T(8,128)(2,1)S(1)}, u32[]{:S(2)}, u32[]{:S(2)}) collective-permute-start(bf16[2,128,256]{2,1,0:T(8,128)(2,1)S(1)} %get-tuple-element.33), channel_id=1, source_target_pairs={{0,4},{4,8},{8,12},{12,0},{1,5},{5,9},{9,13},{13,1},{2,6},{6,10},{... | collective-permute-start | bytes 393224 | tf_op jit(solution)/shard_map/ppermute | solution.py:459
  17.5 0.0 collective-permute-done.5.inners
  17.5 4.7 %main.1 = (bf16[2,16,128,256]{3,2,1,0:T(8,128)(2,1)}, f32[16,128,256]{2,1,0:T(8,128)S(1)}) custom-call(bf16[3,128,256]{2,1,0:T(8,128)(2,1)S(1)} %get-tuple-element.34.edges, bf16[13,128,256]{2,1,0:T(8,128)(2,1)S(1)} %collective-permute-done.5.inners, bf16[3,128,256]{2,1,0:T(8,128)(2,1)S(1)} %collective-permute-done.2.got_0, ...), custom_call_target="tpu_custom_call" | custom-call | flops 30064771072 | bytes 10485760 | tf_op jit(solution)/shard_map/main/pallas_call | solution.py:403
  22.2 0.0 collective-permute-done.8.refs_1_
  22.2 0.0 collective-permute-done.6.products
  22.2 2.0 %collective-permute-done.7.refs_0_ = bf16[8,128,256]{2,1,0:T(8,128)(2,1)S(1)} collective-permute-done((bf16[8,128,256]{2,1,0:T(8,128)(2,1)S(1)}, bf16[8,128,256]{2,1,0:T(8,128)(2,1)S(1)}, u32[]{:S(2)}, u32[]{:S(2)}) %collective-permute-start.7) | collective-permute-done | bytes 524320 | tf_op jit(solution)/shard_map/ppermute | solution.py:450
  24.2 1.3 %inner_finish.1._ = bf16[2,16,128,256]{3,2,1,0:T(8,128)(2,1)} custom-call(f32[16,128,256]{2,1,0:T(8,128)S(1)} %get-tuple-element.45.base, bf16[3,256,256]{2,1,0:T(8,128)(2,1)S(1)} %get-tuple-element.32.time_kernel, bf16[2,128,256]{2,1,0:T(8,128)(2,1)S(1)} %collective-permute-done.6.products, ...), custom_call_target="tpu_custom_call", output_to_operand_aliasing={{}: (5, {})} | custom-call | flops 268435456 | bytes 4194304 | tf_op jit(solution)/shard_map/inner_finish/pallas_call | solution.py:403
  25.5 0.1 collective-permute-done.4.products
  25.6 0.7 %finish.1 = bf16[2,16,128,256]{3,2,1,0:T(8,128)(2,1)} custom-call(bf16[2,128,256]{2,1,0:T(8,128)(2,1)S(1)} %collective-permute-done.4.products, f32[16,128,256]{2,1,0:T(8,128)S(1)} %get-tuple-element.45.base, bf16[2,16,128,256]{3,2,1,0:T(8,128)(2,1)} %inner_finish.1._), custom_call_target="tpu_custom_call", output_to_operand_aliasing={{}: (2, {})} | custom-call | flops 33554432 | bytes 524288 | tf_op jit(solution)/shard_map/finish/pallas_call | solution.py:403
  (6 shorter events, 0.1 us)
Async XLA Ops:
  0.0 6.8 %collective-permute-start = (bf16[3,128,256]{2,1,0:T(8,128)(2,1)S(1)}, bf16[3,128,256]{2,1,0:T(8,128)(2,1)S(1)}, u32[]{:S(2)}, u32[]{:S(2)}) collective-permute-start(bf16[3,128,256]{2,1,0:T(8,128)(2,1)S(1)} %ends.1._), channel_id=1, source_target_pairs={{0,4},{4,8},{8,12},{12,0},{1,5},{5,9},{9,13},{13,1},{2,6},{6,10},{... | collective-permute-start | bytes 589832 | tf_op jit(solution)/shard_map/ppermute | solution.py:421
  2.1 4.8 %collective-permute-start.1 = (bf16[3,128,256]{2,1,0:T(8,128)(2,1)S(1)}, bf16[3,128,256]{2,1,0:T(8,128)(2,1)S(1)}, u32[]{:S(2)}, u32[]{:S(2)}) collective-permute-start(bf16[3,128,256]{2,1,0:T(8,128)(2,1)S(1)} %get-tuple-element.28.edges_b.refs_0_), channel_id=1, source_target_pairs={{0,4},{4,0},{8,12},{12,8},{1,5},{5,1},{9,13},{13,9},{2,6},{6,2},{1... | collective-permute-start | bytes 589832 | tf_op jit(solution)/shard_map/ppermute | solution.py:434
  2.2 2.2 %copy-start = (f32[256]{0:T(256)S(1)}, f32[256]{0:T(256)}, u32[]{:S(2)}) copy-start(f32[256]{0:T(256)} %param.9) | copy-start | bytes 3076
  2.2 2.2 %copy-start.1 = (f32[256]{0:T(256)S(1)}, f32[256]{0:T(256)}, u32[]{:S(2)}) copy-start(f32[256]{0:T(256)} %param.10) | copy-start | bytes 3076
  2.2 2.2 %copy-start.2 = (f32[256]{0:T(256)S(1)}, f32[256]{0:T(256)}, u32[]{:S(2)}) copy-start(f32[256]{0:T(256)} %param.12) | copy-start | bytes 3076
  2.2 15.3 %collective-permute-start.5 = (bf16[13,128,256]{2,1,0:T(8,128)(2,1)S(1)}, bf16[13,128,256]{2,1,0:T(8,128)(2,1)S(1)}, u32[]{:S(2)}, u32[]{:S(2)}) collective-permute-start(bf16[13,128,256]{2,1,0:T(8,128)(2,1)S(1)} %get-tuple-element.26._.inners_b.refs_1_), channel_id=1, source_target_pairs={{0,4},{4,8},{8,12},{12,0},{1,5},{5,9},{9,13},{13,1},{2,6},{6,10},{... | collective-permute-start | bytes 2555912 | tf_op jit(solution)/shard_map/ppermute | solution.py:432
  5.8 16.4 %collective-permute-start.8 = (bf16[6,128,256]{2,1,0:T(8,128)(2,1)S(1)}, bf16[6,128,256]{2,1,0:T(8,128)(2,1)S(1)}, u32[]{:S(2)}, u32[]{:S(2)}) collective-permute-start(bf16[6,128,256]{2,1,0:T(8,128)(2,1)S(1)} %get-tuple-element.44.refs_3_), channel_id=1, source_target_pairs={{0,4},{4,8},{8,12},{12,0},{1,5},{5,9},{9,13},{13,1},{2,6},{6,10},{... | collective-permute-start | bytes 1179656 | tf_op jit(solution)/shard_map/ppermute | solution.py:451
  7.0 8.6 %collective-permute-start.2 = (bf16[3,128,256]{2,1,0:T(8,128)(2,1)S(1)}, bf16[3,128,256]{2,1,0:T(8,128)(2,1)S(1)}, u32[]{:S(2)}, u32[]{:S(2)}) collective-permute-start(bf16[3,128,256]{2,1,0:T(8,128)(2,1)S(1)} %get-tuple-element.29._), channel_id=1, source_target_pairs={{0,1},{1,2},{2,3},{3,7},{4,0},{5,4},{6,5},{7,6},{8,9},{9,10},{10,1... | collective-permute-start | bytes 589832 | tf_op jit(solution)/shard_map/ppermute | solution.py:448
  8.6 7.1 %collective-permute-start.3 = (bf16[3,128,256]{2,1,0:T(8,128)(2,1)S(1)}, bf16[3,128,256]{2,1,0:T(8,128)(2,1)S(1)}, u32[]{:S(2)}, u32[]{:S(2)}) collective-permute-start(bf16[3,128,256]{2,1,0:T(8,128)(2,1)S(1)} %get-tuple-element.30), channel_id=1, source_target_pairs={{1,0},{2,1},{3,2},{7,3},{0,4},{4,5},{5,6},{6,7},{9,8},{10,9},{11,1... | collective-permute-start | bytes 589832 | tf_op jit(solution)/shard_map/ppermute | solution.py:449
  10.8 13.5 %collective-permute-start.7 = (bf16[8,128,256]{2,1,0:T(8,128)(2,1)S(1)}, bf16[8,128,256]{2,1,0:T(8,128)(2,1)S(1)}, u32[]{:S(2)}, u32[]{:S(2)}) collective-permute-start(bf16[8,128,256]{2,1,0:T(8,128)(2,1)S(1)} %get-tuple-element.36._.refs_1_), channel_id=1, source_target_pairs={{0,4},{4,8},{8,12},{1,5},{5,9},{9,13},{2,6},{6,10},{10,14},{3,7},{... | collective-permute-start | bytes 1572872 | tf_op jit(solution)/shard_map/ppermute | solution.py:450
  15.6 1.9 %copy-start.3 = (f32[256]{0:T(256)S(1)}, f32[256]{0:T(256)}, u32[]{:S(2)}) copy-start(f32[256]{0:T(256)} %param.13) | copy-start | bytes 3076
  17.0 5.3 %collective-permute-start.6 = (bf16[2,128,256]{2,1,0:T(8,128)(2,1)S(1)}, bf16[2,128,256]{2,1,0:T(8,128)(2,1)S(1)}, u32[]{:S(2)}, u32[]{:S(2)}) collective-permute-start(bf16[2,128,256]{2,1,0:T(8,128)(2,1)S(1)} %get-tuple-element.33), channel_id=1, source_target_pairs={{0,4},{4,0},{8,12},{12,8},{1,5},{5,1},{9,13},{13,9},{2,6},{6,2},{1... | collective-permute-start | bytes 393224 | tf_op jit(solution)/shard_map/ppermute | solution.py:462
  17.0 8.6 %collective-permute-start.4 = (bf16[2,128,256]{2,1,0:T(8,128)(2,1)S(1)}, bf16[2,128,256]{2,1,0:T(8,128)(2,1)S(1)}, u32[]{:S(2)}, u32[]{:S(2)}) collective-permute-start(bf16[2,128,256]{2,1,0:T(8,128)(2,1)S(1)} %get-tuple-element.33), channel_id=1, source_target_pairs={{0,4},{4,8},{8,12},{12,0},{1,5},{5,9},{9,13},{13,1},{2,6},{6,10},{... | collective-permute-start | bytes 393224 | tf_op jit(solution)/shard_map/ppermute | solution.py:459

commit v10 on v9

--- a/solution.py
+++ b/solution.py
@@ -13,7 +13,7 @@
 ANY = pl.BlockSpec(memory_space=pl.ANY)
 HBM = pl.BlockSpec(memory_space=pltpu.HBM)
 STEP = 2
-RING_ROWS = 6
+RING_ROWS = 4
 
 
 def blocks(first, last):

time: 26.7 us -> 26.7 us (level)
  no operation moved by 1% of the time
where the time goes in v10:
time: 26.7 us; the launch traced here: 26.5 us
  Pallas kernels  17.1 us (64%)
  starting transfers between devices  6.93 us (26%)
  waiting for transfers between devices  2.09 us (8%)
  between operations  0.35 us (1%)
    pallas_call x12, Pallas kernels, call(): pl.pallas_call(kernel, in_specs=list(specs), out_specs=list(out_specs), o...  17.1 us
    ppermute x1, waiting for transfers between devices, body(): arrived = [lax.ppermute(normed_ai[0], 'frame', onward[:-1])]  1.97 us
    ppermute x1, starting transfers between devices, body(): arrived = [lax.ppermute(normed_ai[0], 'frame', onward[:-1])]  1.92 us
    ppermute x1, starting transfers between devices, body(): got_0 = lax.ppermute(send_0, ('frame', 'band'), ring)  1.59 us
    ppermute x1, starting transfers between devices, body(): arrived += [lax.ppermute(part, 'frame', onward) for part in normed_ai[1:]]  1.07 us
    ppermute x1, starting transfers between devices, body(): edge = [lax.ppermute(ends, 'frame', onward)]  0.78 us
  transfers between devices with their start and end apart: 9, of which 2 were waited for; matrix products, arithmetic and copies ran while one was open for 0% of the time, Pallas kernels for 62%

profile of v10, /device:TPU:18, one launch (start us, length us, event | category | flops | bytes accessed | tf_op | source)
XLA Modules:
  0.0 26.5 jit_solution(16712318035976830721)
XLA Ops:
  0.0 0.8 %collective-permute-start = (bf16[3,128,256]{2,1,0:T(8,128)(2,1)S(1)}, bf16[3,128,256]{2,1,0:T(8,128)(2,1)S(1)}, u32[]{:S(2)}, u32[]{:S(2)}) collective-permute-start(bf16[3,128,256]{2,1,0:T(8,128)(2,1)S(1)} %ends.1._), channel_id=1, source_target_pairs={{0,4},{4,8},{8,12},{12,0},{1,5},{5,9},{9,13},{13,1},{2,6},{6,10},{... | collective-permute-start | bytes 589832 | tf_op jit(solution)/shard_map/ppermute | solution.py:421
  0.8 1.3 %load.1 = (bf16[3,128,256]{2,1,0:T(8,128)(2,1)S(1)}, bf16[13,128,256]{2,1,0:T(8,128)(2,1)S(1)}) custom-call(bf16[3,128,256]{2,1,0:T(8,128)(2,1)S(1)} %ends.1._, bf16[2,16,128,256]{3,2,1,0:T(8,128)(2,1)} %feats.5), custom_call_target="tpu_custom_call" | custom-call | tf_op jit(solution)/shard_map/load/pallas_call | solution.py:403
  2.1 0.1 collective-permute-start.1
  2.2 0.0 copy-start.1
  2.2 0.0 copy-start.2
  2.2 0.5 %collective-permute-start.5 = (bf16[13,128,256]{2,1,0:T(8,128)(2,1)S(1)}, bf16[13,128,256]{2,1,0:T(8,128)(2,1)S(1)}, u32[]{:S(2)}, u32[]{:S(2)}) collective-permute-start(bf16[13,128,256]{2,1,0:T(8,128)(2,1)S(1)} %get-tuple-element.26._.inners_b.refs_1_), channel_id=1, source_target_pairs={{0,4},{4,8},{8,12},{12,0},{1,5},{5,9},{9,13},{13,1},{2,6},{6,10},{... | collective-permute-start | bytes 2555912 | tf_op jit(solution)/shard_map/ppermute | solution.py:432
  2.7 1.7 %load_rest.1 = (bf16[16,128,256]{2,1,0:T(8,128)(2,1)S(1)}, bf16[3,3,256,256]{3,2,1,0:T(8,128)(2,1)S(1)}, bf16[3,256,256]{2,1,0:T(8,128)(2,1)S(1)}) custom-call(bf16[13,128,256]{2,1,0:T(8,128)(2,1)S(1)} %get-tuple-element.26._.inners_b.refs_1_, bf16[2,16,128,256]{3,2,1,0:T(8,128)(2,1)} %feats.5, bf16[3,3,256,256]{3,2,1,0:T(8,128)(2,1)} %kernel.1, ...), custom_call_target="tpu_custom_call" | custom-call | tf_op jit(solution)/shard_map/load_rest/pallas_call | solution.py:403
  4.4 0.0 copy-done
  4.4 1.0 %inner_a_ring.1 = (f32[4,128,256]{2,1,0:T(8,128)S(1)}, bf16[4,128,256]{2,1,0:T(8,128)(2,1)S(1)}) custom-call(bf16[16,128,256]{2,1,0:T(8,128)(2,1)S(1)} %get-tuple-element.27.raw_a.refs_0_._, bf16[16,128,256]{2,1,0:T(8,128)(2,1)S(1)} %get-tuple-element.27.raw_a.refs_0_._, bf16[3,3,256,256]{3,2,1,0:T(8,128)(2,1)S(1)} %get-tuple-element.31.kernel.refs_1_.refs_2_, ...), custom_call_target="tpu_custom_call" | custom-call | flops 603979776 | bytes 786432 | tf_op jit(solution)/shard_map/inner_a_ring/pallas_call | solution.py:403
  5.5 1.1 %collective-permute-start.8 = (bf16[4,128,256]{2,1,0:T(8,128)(2,1)S(1)}, bf16[4,128,256]{2,1,0:T(8,128)(2,1)S(1)}, u32[]{:S(2)}, u32[]{:S(2)}) collective-permute-start(bf16[4,128,256]{2,1,0:T(8,128)(2,1)S(1)} %get-tuple-element.44.refs_3_), channel_id=1, source_target_pairs={{0,4},{4,8},{8,12},{12,0},{1,5},{5,9},{9,13},{13,1},{2,6},{6,10},{... | collective-permute-start | bytes 786440 | tf_op jit(solution)/shard_map/ppermute | solution.py:451
  6.5 0.0 collective-permute-done.source
  6.6 0.0 collective-permute-done.1.refs_1_
  6.6 0.1 halo.1
  6.6 1.6 %collective-permute-start.2 = (bf16[3,128,256]{2,1,0:T(8,128)(2,1)S(1)}, bf16[3,128,256]{2,1,0:T(8,128)(2,1)S(1)}, u32[]{:S(2)}, u32[]{:S(2)}) collective-permute-start(bf16[3,128,256]{2,1,0:T(8,128)(2,1)S(1)} %get-tuple-element.29._), channel_id=1, source_target_pairs={{0,1},{1,2},{2,3},{3,7},{4,0},{5,4},{6,5},{7,6},{8,9},{9,10},{10,1... | collective-permute-start | bytes 589832 | tf_op jit(solution)/shard_map/ppermute | solution.py:448
  8.2 0.4 %collective-permute-start.3 = (bf16[3,128,256]{2,1,0:T(8,128)(2,1)S(1)}, bf16[3,128,256]{2,1,0:T(8,128)(2,1)S(1)}, u32[]{:S(2)}, u32[]{:S(2)}) collective-permute-start(bf16[3,128,256]{2,1,0:T(8,128)(2,1)S(1)} %get-tuple-element.30), channel_id=1, source_target_pairs={{1,0},{2,1},{3,2},{7,3},{0,4},{4,5},{5,6},{6,7},{9,8},{10,9},{11,1... | collective-permute-start | bytes 589832 | tf_op jit(solution)/shard_map/ppermute | solution.py:449
  8.7 2.1 %inner_a.1 = (f32[10,128,256]{2,1,0:T(8,128)S(1)}, bf16[10,128,256]{2,1,0:T(8,128)(2,1)S(1)}) custom-call(bf16[3,128,256]{2,1,0:T(8,128)(2,1)S(1)} %get-tuple-element.29._, bf16[16,128,256]{2,1,0:T(8,128)(2,1)S(1)} %get-tuple-element.27.raw_a.refs_0_._, bf16[3,3,256,256]{3,2,1,0:T(8,128)(2,1)S(1)} %get-tuple-element.31.kernel.refs_1_.refs_2_, ...), custom_call_target="tpu_custom_call" | custom-call | flops 12079595520 | bytes 1966080 | tf_op jit(solution)/shard_map/inner_a/pallas_call | solution.py:403
  10.8 1.9 %collective-permute-start.7 = (bf16[10,128,256]{2,1,0:T(8,128)(2,1)S(1)}, bf16[10,128,256]{2,1,0:T(8,128)(2,1)S(1)}, u32[]{:S(2)}, u32[]{:S(2)}) collective-permute-start(bf16[10,128,256]{2,1,0:T(8,128)(2,1)S(1)} %get-tuple-element.36._.refs_1_), channel_id=1, source_target_pairs={{0,4},{4,8},{8,12},{1,5},{5,9},{9,13},{2,6},{6,10},{10,14},{3,7},{... | collective-permute-start | bytes 1966088 | tf_op jit(solution)/shard_map/ppermute | solution.py:450
  12.7 2.9 %inner_b.1 = (f32[14,128,256]{2,1,0:T(8,128)S(1)}, bf16[14,128,256]{2,1,0:T(8,128)(2,1)S(1)}) custom-call(bf16[10,128,256]{2,1,0:T(8,128)(2,1)S(1)} %get-tuple-element.36._.refs_1_, bf16[3,128,256]{2,1,0:T(8,128)(2,1)S(1)} %get-tuple-element.28.edges_b.refs_0_, bf16[13,128,256]{2,1,0:T(8,128)(2,1)S(1)} %get-tuple-element.26._.inners_b.refs_1_, ...), custom_call_target="tpu_custom_call" | custom-call | flops 2113929216 | bytes 2752512 | tf_op jit(solution)/shard_map/inner_b/pallas_call | solution.py:403
  15.6 0.0 copy-start.3
  15.6 0.0 collective-permute-done.2.got_0
  15.6 0.0 collective-permute-done.3.got_1
  15.7 1.3 %edges.1 = (f32[2,128,256]{2,1,0:T(8,128)S(1)}, bf16[2,128,256]{2,1,0:T(8,128)(2,1)S(1)}, f32[2,128,256]{2,1,0:T(8,128)S(1)}, bf16[2,128,256]{2,1,0:T(8,128)(2,1)S(1)}, bf16[2,128,256]{2,1,0:T(8,128)(2,1)S(1)}) custom-call(bf16[16,128,256]{2,1,0:T(8,128)(2,1)S(1)} %get-tuple-element.27.raw_a.refs_0_._, ...), custom_call_target="tpu_custom_call" | custom-call | flops 603979776 | bytes 786432 | tf_op jit(solution)/shard_map/edges/pallas_call | solution.py:403
  17.0 0.1 collective-permute-start.6
  17.1 0.5 %collective-permute-start.4 = (bf16[2,128,256]{2,1,0:T(8,128)(2,1)S(1)}, bf16[2,128,256]{2,1,0:T(8,128)(2,1)S(1)}, u32[]{:S(2)}, u32[]{:S(2)}) collective-permute-start(bf16[2,128,256]{2,1,0:T(8,128)(2,1)S(1)} %get-tuple-element.33), channel_id=1, source_target_pairs={{0,4},{4,8},{8,12},{12,0},{1,5},{5,9},{9,13},{13,1},{2,6},{6,10},{... | collective-permute-start | bytes 393224 | tf_op jit(solution)/shard_map/ppermute | solution.py:459
  17.6 0.0 collective-permute-done.5.inners
  17.6 4.7 %main.1 = (bf16[2,16,128,256]{3,2,1,0:T(8,128)(2,1)}, f32[16,128,256]{2,1,0:T(8,128)S(1)}) custom-call(bf16[3,128,256]{2,1,0:T(8,128)(2,1)S(1)} %get-tuple-element.34.edges, bf16[13,128,256]{2,1,0:T(8,128)(2,1)S(1)} %collective-permute-done.5.inners, bf16[3,128,256]{2,1,0:T(8,128)(2,1)S(1)} %collective-permute-done.2.got_0, ...), custom_call_target="tpu_custom_call" | custom-call | flops 30064771072 | bytes 10485760 | tf_op jit(solution)/shard_map/main/pallas_call | solution.py:403
  22.2 0.0 collective-permute-done.8.refs_1_
  22.3 0.0 collective-permute-done.6.products
  22.3 2.0 %collective-permute-done.7.refs_0_ = bf16[10,128,256]{2,1,0:T(8,128)(2,1)S(1)} collective-permute-done((bf16[10,128,256]{2,1,0:T(8,128)(2,1)S(1)}, bf16[10,128,256]{2,1,0:T(8,128)(2,1)S(1)}, u32[]{:S(2)}, u32[]{:S(2)}) %collective-permute-start.7) | collective-permute-done | bytes 655392 | tf_op jit(solution)/shard_map/ppermute | solution.py:450
  24.2 1.3 %inner_finish.1._ = bf16[2,16,128,256]{3,2,1,0:T(8,128)(2,1)} custom-call(f32[16,128,256]{2,1,0:T(8,128)S(1)} %get-tuple-element.45.base, bf16[3,256,256]{2,1,0:T(8,128)(2,1)S(1)} %get-tuple-element.32.time_kernel, bf16[2,128,256]{2,1,0:T(8,128)(2,1)S(1)} %collective-permute-done.6.products, ...), custom_call_target="tpu_custom_call", output_to_operand_aliasing={{}: (5, {})} | custom-call | flops 268435456 | bytes 4194304 | tf_op jit(solution)/shard_map/inner_finish/pallas_call | solution.py:403
  25.5 0.1 collective-permute-done.4.products
  25.6 0.7 %finish.1 = bf16[2,16,128,256]{3,2,1,0:T(8,128)(2,1)} custom-call(bf16[2,128,256]{2,1,0:T(8,128)(2,1)S(1)} %collective-permute-done.4.products, f32[16,128,256]{2,1,0:T(8,128)S(1)} %get-tuple-element.45.base, bf16[2,16,128,256]{3,2,1,0:T(8,128)(2,1)} %inner_finish.1._), custom_call_target="tpu_custom_call", output_to_operand_aliasing={{}: (2, {})} | custom-call | flops 33554432 | bytes 524288 | tf_op jit(solution)/shard_map/finish/pallas_call | solution.py:403
  (6 shorter events, 0.1 us)
Async XLA Ops:
  0.0 6.5 %collective-permute-start = (bf16[3,128,256]{2,1,0:T(8,128)(2,1)S(1)}, bf16[3,128,256]{2,1,0:T(8,128)(2,1)S(1)}, u32[]{:S(2)}, u32[]{:S(2)}) collective-permute-start(bf16[3,128,256]{2,1,0:T(8,128)(2,1)S(1)} %ends.1._), channel_id=1, source_target_pairs={{0,4},{4,8},{8,12},{12,0},{1,5},{5,9},{9,13},{13,1},{2,6},{6,10},{... | collective-permute-start | bytes 589832 | tf_op jit(solution)/shard_map/ppermute | solution.py:421
  2.1 4.4 %collective-permute-start.1 = (bf16[3,128,256]{2,1,0:T(8,128)(2,1)S(1)}, bf16[3,128,256]{2,1,0:T(8,128)(2,1)S(1)}, u32[]{:S(2)}, u32[]{:S(2)}) collective-permute-start(bf16[3,128,256]{2,1,0:T(8,128)(2,1)S(1)} %get-tuple-element.28.edges_b.refs_0_), channel_id=1, source_target_pairs={{0,4},{4,0},{8,12},{12,8},{1,5},{5,1},{9,13},{13,9},{2,6},{6,2},{1... | collective-permute-start | bytes 589832 | tf_op jit(solution)/shard_map/ppermute | solution.py:434
  2.2 2.2 %copy-start = (f32[256]{0:T(256)S(1)}, f32[256]{0:T(256)}, u32[]{:S(2)}) copy-start(f32[256]{0:T(256)} %param.9) | copy-start | bytes 3076
  2.2 2.2 %copy-start.1 = (f32[256]{0:T(256)S(1)}, f32[256]{0:T(256)}, u32[]{:S(2)}) copy-start(f32[256]{0:T(256)} %param.10) | copy-start | bytes 3076
  2.2 2.2 %copy-start.2 = (f32[256]{0:T(256)S(1)}, f32[256]{0:T(256)}, u32[]{:S(2)}) copy-start(f32[256]{0:T(256)} %param.12) | copy-start | bytes 3076
  2.2 15.3 %collective-permute-start.5 = (bf16[13,128,256]{2,1,0:T(8,128)(2,1)S(1)}, bf16[13,128,256]{2,1,0:T(8,128)(2,1)S(1)}, u32[]{:S(2)}, u32[]{:S(2)}) collective-permute-start(bf16[13,128,256]{2,1,0:T(8,128)(2,1)S(1)} %get-tuple-element.26._.inners_b.refs_1_), channel_id=1, source_target_pairs={{0,4},{4,8},{8,12},{12,0},{1,5},{5,9},{9,13},{13,1},{2,6},{6,10},{... | collective-permute-start | bytes 2555912 | tf_op jit(solution)/shard_map/ppermute | solution.py:432
  5.5 16.8 %collective-permute-start.8 = (bf16[4,128,256]{2,1,0:T(8,128)(2,1)S(1)}, bf16[4,128,256]{2,1,0:T(8,128)(2,1)S(1)}, u32[]{:S(2)}, u32[]{:S(2)}) collective-permute-start(bf16[4,128,256]{2,1,0:T(8,128)(2,1)S(1)} %get-tuple-element.44.refs_3_), channel_id=1, source_target_pairs={{0,4},{4,8},{8,12},{12,0},{1,5},{5,9},{9,13},{13,1},{2,6},{6,10},{... | collective-permute-start | bytes 786440 | tf_op jit(solution)/shard_map/ppermute | solution.py:451
  6.6 9.0 %collective-permute-start.2 = (bf16[3,128,256]{2,1,0:T(8,128)(2,1)S(1)}, bf16[3,128,256]{2,1,0:T(8,128)(2,1)S(1)}, u32[]{:S(2)}, u32[]{:S(2)}) collective-permute-start(bf16[3,128,256]{2,1,0:T(8,128)(2,1)S(1)} %get-tuple-element.29._), channel_id=1, source_target_pairs={{0,1},{1,2},{2,3},{3,7},{4,0},{5,4},{6,5},{7,6},{8,9},{9,10},{10,1... | collective-permute-start | bytes 589832 | tf_op jit(solution)/shard_map/ppermute | solution.py:448
  8.2 7.4 %collective-permute-start.3 = (bf16[3,128,256]{2,1,0:T(8,128)(2,1)S(1)}, bf16[3,128,256]{2,1,0:T(8,128)(2,1)S(1)}, u32[]{:S(2)}, u32[]{:S(2)}) collective-permute-start(bf16[3,128,256]{2,1,0:T(8,128)(2,1)S(1)} %get-tuple-element.30), channel_id=1, source_target_pairs={{1,0},{2,1},{3,2},{7,3},{0,4},{4,5},{5,6},{6,7},{9,8},{10,9},{11,1... | collective-permute-start | bytes 589832 | tf_op jit(solution)/shard_map/ppermute | solution.py:449
  10.8 13.4 %collective-permute-start.7 = (bf16[10,128,256]{2,1,0:T(8,128)(2,1)S(1)}, bf16[10,128,256]{2,1,0:T(8,128)(2,1)S(1)}, u32[]{:S(2)}, u32[]{:S(2)}) collective-permute-start(bf16[10,128,256]{2,1,0:T(8,128)(2,1)S(1)} %get-tuple-element.36._.refs_1_), channel_id=1, source_target_pairs={{0,4},{4,8},{8,12},{1,5},{5,9},{9,13},{2,6},{6,10},{10,14},{3,7},{... | collective-permute-start | bytes 1966088 | tf_op jit(solution)/shard_map/ppermute | solution.py:450
  15.6 1.9 %copy-start.3 = (f32[256]{0:T(256)S(1)}, f32[256]{0:T(256)}, u32[]{:S(2)}) copy-start(f32[256]{0:T(256)} %param.13) | copy-start | bytes 3076
  17.0 5.3 %collective-permute-start.6 = (bf16[2,128,256]{2,1,0:T(8,128)(2,1)S(1)}, bf16[2,128,256]{2,1,0:T(8,128)(2,1)S(1)}, u32[]{:S(2)}, u32[]{:S(2)}) collective-permute-start(bf16[2,128,256]{2,1,0:T(8,128)(2,1)S(1)} %get-tuple-element.33), channel_id=1, source_target_pairs={{0,4},{4,0},{8,12},{12,8},{1,5},{5,1},{9,13},{13,9},{2,6},{6,2},{1... | collective-permute-start | bytes 393224 | tf_op jit(solution)/shard_map/ppermute | solution.py:462
  17.1 8.6 %collective-permute-start.4 = (bf16[2,128,256]{2,1,0:T(8,128)(2,1)S(1)}, bf16[2,128,256]{2,1,0:T(8,128)(2,1)S(1)}, u32[]{:S(2)}, u32[]{:S(2)}) collective-permute-start(bf16[2,128,256]{2,1,0:T(8,128)(2,1)S(1)} %get-tuple-element.33), channel_id=1, source_target_pairs={{0,4},{4,8},{8,12},{12,0},{1,5},{5,9},{9,13},{13,1},{2,6},{6,10},{... | collective-permute-start | bytes 393224 | tf_op jit(solution)/shard_map/ppermute | solution.py:459
